TPU v7x, 32 devices: a whole 2x2x4 slice. The times are simulated.
32 devices in a mesh: groups: 2 (over x), wide: 8 (over z, y), narrow: 2 (over core).
Axes of the slice: x: 2, y: 2, z: 4, core: 2. Of those that a mesh axis runs over, the one named last changes fastest.
Arguments:
- tokens: bfloat16 [32, 16384], P(('groups', 'wide'), 'narrow'), parts along dimension 0, may hold values from -48 to 48
- lengths: int32 [8], P('groups'), parts along dimension 0, may hold values from 1 to 8, 16 in all
- w_query: bfloat16 [16384, 16384], P('narrow', 'wide'), may hold values from -0.046875 to 0.046875
- w_keyval: bfloat16 [16384, 2048], P('narrow', 'wide'), may hold values from -0.046875 to 0.046875
- w_out: bfloat16 [16384, 16384], P('wide', 'narrow'), may hold values from -0.046875 to 0.046875
Outputs:
- mixed: bfloat16 [32, 16384], P(('groups', 'wide'), 'narrow'), parts along dimension 0
There are 2 independent parts, one for each index of `groups`. A program takes and returns all parts, laid end to end along the dimension named above; an argument that names none is the same for every part. Nothing has to cross between parts.
Inputs may be any that keep to these rules, and one draw needn't show every extreme that they name: The lengths sum to 16; prompt s occupies the rows after the first s lengths.
All inputs are finite; a program needn't handle non-finite values.
Results may differ from a plain program's by a relative error of at most 0.0076.
Values may be sent and summed in bfloat16 or wider, within the bound.
No kernel may reach another device: no remote copies, remote signals or barrier semaphores. Data moves between devices by JAX's collectives and lax.ppermute only.
A program may use at most 192 MiB of HBM per device.

v0:
```python
import jax
import jax.numpy as jnp
from jax import lax
from jax.sharding import PartitionSpec as P

HEADS = 128
KV_HEADS = 8
HEAD_DIM = 128


theta_base = 500000.0


def positions(lengths, total):
    index = jnp.arange(total, dtype=jnp.int32)
    ends = jnp.cumsum(lengths)
    starts = ends - lengths
    member = (index[:, None] >= ends[None, :]).astype(jnp.int32)
    segment = jnp.sum(member, axis=1)
    onehot = (segment[:, None] == jnp.arange(lengths.shape[0], dtype=jnp.int32)[None, :]).astype(
        jnp.int32
    )
    offset = index - jnp.sum(onehot * starts[None, :], axis=1)
    return (segment, offset)


def rotate(values, offset):
    half = values.shape[-1] // 2
    freq = theta_base ** (-(jnp.arange(half, dtype=jnp.float32) * 2.0) / values.shape[-1])
    angle = offset.astype(jnp.float32)[:, None] * freq[None, :]
    cosine = jnp.cos(angle)[:, None, :]
    sine = jnp.sin(angle)[:, None, :]
    first = values[..., :half]
    second = values[..., half:]
    return jnp.concatenate(
        [first * cosine - second * sine, second * cosine + first * sine], axis=-1
    )


def attend(query, keys, values, segment):
    total = query.shape[0]
    scores = jnp.einsum("qhd,khd->hqk", query, keys, preferred_element_type=jnp.float32) / jnp.sqrt(
        jnp.float32(query.shape[-1])
    )
    index = jnp.arange(total, dtype=jnp.int32)
    allowed = (segment[:, None] == segment[None, :]) & (index[None, :] <= index[:, None])
    scores = jnp.where(allowed[None], scores, jnp.float32(-1e30))
    top = jnp.max(scores, axis=-1, keepdims=True)
    weights = jnp.exp(scores - top)
    probs = (weights / jnp.sum(weights, axis=-1, keepdims=True)).astype(jnp.bfloat16)
    return jnp.einsum("hqk,khd->qhd", probs, values, preferred_element_type=jnp.float32).astype(
        jnp.bfloat16
    )


def local(tokens, lengths, w_query, w_keyval, w_out):
    query_cols = w_query.shape[1]
    local_heads = query_cols // HEAD_DIM
    piece = lax.all_gather(tokens, "wide", axis=0, tiled=True)
    partial_sums = jnp.concatenate(
        [
            jnp.dot(piece, w_query, preferred_element_type=jnp.float32),
            jnp.dot(piece, w_keyval, preferred_element_type=jnp.float32),
        ],
        axis=1,
    )
    total = partial_sums.shape[0]
    query_part = partial_sums[:, :query_cols]
    keyval_part = partial_sums[:, query_cols:]
    first_head = lax.axis_index("wide") * local_heads
    query = lax.psum(query_part, "narrow")
    head_ids = first_head + jnp.arange(local_heads, dtype=jnp.int32)
    summed = lax.psum(keyval_part, "narrow").astype(jnp.bfloat16)
    keyval = lax.all_gather(summed, "wide", axis=1, tiled=True)
    segment, offset = positions(lengths, total)
    kv_width = KV_HEADS * HEAD_DIM
    keys = rotate(
        keyval[:, :kv_width].astype(jnp.float32).reshape(total, KV_HEADS, HEAD_DIM), offset
    ).astype(jnp.bfloat16)
    values = keyval[:, kv_width:].reshape(total, KV_HEADS, HEAD_DIM)
    kv_ids = head_ids // (HEADS // KV_HEADS)
    keys_sel = jnp.take(keys, kv_ids, axis=1)
    values_sel = jnp.take(values, kv_ids, axis=1)
    query_rot = rotate(query.reshape(total, -1, HEAD_DIM), offset).astype(jnp.bfloat16)
    attended = attend(query_rot, keys_sel, values_sel, segment).reshape(total, -1)
    mixed = lax.psum_scatter(
        jnp.dot(attended, w_out, preferred_element_type=jnp.float32),
        "wide",
        scatter_dimension=0,
        tiled=True,
    )
    return mixed.astype(jnp.bfloat16)


def solution(mesh):
    in_specs = (
        P(("groups", "wide"), "narrow"),
        P("groups"),
        P("narrow", "wide"),
        P("narrow", "wide"),
        P("wide", "narrow"),
    )
    out_specs = P(("groups", "wide"), "narrow")
    return jax.shard_map(local, mesh=mesh, in_specs=in_specs, out_specs=out_specs, check_vma=False)
```

profile of v0, /device:TPU:0, one launch (start us, length us, event | category | flops | bytes accessed | tf_op | source)
XLA Modules:
  0.0 159.5 jit_solution(11805619078646518280)
XLA Ops:
  6.5 32.9 %all-gather = bf16[8,2,8192]{2,1,0:T(2,128)(2,1)S(1)} all-gather(bf16[1,2,8192]{2,1,0:T(2,128)(2,1)} %bitcast.44), channel_id=1, replica_groups=mesh['groups'=2,'wide'=8,'narrow'=2] {'wide'}, dimensions={0}, use_global_device_ids=true | all-gather | bytes 294912 | tf_op jit(solution)/shard_map/all_gather | solution.py:59
  39.4 0.1 reshape.175
  39.5 12.8 %convolution_bitcast_fusion = f32[2,16,8,128]{3,2,1,0:T(8,128)S(1)} fusion(bf16[16,8192]{1,0:T(8,128)(2,1)S(1)} %reshape.175, bf16[8192,2048]{1,0:T(8,128)(2,1)} %param.9), kind=kOutput, calls=%fused_computation.7 | convolution fusion | flops 536870912 | bytes 33947648 | tf_op jit(solution)/shard_map/dot_general | solution.py:62
  52.3 0.7 copy.43
  53.1 0.2 reduce-window.8
  53.2 0.1 convert_reduce_fusion
  53.3 0.1 fusion.20
  53.4 0.1 select_reduce_fusion
  53.5 2.8 %fusion.45 = f32[16,256]{1,0:T(8,128)S(1)} fusion(bf16[16,8192]{1,0:T(8,128)(2,1)S(1)} %reshape.175, bf16[8192,256]{1,0:T(8,128)(2,1)} %param.10), kind=kOutput, calls=%fused_computation.64 | convolution fusion | flops 67108864 | bytes 4472832 | tf_op jit(solution)/shard_map/dot_general | solution.py:63
  56.3 3.4 %psum.14 = bf16[16,256]{1,0:T(8,128)(2,1)S(1)} all-reduce(f32[16,256]{1,0:T(8,128)S(1)} %fusion.45), channel_id=1, replica_groups=mesh['groups'=2,'wide'=8,'narrow'=2] {'narrow'}, use_global_device_ids=true, to_apply=%region_0.0 | all-reduce | flops 4096 | bytes 24576 | tf_op jit(solution)/shard_map/psum | solution.py:73
  59.7 30.5 %all_gather.7 = bf16[16,2048]{1,0:T(8,128)(2,1)S(1)} all-gather(bf16[16,256]{1,0:T(8,128)(2,1)S(1)} %psum.14), channel_id=1, replica_groups=mesh['groups'=2,'wide'=8,'narrow'=2] {'wide'}, dimensions={1}, use_global_device_ids=true | all-gather | bytes 73728 | tf_op jit(solution)/shard_map/all_gather | solution.py:74
  90.2 0.1 fusion.39
  90.3 0.1 multiply_cosine_fusion
  90.5 0.1 pad_maximum_fusion
  90.6 0.6 gather_fusion.1
  91.2 0.6 gather_fusion
  91.8 0.6 dynamic-slice
  93.0 0.0 all-reduce.4.cloned.1.call-done
  93.1 1.1 subtract_convert_fusion
  94.2 0.3 fusion.40
  94.4 0.2 fusion.4
  94.7 12.8 %fusion.5 = f32[16,8192]{1,0:T(8,128)S(1)} fusion(bf16[2048,8192]{1,0:T(8,128)(2,1)} %param.11, bf16[16,2,8,128]{3,2,1,0:T(8,128)(2,1)S(1)} %fusion.4), kind=kOutput, calls=%fused_computation.14 | convolution fusion | flops 536870912 | bytes 34144256 | tf_op jit(solution)/shard_map/dot_general | solution.py:87
  107.5 44.4 %all-reduce.5 = bf16[16,8192]{1,0:T(8,128)(2,1)S(1)} all-reduce(f32[16,8192]{1,0:T(8,128)S(1)} %fusion.5), channel_id=2, replica_groups=mesh['groups'=2,'wide'=8,'narrow'=2] {'wide'}, use_global_device_ids=true, to_apply=%region_7.9.clone | all-reduce | flops 131072 | bytes 786432
  152.0 0.7 dynamic-slice_convert_fusion
  (16 shorter events, 0.1 us)
Async XLA Ops:
  6.5 85.2 %copy-start.1 = (u32[32]{0:T(128)S(1)}, u32[32]{0:T(128)}, u32[]{:S(2)}) copy-start(u32[32]{0:T(128)} %constant.57) | copy-start | bytes 388
  6.5 46.5 %copy-start = (s32[4]{0:T(128)S(1)}, s32[4]{0:T(128)}, u32[]{:S(2)}) copy-start(s32[4]{0:T(128)} %param.8) | copy-start | bytes 52
  6.5 86.5 %all-reduce.4.cloned.1.call-start = ((), (), s32[]{:S(2)}) async-start(), calls=%async_computation | async-start | bytes 262144 | tf_op jit(solution)/shard_map/psum | solution.py:71
Sparse Core Ops, SparseCore 0:
  53.1 18.9 all-reduce.3
where the time goes:
time: 160 us; the launch traced here: 159 us
  blocking collectives  111 us (69%)
  matrix products  29 us (18%)
  between operations  14.2 us (9%)
  local copies, waits for them, and re-layouts  3.27 us (2%)
  other arithmetic  1.82 us (1%)
    unnamed x1, blocking collectives  44.4 us
    all_gather x1, blocking collectives, local(): piece = lax.all_gather(tokens, 'wide', axis=0, tiled=True)  32.9 us
    all_gather x1, blocking collectives, local(): keyval = lax.all_gather(summed, 'wide', axis=1, tiled=True)  30.5 us
    dot_general x1, matrix products, local(): jnp.dot(attended, w_out, preferred_element_type=jnp.float32)  12.8 us
    dot_general x1, matrix products, local(): jnp.dot(piece, w_query, preferred_element_type=jnp.float32)  12.8 us
    psum x1, blocking collectives, local(): summed = lax.psum(keyval_part, 'narrow').astype(jnp.bfloat16)  3.37 us
  transfers between devices with their start and end apart: 1, of which 0 were waited for; matrix products, arithmetic and copies ran while one was open for 3% of the time, Pallas kernels for 0%

commit v1 on v0

v1 whole, which is shorter than its diff:
```python
import functools
import math

import jax
import jax.numpy as jnp
import numpy as np
from jax import lax
from jax.experimental import pallas as pl
from jax.experimental.pallas import tpu as pltpu
from jax.sharding import PartitionSpec as P

HEADS = 128
KV_HEADS = 8
HEAD_DIM = 128
theta_base = 500000.0
F32 = jnp.float32
BF16 = jnp.bfloat16
MIB = 1 << 20


def vspec():
    return pl.BlockSpec(memory_space=pltpu.VMEM)


def aspec():
    return pl.BlockSpec(memory_space=pltpu.HBM)


def near(x):
    return pltpu.with_memory_space_constraint(x, pltpu.VMEM)


def call(kernel, name, ins, outs, scratch=(), limit=4, far=0, cost=0, smem=0, after=()):
    if after:
        inner, skip = kernel, len(after)
        kernel = lambda *refs: inner(*refs[skip:])
        ins = [*[near(x) for x in after], *ins]
    if far:
        ins = [*ins[:-far], *[pltpu.with_memory_space_constraint(x, pltpu.HBM) for x in ins[-far:]]]
    specs = [pl.BlockSpec(memory_space=pltpu.SMEM)] * smem
    specs += [vspec()] * (len(ins) - smem - far) + [aspec()] * far
    return pl.pallas_call(
        kernel,
        out_shape=tuple(outs),
        in_specs=specs,
        out_specs=(vspec(),) * len(outs),
        scratch_shapes=list(scratch),
        compiler_params=pltpu.CompilerParams(vmem_limit_bytes=limit * MIB),
        cost_estimate=pl.CostEstimate(flops=0, bytes_accessed=cost, transcendentals=0),
        name=name,
    )(*ins)


def fetched(w, lo, hi):
    return pltpu.VMEM((w.shape[0], hi - lo), BF16)


def fetches(sources, targets, spans, sems):
    return [
        pltpu.make_async_copy(src.at[:, pl.ds(lo, hi - lo)], dst, sems.at[i])
        for i, (src, dst, (lo, hi)) in enumerate(zip(sources, targets, spans))
    ]


def ahead_kernel(*refs, spans):
    n = len(spans)
    copies = fetches(refs[:n], refs[n : 2 * n], spans, refs[-1])
    for copy in copies:
        copy.start()
    for copy in copies:
        copy.wait()


def ahead(name, sources, spans, after=()):
    nbytes = sum(w.shape[0] * (hi - lo) * 2 for w, (lo, hi) in zip(sources, spans))
    return call(
        functools.partial(ahead_kernel, spans=spans),
        name,
        sources,
        [fetched(w, lo, hi) for w, (lo, hi) in zip(sources, spans)],
        [pltpu.SemaphoreType.DMA((len(spans),))],
        limit=1,
        far=len(sources),
        cost=nbytes,
        after=after,
    )


def join_kernel(a_ref, b_ref, o_ref):
    n = a_ref.shape[0]
    o_ref[:n] = a_ref[...]
    o_ref[n:] = b_ref[...]


def keyval_kernel(a_ref, b_ref, w_ref, *refs, order, spans):
    n = len(spans)
    sources, (x_out, kv_out), targets = refs[:n], refs[n : n + 2], refs[n + 2 : 2 * n + 2]
    x32, sems = refs[2 * n + 2 :]
    copies = fetches(sources, targets, spans, sems)
    for copy in copies:
        copy.start()
    count, rows = a_ref.shape[:2]
    for i in range(count):
        for base, ref in ((order[i], a_ref), (order[count + i], b_ref)):
            x32[rows * base : rows * (base + 1), :] = ref[i].astype(F32)
    x_out[...] = x32[...].astype(BF16)
    kv_out[...] = jnp.dot(x_out[...], w_ref[...], preferred_element_type=F32)
    for copy in copies:
        copy.wait()


def query_kernel(x_ref, *refs, parts, spans):
    n = len(spans)
    w_refs, sources, q_out, targets = refs[:parts], refs[parts : parts + n], refs[parts + n], refs[parts + n + 1 : -1]
    copies = fetches(sources, targets, spans, refs[-1])
    for copy in copies:
        copy.start()
    at = 0
    for w_ref in w_refs:
        width = w_ref.shape[1]
        step = math.gcd(width, 512)

        @pl.loop(0, width // step)
        def _(j):
            part = jnp.dot(x_ref[...], w_ref[:, pl.ds(pl.multiple_of(j * step, step), step)], preferred_element_type=F32)
            q_out[:, pl.ds(pl.multiple_of(at + j * step, step), step)] = part

        at += width
    for copy in copies:
        copy.wait()


def pair_kernel(mine_ref, other_ref, one_ref, two_ref, *, width, rows):
    me = lax.axis_index("wide")
    total = (mine_ref[...] + other_ref[...]).astype(BF16)
    row = lax.broadcasted_iota(jnp.int32, (total.shape[0],) * 2, 0)
    col = lax.broadcasted_iota(jnp.int32, (total.shape[0],) * 2, 1)
    order = (col == rows * jnp.bitwise_xor(row // rows, me) + lax.rem(row, rows)).astype(F32).astype(BF16)
    total = jnp.dot(order, total, preferred_element_type=F32)
    left, right = total[:, :width], total[:, width:]
    low = me < lax.axis_size("wide") // 2
    one_ref[...] = jnp.where(low, left, right).astype(BF16)
    two_ref[...] = jnp.where(low, right, left).astype(BF16)


def positions(token, len_ref):
    end = jnp.int32(0)
    segment = jnp.zeros_like(token)
    start = jnp.zeros_like(token)
    for i in range(len_ref.shape[0]):
        end = end + len_ref[i]
        past = token >= end
        segment = segment + past.astype(jnp.int32)
        start = start + jnp.where(past, len_ref[i], 0)
    return segment, token - start


def attend_kernel(len_ref, freq_ref, one_ref, two_ref, *refs, parts, rows, spans):
    n = len(spans)
    mine_refs, other_refs, refs = refs[:parts], refs[parts : 2 * parts], refs[2 * parts :]
    sources, att, targets, sems = refs[:n], refs[n], refs[n + 1 : -1], refs[-1]
    copies = fetches(sources, targets, spans, sems)
    for copy in copies:
        copy.start()
    me = lax.axis_index("wide")
    total, dim = one_ref.shape
    odd = lax.rem(me, 2) == 1
    one, two = one_ref[...].astype(F32), two_ref[...].astype(F32)
    keys = jnp.where(odd, two, one)
    values = jnp.where(odd, one, two).astype(BF16)
    freq = freq_ref[...]

    def owner(row):
        return rows * jnp.bitwise_xor(row // rows, me) + lax.rem(row, rows)

    def tables(token):
        angle = positions(token, len_ref)[1].astype(F32) * freq
        lane = lax.broadcasted_iota(jnp.int32, angle.shape, 1)
        sine = jnp.sin(angle)
        return jnp.cos(angle), jnp.where(lane < dim // 2, -sine, sine)

    def rotate(u, cosine, sine):
        return u * cosine + pltpu.roll(u, dim // 2, 1) * sine

    row = lax.broadcasted_iota(jnp.int32, (total, dim), 0)
    keys_rot = rotate(keys, *tables(row)).astype(BF16)
    cosine, sine = tables(owner(row))
    turned = []
    for mine_ref, other_ref in zip(mine_refs, other_refs):
        query = mine_ref[...] + other_ref[...]
        for h in range(query.shape[1] // dim):
            turned.append(rotate(query[:, dim * h : dim * (h + 1)], cosine, sine).astype(BF16))
    stack = jnp.concatenate(turned, axis=0)
    scores = lax.dot_general(stack, keys_rot, (((1,), (1,)), ((), ())), preferred_element_type=F32)
    scores = scores / F32(math.sqrt(dim))
    qtok = owner(lax.rem(lax.broadcasted_iota(jnp.int32, scores.shape, 0), total))
    ktok = lax.broadcasted_iota(jnp.int32, scores.shape, 1)
    allowed = (positions(qtok, len_ref)[0] == positions(ktok, len_ref)[0]) & (ktok <= qtok)
    scores = jnp.where(allowed, scores, F32(-1e30))
    weights = jnp.exp(scores - jnp.max(scores, axis=1, keepdims=True))
    probs = (weights / jnp.sum(weights, axis=1, keepdims=True)).astype(BF16)
    mixed = jnp.dot(probs, values, preferred_element_type=F32).astype(BF16)
    for h in range(len(turned)):
        att[:, dim * h : dim * (h + 1)] = mixed[total * h : total * (h + 1), :]
    for copy in copies:
        copy.wait()


def output_kernel(att_ref, *refs, near_parts, lo, hi, pieces, spans):
    n = len(spans)
    w_refs, refs = refs[:near_parts], refs[near_parts:]
    sources, refs = refs[:n], refs[n:]
    keep_ref, send_ref, targets = refs[0], refs[1], refs[2 : 2 + n]
    acc, sems = refs[2 + n :]
    copies = fetches(sources, targets, spans, sems)
    for copy in copies:
        copy.start()
    at = 0
    for k, w_ref in enumerate(w_refs):
        width = w_ref.shape[1]
        step = math.gcd(width, 512)

        @pl.loop(0, width // step)
        def _(j):
            part = jnp.dot(att_ref[...], w_ref[:, pl.ds(pl.multiple_of(j * step, step), step)], preferred_element_type=F32)
            acc[:, pl.ds(pl.multiple_of(at + j * step, step), step)] = part

        at += width
    rows = acc.shape[0] // pieces
    for s in range(0, pieces, 2):
        keep_ref[s // 2] = acc[rows * s : rows * (s + 1), :]
        send_ref[s // 2] = acc[rows * (s + 1) : rows * (s + 2), :].astype(BF16)
    for copy in copies:
        copy.wait()


def near_sum_kernel(keep_ref, got_ref, own_ref, *outs):
    for k in range(keep_ref.shape[0]):
        part = keep_ref[k] + got_ref[k].astype(F32)
        if k == 0:
            own_ref[...] = part
        else:
            outs[k - 1][...] = part.astype(BF16)


def total_kernel(*refs, parts, count):
    out = refs[-1]
    at = 0
    for p in range(parts):
        mine = refs[p * count]
        total = mine[...]
        for r in refs[p * count + 1 : (p + 1) * count]:
            total = total + r[...].astype(F32)
        out[:, at : at + mine.shape[1]] = total.astype(BF16)
        at += mine.shape[1]


def swap(x, axis, size, bit):
    return lax.ppermute(x, axis, [(i, i ^ bit) for i in range(size)])


def shaped(*shape, dtype=F32):
    return jax.ShapeDtypeStruct(shape, dtype)


def plain_positions(lengths, total):
    index = jnp.arange(total, dtype=jnp.int32)
    ends = jnp.cumsum(lengths)
    past = index[:, None] >= ends[None, :]
    segment = jnp.sum(past.astype(jnp.int32), axis=1)
    offset = index - jnp.sum(jnp.where(past, lengths[None, :], 0), axis=1)
    return segment, offset


def plain_rotate(values, offset):
    half = values.shape[-1] // 2
    freq = theta_base ** (-(jnp.arange(half, dtype=F32) * 2.0) / values.shape[-1])
    angle = offset.astype(F32)[:, None] * freq[None, :]
    cosine = jnp.cos(angle)[:, None, :]
    sine = jnp.sin(angle)[:, None, :]
    first, second = values[..., :half], values[..., half:]
    return jnp.concatenate([first * cosine - second * sine, second * cosine + first * sine], axis=-1)


def plain_attend(query, keys, values, segment):
    total = query.shape[0]
    scores = jnp.einsum("qhd,khd->hqk", query, keys, preferred_element_type=F32) / jnp.sqrt(F32(query.shape[-1]))
    index = jnp.arange(total, dtype=jnp.int32)
    allowed = (segment[:, None] == segment[None, :]) & (index[None, :] <= index[:, None])
    scores = jnp.where(allowed[None], scores, F32(-1e30))
    weights = jnp.exp(scores - jnp.max(scores, axis=-1, keepdims=True))
    probs = (weights / jnp.sum(weights, axis=-1, keepdims=True)).astype(BF16)
    return jnp.einsum("hqk,khd->qhd", probs, values, preferred_element_type=F32).astype(BF16)


def plain(tokens, lengths, w_query, w_keyval, w_out):
    q_cols = w_query.shape[1]
    heads = q_cols // HEAD_DIM
    piece = lax.all_gather(tokens, "wide", axis=0, tiled=True)
    query_part = jnp.dot(piece, w_query, preferred_element_type=F32)
    keyval_part = jnp.dot(piece, w_keyval, preferred_element_type=F32)
    total = piece.shape[0]
    query = lax.psum(query_part, "narrow")
    summed = lax.psum(keyval_part, "narrow").astype(BF16)
    keyval = lax.all_gather(summed, "wide", axis=1, tiled=True)
    segment, offset = plain_positions(lengths, total)
    kv_width = KV_HEADS * HEAD_DIM
    keys = plain_rotate(keyval[:, :kv_width].astype(F32).reshape(total, KV_HEADS, HEAD_DIM), offset).astype(BF16)
    values = keyval[:, kv_width:].reshape(total, KV_HEADS, HEAD_DIM)
    head_ids = lax.axis_index("wide") * heads + jnp.arange(heads, dtype=jnp.int32)
    kv_ids = head_ids // (HEADS // KV_HEADS)
    query_rot = plain_rotate(query.reshape(total, -1, HEAD_DIM), offset).astype(BF16)
    attended = plain_attend(query_rot, jnp.take(keys, kv_ids, axis=1), jnp.take(values, kv_ids, axis=1), segment)
    mixed = lax.psum_scatter(
        jnp.dot(attended.reshape(total, -1), w_out, preferred_element_type=F32), "wide", scatter_dimension=0, tiled=True
    )
    return mixed.astype(BF16)


def local(tokens, lengths, w_query, w_keyval, w_out):
    wide = lax.axis_size("wide")
    rows, depth = tokens.shape
    total = rows * wide
    kv_cols, q_cols, out_cols = w_keyval.shape[1], w_query.shape[1], w_out.shape[1]
    inner = w_out.shape[0]
    bits = [1 << b for b in reversed(range(wide.bit_length() - 1))]
    cuts = [0, q_cols // 8, 3 * q_cols // 8, 7 * q_cols // 8]
    x = tokens[None]
    order = [0]
    w_near = []
    kv_near = None
    for i, bit in enumerate(bits):
        other = swap(x, "wide", wide, bit)
        if i == 0:
            kv_near, w0 = ahead("ahead%d" % i, [w_keyval, w_query], [(0, kv_cols), (cuts[0], cuts[1])])
        else:
            (w0,) = ahead("ahead%d" % i, [w_query], [(cuts[i], cuts[i + 1])], after=[x])
        w_near.append(w0)
        order = order + [s ^ bit for s in order]
        if i < len(bits) - 1:
            (x,) = call(join_kernel, "join%d" % i, [x, other], [shaped(2 * x.shape[0], rows, depth, dtype=BF16)], limit=2, after=[w0])
    x, kv, w3 = call(
        functools.partial(keyval_kernel, order=order, spans=[(cuts[3], q_cols)]),
        "keyval",
        [x, other, near(kv_near), w_query],
        [shaped(total, depth, dtype=BF16), shaped(total, kv_cols), fetched(w_query, cuts[3], q_cols)],
        [pltpu.VMEM((total, depth), F32), pltpu.SemaphoreType.DMA((1,))],
        limit=4,
        far=1,
        after=[w_near[-1]],
    )
    w_near.append(w3)
    kv_other = swap(kv, "narrow", 2, 1)
    o_cuts = [0, out_cols // 8, 3 * out_cols // 8, out_cols // 2, out_cols * 5 // 8, out_cols]

    def query(name, weights, span, after=()):
        return call(
            functools.partial(query_kernel, parts=len(weights), spans=[span]),
            name,
            [x, *[near(w) for w in weights], w_out],
            [shaped(total, sum(w.shape[1] for w in weights)), fetched(w_out, *span)],
            [pltpu.SemaphoreType.DMA((1,))],
            limit=2,
            far=1,
            cost=sum(w.size * 2 for w in weights),
            after=after,
        )

    q0, o0 = query("query0", w_near[:2], (o_cuts[0], o_cuts[1]))
    one, two = call(
        functools.partial(pair_kernel, width=HEAD_DIM, rows=rows),
        "pair",
        [kv, kv_other],
        [shaped(total, HEAD_DIM, dtype=BF16)] * 2,
        limit=1,
        after=[o0],
    )
    half = wide // 2
    first = [(s, 2 * s) if s < half else (s, 2 * (s - half) + 1) for s in range(wide)]
    second = [(s, 2 * s + 1) if s < half else (s, 2 * (s - half)) for s in range(wide)]
    sent = one
    one = lax.ppermute(one, "wide", first)
    two = lax.ppermute(two, "wide", second)
    q0_other = swap(q0, "narrow", 2, 1)
    q1, o1 = query("query1", w_near[2:], (o_cuts[1], o_cuts[2]), after=[sent])
    q1_other = swap(q1, "narrow", 2, 1)
    (o2,) = ahead("ahead_out", [w_out], [(o_cuts[2], o_cuts[3])], after=[q1])
    freq = theta_base ** (-(np.arange(HEAD_DIM) % (HEAD_DIM // 2)) * 2.0 / HEAD_DIM)
    freq = jnp.asarray(freq[None, :], F32)
    att, o3 = call(
        functools.partial(attend_kernel, parts=2, rows=rows, spans=[(o_cuts[3], o_cuts[4])]),
        "attend",
        [lengths, freq, one, two, q0, q1, q0_other, q1_other, w_out],
        [shaped(total, q_cols, dtype=BF16), fetched(w_out, o_cuts[3], o_cuts[4])],
        [pltpu.SemaphoreType.DMA((1,))],
        limit=4,
        far=1,
        smem=1,
    )

    def output(name, weights, span):
        width = sum(w.shape[1] for w in weights)
        return call(
            functools.partial(output_kernel, near_parts=len(weights), lo=0, hi=0, pieces=wide, spans=[span] if span else []),
            name,
            [att, *[near(w) for w in weights], *([w_out] if span else [])],
            [shaped(wide // 2, rows, width), shaped(wide // 2, rows, width, dtype=BF16)]
            + ([fetched(w_out, *span)] if span else []),
            [pltpu.VMEM((total, width), F32), pltpu.SemaphoreType.DMA((1,))],
            limit=4,
            far=1 if span else 0,
            cost=sum(w.size * 2 for w in weights),
        )

    keep0, send0, o4 = output("output0", [o0, o1, o2, o3], (o_cuts[4], o_cuts[5]))
    got0 = swap(send0, "wide", wide, 1)
    keep1, send1 = output("output1", [o4], None)
    got1 = swap(send1, "wide", wide, 1)

    def finish(name, keep, got):
        count, _, width = keep.shape
        mine, *others = call(
            near_sum_kernel,
            name,
            [keep, got],
            [shaped(rows, width)] + [shaped(rows, width, dtype=BF16)] * (count - 1),
            limit=1,
        )
        back = {k: swap(others[k - 1], "wide", wide, 2 * k) for k in reversed(range(1, count))}
        return [mine] + [back[k] for k in range(1, count)]

    parts = finish("sum0", keep0, got0) + finish("sum1", keep1, got1)
    return call(
        functools.partial(total_kernel, parts=2, count=wide // 2),
        "total",
        parts,
        [shaped(rows, out_cols, dtype=BF16)],
        limit=1,
    )[0]


def solution(mesh):
    in_specs = (
        P(("groups", "wide"), "narrow"),
        P("groups"),
        P("narrow", "wide"),
        P("narrow", "wide"),
        P("wide", "narrow"),
    )
    out_specs = P(("groups", "wide"), "narrow")
    body = local if mesh.shape["wide"] == KV_HEADS and mesh.shape["narrow"] == 2 else plain
    return jax.shard_map(body, mesh=mesh, in_specs=in_specs, out_specs=out_specs, check_vma=False)
```

time: 160 us -> 64.2 us (0.40)
  blocking collectives: 111 us -> 0 us
  Pallas kernels: 0 us -> 33.4 us
  matrix products: 29 us -> 0 us
  starting transfers between devices: 0.01 us -> 21.4 us
  between operations: 14.2 us -> 0.19 us
  waiting for transfers between devices: 0.04 us -> 8.78 us
  local copies, waits for them, and re-layouts: 3.27 us -> 0.01 us
  other arithmetic: 1.82 us -> 0 us
    all_gather x2 -> x0, blocking collectives: 63.4 us -> none  [the longest x1 32.9 us: local(): piece = lax.all_gather(tokens, 'wide', axis=0, tiled=True)]
    unnamed x1 -> x0, blocking collectives: 44.4 us -> none
    pallas_call x0 -> x16, Pallas kernels: none -> 33.4 us  [call(): pl.pallas_call(kernel, out_shape=tuple(outs), in_specs=specs, out_specs=(...]
    dot_general x4 -> x0, matrix products: 28.7 us -> none  [the longest x1 12.8 us: local(): jnp.dot(attended, w_out, preferred_element_type=jnp.float32)]
    ppermute x0 -> x16, starting transfers between devices: none -> 21.4 us  [the longest x14 20.3 us: swap(): return lax.ppermute(x, axis, [(i, i ^ bit) for i in range(size)])]
    ppermute x0 -> x16, waiting for transfers between devices: none -> 8.78 us  [the longest x14 7.64 us: swap(): return lax.ppermute(x, axis, [(i, i ^ bit) for i in range(size)])]
    psum x1 -> x0, blocking collectives: 3.37 us -> none  [local(): summed = lax.psum(keyval_part, 'narrow').astype(jnp.bfloat16)]
  transfers between devices with their start and end apart: 1 -> 16, of which waited for: 0 -> 4; matrix products, arithmetic and copies ran while one was open for 3% -> 0% of each run, Pallas kernels for 0% -> 31%
where the time goes in v1:
time: 64.2 us; the launch traced here: 63.8 us
  Pallas kernels  33.4 us (52%)
  starting transfers between devices  21.4 us (33%)
  waiting for transfers between devices  8.78 us (14%)
    pallas_call x16, Pallas kernels, call(): pl.pallas_call(kernel, out_shape=tuple(outs), in_specs=specs, out_specs=(...  33.4 us
    ppermute x14, starting transfers between devices, swap(): return lax.ppermute(x, axis, [(i, i ^ bit) for i in range(size)])  20.3 us
    ppermute x14, waiting for transfers between devices, swap(): return lax.ppermute(x, axis, [(i, i ^ bit) for i in range(size)])  7.64 us
  transfers between devices with their start and end apart: 16, of which 4 were waited for; matrix products, arithmetic and copies ran while one was open for 0% of the time, Pallas kernels for 31%

profile of v1, /device:TPU:0, one launch (start us, length us, event | category | flops | bytes accessed | tf_op | source)
XLA Modules:
  0.0 63.8 jit_solution(1538758996970032056)
XLA Ops:
  0.0 4.0 %collective-permute-start = (bf16[1,2,8192]{2,1,0:T(2,128)(2,1)}, bf16[1,2,8192]{2,1,0:T(2,128)(2,1)S(1)}, u32[]{:S(2)}, u32[]{:S(2)}) collective-permute-start(bf16[1,2,8192]{2,1,0:T(2,128)(2,1)} %bitcast.1), channel_id=1, source_target_pairs={{0,8},{2,10},{4,12},{6,14},{8,0},{10,2},{12,4},{14,6},{1,9},{3,11}... | collective-permute-start | bytes 98312 | tf_op jit(solution)/shard_map/ppermute | solution.py:259
  4.0 3.5 %ahead0.1 = (bf16[8192,256]{1,0:T(8,128)(2,1)S(1)}, bf16[8192,256]{1,0:T(8,128)(2,1)S(1)}) custom-call(bf16[8192,256]{1,0:T(8,128)(2,1)} %refs_0_.1, bf16[8192,2048]{1,0:T(8,128)(2,1)} %refs_4_.4), custom_call_target="tpu_custom_call" | custom-call | bytes 8388608 | tf_op jit(solution)/shard_map/ahead0/pallas_call | solution.py:42
  7.6 1.6 %collective-permute-start.1 = (bf16[2,2,8192]{2,1,0:T(2,128)(2,1)S(1)}, bf16[2,2,8192]{2,1,0:T(2,128)(2,1)S(1)}, u32[]{:S(2)}, u32[]{:S(2)}) collective-permute-start(bf16[2,2,8192]{2,1,0:T(2,128)(2,1)S(1)} %join0.1.refs_0_.refs_1_), channel_id=1, source_target_pairs={{0,4},{2,6},{4,0},{6,2},{8,12},{10,14},{12,8},{14,10},{1,5},{3,7},... | collective-permute-start | bytes 196616 | tf_op jit(solution)/shard_map/ppermute | solution.py:259
  9.2 3.4 %ahead1.1.refs_0_.refs_1_ = bf16[8192,512]{1,0:T(8,128)(2,1)S(1)} custom-call(bf16[2,2,8192]{2,1,0:T(2,128)(2,1)S(1)} %join0.1.refs_0_.refs_1_, bf16[8192,2048]{1,0:T(8,128)(2,1)} %refs_4_.4), custom_call_target="tpu_custom_call" | custom-call | bytes 8388608 | tf_op jit(solution)/shard_map/ahead1/pallas_call | solution.py:42
  12.6 1.6 %collective-permute-start.2 = (bf16[4,2,8192]{2,1,0:T(2,128)(2,1)S(1)}, bf16[4,2,8192]{2,1,0:T(2,128)(2,1)S(1)}, u32[]{:S(2)}, u32[]{:S(2)}) collective-permute-start(bf16[4,2,8192]{2,1,0:T(2,128)(2,1)S(1)} %join1.1.refs_0_.refs_1_), channel_id=1, source_target_pairs={{0,2},{2,0},{4,6},{6,4},{8,10},{10,8},{12,14},{14,12},{1,3},{3,1},... | collective-permute-start | bytes 393224 | tf_op jit(solution)/shard_map/ppermute | solution.py:259
  14.2 5.8 %ahead2.1.refs_0_.refs_2_ = bf16[8192,1024]{1,0:T(8,128)(2,1)S(1)} custom-call(bf16[4,2,8192]{2,1,0:T(2,128)(2,1)S(1)} %join1.1.refs_0_.refs_1_, bf16[8192,2048]{1,0:T(8,128)(2,1)} %refs_4_.4), custom_call_target="tpu_custom_call" | custom-call | bytes 16777216 | tf_op jit(solution)/shard_map/ahead2/pallas_call | solution.py:42
  20.0 2.3 %keyval.1 = (bf16[16,8192]{1,0:T(8,128)(2,1)S(1)}, f32[16,256]{1,0:T(8,128)S(1)}, bf16[8192,256]{1,0:T(8,128)(2,1)S(1)}) custom-call(bf16[8192,1024]{1,0:T(8,128)(2,1)S(1)} %ahead2.1.refs_0_.refs_2_, bf16[4,2,8192]{2,1,0:T(2,128)(2,1)S(1)} %join1.1.refs_0_.refs_1_, bf16[4,2,8192]{2,1,0:T(2,128)(2,1)S(1)} %collective-permute-done.2.refs_2_, ...), custom_call_target="tpu_custom_call" | custom-call | tf_op jit(solution)/shard_map/keyval/pallas_call | solution.py:42
  22.4 2.2 %query0.1 = (f32[16,768]{1,0:T(8,128)S(1)}, bf16[2048,1024]{1,0:T(8,128)(2,1)S(1)}) custom-call(bf16[16,8192]{1,0:T(8,128)(2,1)S(1)} %get-tuple-element.33.x_ref.refs_1_, bf16[8192,256]{1,0:T(8,128)(2,1)S(1)} %get-tuple-element.31.refs_0_, bf16[8192,512]{1,0:T(8,128)(2,1)S(1)} %ahead1.1.refs_0_.refs_1_, bf16[2048,8192]{1,0:T(8,128)(2,1)} %refs_4_.7), custom_call_target="tpu_custom_call" | custom-call | bytes 12582912 | tf_op jit(solution)/shard_map/query0/pallas_call | solution.py:42
  24.7 3.4 %query1.1 = (f32[16,1280]{1,0:T(8,128)S(1)}, bf16[2048,2048]{1,0:T(8,128)(2,1)S(1)}) custom-call(bf16[16,128]{1,0:T(8,128)(2,1)S(1)} %get-tuple-element.36.refs_0_, bf16[16,8192]{1,0:T(8,128)(2,1)S(1)} %get-tuple-element.33.x_ref.refs_1_, bf16[8192,1024]{1,0:T(8,128)(2,1)S(1)} %ahead2.1.refs_0_.refs_2_, bf16[8192,256]{1,0:T(8,128)(2,1)S(1)} %get-tuple-element.39.refs_3_, ...), custom_call_target="tpu_custom_call" | custom-call | bytes 20971520 | tf_op jit(solution)/shard_map/query1/pallas_call | solution.py:42
  30.0 2.2 %ahead_out.1.refs_2_ = bf16[2048,1024]{1,0:T(8,128)(2,1)S(1)} custom-call(f32[16,1280]{1,0:T(8,128)S(1)} %get-tuple-element.40.refs_1_.refs_0_, bf16[2048,8192]{1,0:T(8,128)(2,1)} %refs_4_.7), custom_call_target="tpu_custom_call" | custom-call | bytes 4194304 | tf_op jit(solution)/shard_map/ahead_out/pallas_call | solution.py:42
  32.2 1.1 %collective-permute-done.5.two_ref = bf16[16,128]{1,0:T(8,128)(2,1)S(1)} collective-permute-done((bf16[16,128]{1,0:T(8,128)(2,1)S(1)}, bf16[16,128]{1,0:T(8,128)(2,1)S(1)}, u32[]{:S(2)}, u32[]{:S(2)}) %collective-permute-start.5) | collective-permute-done | bytes 4128 | tf_op jit(solution)/shard_map/ppermute | solution.py:383
  33.3 2.8 %attend.1 = (bf16[16,2048]{1,0:T(8,128)(2,1)S(1)}, bf16[2048,1024]{1,0:T(8,128)(2,1)S(1)}) custom-call(s32[4]{0:T(128)S(1)} %copy-done.1, f32[1,128]{1,0:T(1,128)S(1)} %copy-done.2, bf16[16,128]{1,0:T(8,128)(2,1)S(1)} %collective-permute-done.4.one_ref, bf16[16,128]{1,0:T(8,128)(2,1)S(1)} %collective-permute-done.5.two_ref, ...), custom_call_target="tpu_custom_call" | custom-call | tf_op jit(solution)/shard_map/attend/pallas_call | solution.py:42
  36.1 4.6 %output0.1 = (f32[4,2,5120]{2,1,0:T(2,128)S(1)}, bf16[4,2,5120]{2,1,0:T(2,128)(2,1)S(1)}, bf16[2048,3072]{1,0:T(8,128)(2,1)S(1)}) custom-call(bf16[16,2048]{1,0:T(8,128)(2,1)S(1)} %get-tuple-element.41.att_ref, bf16[2048,1024]{1,0:T(8,128)(2,1)S(1)} %get-tuple-element.34.refs_0_, bf16[2048,2048]{1,0:T(8,128)(2,1)S(1)} %get-tuple-element.42.refs_1_, ...), custom_call_target="tpu_custom_call" | custom-call | bytes 20971520 | tf_op jit(solution)/shard_map/output0/pallas_call | solution.py:42
  40.7 4.2 %collective-permute-start.8 = (bf16[4,2,5120]{2,1,0:T(2,128)(2,1)S(1)}, bf16[4,2,5120]{2,1,0:T(2,128)(2,1)S(1)}, u32[]{:S(2)}, u32[]{:S(2)}) collective-permute-start(bf16[4,2,5120]{2,1,0:T(2,128)(2,1)S(1)} %get-tuple-element.45), channel_id=1, source_target_pairs={{0,2},{2,0},{4,6},{6,4},{8,10},{10,8},{12,14},{14,12},{1,3},{3,1},... | collective-permute-start | bytes 245768 | tf_op jit(solution)/shard_map/ppermute | solution.py:259
  44.9 2.4 %output1.1 = (f32[4,2,3072]{2,1,0:T(2,128)S(1)}, bf16[4,2,3072]{2,1,0:T(2,128)(2,1)S(1)}) custom-call(bf16[16,2048]{1,0:T(8,128)(2,1)S(1)} %get-tuple-element.41.att_ref, bf16[2048,3072]{1,0:T(8,128)(2,1)S(1)} %get-tuple-element.50.refs_0_), custom_call_target="tpu_custom_call" | custom-call | bytes 12582912 | tf_op jit(solution)/shard_map/output1/pallas_call | solution.py:42
  47.4 4.1 %collective-permute-done.12.got_ref = bf16[4,2,3072]{2,1,0:T(2,128)(2,1)S(1)} collective-permute-done((bf16[4,2,3072]{2,1,0:T(2,128)(2,1)S(1)}, bf16[4,2,3072]{2,1,0:T(2,128)(2,1)S(1)}, u32[]{:S(2)}, u32[]{:S(2)}) %collective-permute-start.12) | collective-permute-done | bytes 49184 | tf_op jit(solution)/shard_map/ppermute | solution.py:259
  51.5 0.8 %collective-permute-start.13 = (bf16[2,3072]{1,0:T(2,128)(2,1)S(1)}, bf16[2,3072]{1,0:T(2,128)(2,1)S(1)}, u32[]{:S(2)}, u32[]{:S(2)}) collective-permute-start(bf16[2,3072]{1,0:T(2,128)(2,1)S(1)} %get-tuple-element.54), channel_id=1, source_target_pairs={{0,4},{2,6},{4,0},{6,2},{8,12},{10,14},{12,8},{14,10},{1,5},{3,7},... | collective-permute-start | bytes 36872 | tf_op jit(solution)/shard_map/ppermute | solution.py:259
  52.4 1.3 %collective-permute-start.9 = (bf16[2,5120]{1,0:T(2,128)(2,1)S(1)}, bf16[2,5120]{1,0:T(2,128)(2,1)S(1)}, u32[]{:S(2)}, u32[]{:S(2)}) collective-permute-start(bf16[2,5120]{1,0:T(2,128)(2,1)S(1)} %get-tuple-element.47), channel_id=1, source_target_pairs={{0,4},{2,6},{4,0},{6,2},{8,12},{10,14},{12,8},{14,10},{1,5},{3,7},... | collective-permute-start | bytes 61448 | tf_op jit(solution)/shard_map/ppermute | solution.py:259
  53.8 1.5 %collective-permute-start.10 = (bf16[2,5120]{1,0:T(2,128)(2,1)S(1)}, bf16[2,5120]{1,0:T(2,128)(2,1)S(1)}, u32[]{:S(2)}, u32[]{:S(2)}) collective-permute-start(bf16[2,5120]{1,0:T(2,128)(2,1)S(1)} %get-tuple-element.48), channel_id=1, source_target_pairs={{0,8},{2,10},{4,12},{6,14},{8,0},{10,2},{12,4},{14,6},{1,9},{3,11}... | collective-permute-start | bytes 61448 | tf_op jit(solution)/shard_map/ppermute | solution.py:259
  55.3 1.6 %collective-permute-start.11 = (bf16[2,5120]{1,0:T(2,128)(2,1)S(1)}, bf16[2,5120]{1,0:T(2,128)(2,1)S(1)}, u32[]{:S(2)}, u32[]{:S(2)}) collective-permute-start(bf16[2,5120]{1,0:T(2,128)(2,1)S(1)} %get-tuple-element.49), channel_id=1, source_target_pairs={{0,12},{2,14},{4,8},{6,10},{8,4},{10,6},{12,0},{14,2},{1,13},{3,15... | collective-permute-start | bytes 61448 | tf_op jit(solution)/shard_map/ppermute | solution.py:259
  56.9 0.8 %collective-permute-start.14 = (bf16[2,3072]{1,0:T(2,128)(2,1)S(1)}, bf16[2,3072]{1,0:T(2,128)(2,1)S(1)}, u32[]{:S(2)}, u32[]{:S(2)}) collective-permute-start(bf16[2,3072]{1,0:T(2,128)(2,1)S(1)} %get-tuple-element.55), channel_id=1, source_target_pairs={{0,8},{2,10},{4,12},{6,14},{8,0},{10,2},{12,4},{14,6},{1,9},{3,11}... | collective-permute-start | bytes 36872 | tf_op jit(solution)/shard_map/ppermute | solution.py:259
  57.7 2.0 %collective-permute-start.15 = (bf16[2,3072]{1,0:T(2,128)(2,1)S(1)}, bf16[2,3072]{1,0:T(2,128)(2,1)S(1)}, u32[]{:S(2)}, u32[]{:S(2)}) collective-permute-start(bf16[2,3072]{1,0:T(2,128)(2,1)S(1)} %get-tuple-element.56), channel_id=1, source_target_pairs={{0,12},{2,14},{4,8},{6,10},{8,4},{10,6},{12,0},{14,2},{1,13},{3,15... | collective-permute-start | bytes 36872 | tf_op jit(solution)/shard_map/ppermute | solution.py:259
  59.6 1.8 %collective-permute-done.14.refs_6_ = bf16[2,3072]{1,0:T(2,128)(2,1)S(1)} collective-permute-done((bf16[2,3072]{1,0:T(2,128)(2,1)S(1)}, bf16[2,3072]{1,0:T(2,128)(2,1)S(1)}, u32[]{:S(2)}, u32[]{:S(2)}) %collective-permute-start.14) | collective-permute-done | bytes 12320 | tf_op jit(solution)/shard_map/ppermute | solution.py:259
  61.5 1.7 %collective-permute-done.15.refs_7_ = bf16[2,3072]{1,0:T(2,128)(2,1)S(1)} collective-permute-done((bf16[2,3072]{1,0:T(2,128)(2,1)S(1)}, bf16[2,3072]{1,0:T(2,128)(2,1)S(1)}, u32[]{:S(2)}, u32[]{:S(2)}) %collective-permute-start.15) | collective-permute-done | bytes 12320 | tf_op jit(solution)/shard_map/ppermute | solution.py:259
  (30 shorter events, 2.9 us)
Async XLA Ops:
  0.0 7.5 %copy-start = (bf16[2,8192]{1,0:T(2,128)(2,1)S(1)}, bf16[2,8192]{1,0:T(2,128)(2,1)}, u32[]{:S(2)}) copy-start(bf16[2,8192]{1,0:T(2,128)(2,1)} %param.6) | copy-start | bytes 98308
  0.0 7.5 %collective-permute-start = (bf16[1,2,8192]{2,1,0:T(2,128)(2,1)}, bf16[1,2,8192]{2,1,0:T(2,128)(2,1)S(1)}, u32[]{:S(2)}, u32[]{:S(2)}) collective-permute-start(bf16[1,2,8192]{2,1,0:T(2,128)(2,1)} %bitcast.1), channel_id=1, source_target_pairs={{0,8},{2,10},{4,12},{6,14},{8,0},{10,2},{12,4},{14,6},{1,9},{3,11}... | collective-permute-start | bytes 98312 | tf_op jit(solution)/shard_map/ppermute | solution.py:259
  7.6 5.0 %collective-permute-start.1 = (bf16[2,2,8192]{2,1,0:T(2,128)(2,1)S(1)}, bf16[2,2,8192]{2,1,0:T(2,128)(2,1)S(1)}, u32[]{:S(2)}, u32[]{:S(2)}) collective-permute-start(bf16[2,2,8192]{2,1,0:T(2,128)(2,1)S(1)} %join0.1.refs_0_.refs_1_), channel_id=1, source_target_pairs={{0,4},{2,6},{4,0},{6,2},{8,12},{10,14},{12,8},{14,10},{1,5},{3,7},... | collective-permute-start | bytes 196616 | tf_op jit(solution)/shard_map/ppermute | solution.py:259
  12.6 7.4 %collective-permute-start.2 = (bf16[4,2,8192]{2,1,0:T(2,128)(2,1)S(1)}, bf16[4,2,8192]{2,1,0:T(2,128)(2,1)S(1)}, u32[]{:S(2)}, u32[]{:S(2)}) collective-permute-start(bf16[4,2,8192]{2,1,0:T(2,128)(2,1)S(1)} %join1.1.refs_0_.refs_1_), channel_id=1, source_target_pairs={{0,2},{2,0},{4,6},{6,4},{8,10},{10,8},{12,14},{14,12},{1,3},{3,1},... | collective-permute-start | bytes 393224 | tf_op jit(solution)/shard_map/ppermute | solution.py:259
  22.3 2.3 %collective-permute-start.3 = (f32[16,256]{1,0:T(8,128)S(1)}, f32[16,256]{1,0:T(8,128)S(1)}, u32[]{:S(2)}, u32[]{:S(2)}) collective-permute-start(f32[16,256]{1,0:T(8,128)S(1)} %get-tuple-element.35.refs_1_), channel_id=1, source_target_pairs={{0,1},{1,0},{2,3},{3,2},{4,5},{5,4},{6,7},{7,6},{8,9},{9,8},{10,11... | collective-permute-start | bytes 49160 | tf_op jit(solution)/shard_map/ppermute | solution.py:259
  28.1 5.2 %collective-permute-start.7 = (f32[16,1280]{1,0:T(8,128)S(1)}, f32[16,1280]{1,0:T(8,128)S(1)}, u32[]{:S(2)}, u32[]{:S(2)}) collective-permute-start(f32[16,1280]{1,0:T(8,128)S(1)} %get-tuple-element.40.refs_1_.refs_0_), channel_id=1, source_target_pairs={{0,1},{1,0},{2,3},{3,2},{4,5},{5,4},{6,7},{7,6},{8,9},{9,8},{10,11... | collective-permute-start | bytes 245768 | tf_op jit(solution)/shard_map/ppermute | solution.py:259
  28.7 4.6 %collective-permute-start.6 = (f32[16,768]{1,0:T(8,128)S(1)}, f32[16,768]{1,0:T(8,128)S(1)}, u32[]{:S(2)}, u32[]{:S(2)}) collective-permute-start(f32[16,768]{1,0:T(8,128)S(1)} %get-tuple-element.38.refs_0_), channel_id=1, source_target_pairs={{0,1},{1,0},{2,3},{3,2},{4,5},{5,4},{6,7},{7,6},{8,9},{9,8},{10,11... | collective-permute-start | bytes 147464 | tf_op jit(solution)/shard_map/ppermute | solution.py:259
  28.8 4.5 %copy-start.1 = (s32[4]{0:T(128)S(1)}, s32[4]{0:T(128)}, u32[]{:S(2)}) copy-start(s32[4]{0:T(128)} %len_ref.1) | copy-start | bytes 52
  28.8 4.5 %copy-start.2 = (f32[1,128]{1,0:T(1,128)S(1)}, f32[1,128]{1,0:T(1,128)}, u32[]{:S(2)}) copy-start(f32[1,128]{1,0:T(1,128)} %constant.2.clone.freq_ref) | copy-start | bytes 1540
  28.8 4.5 %collective-permute-start.5 = (bf16[16,128]{1,0:T(8,128)(2,1)S(1)}, bf16[16,128]{1,0:T(8,128)(2,1)S(1)}, u32[]{:S(2)}, u32[]{:S(2)}) collective-permute-start(bf16[16,128]{1,0:T(8,128)(2,1)S(1)} %get-tuple-element.37), channel_id=1, source_target_pairs={{0,2},{2,6},{4,10},{6,14},{8,0},{10,4},{12,8},{14,12},{1,3},{3,7},... | collective-permute-start | bytes 12296 | tf_op jit(solution)/shard_map/ppermute | solution.py:383
  29.3 4.0 %collective-permute-start.4 = (bf16[16,128]{1,0:T(8,128)(2,1)S(1)}, bf16[16,128]{1,0:T(8,128)(2,1)S(1)}, u32[]{:S(2)}, u32[]{:S(2)}) collective-permute-start(bf16[16,128]{1,0:T(8,128)(2,1)S(1)} %get-tuple-element.36.refs_0_), channel_id=1, source_target_pairs={{0,0},{2,4},{4,8},{6,12},{8,2},{10,6},{12,10},{14,14},{1,1},{3,5},... | collective-permute-start | bytes 12296 | tf_op jit(solution)/shard_map/ppermute | solution.py:382
  40.7 11.6 %collective-permute-start.8 = (bf16[4,2,5120]{2,1,0:T(2,128)(2,1)S(1)}, bf16[4,2,5120]{2,1,0:T(2,128)(2,1)S(1)}, u32[]{:S(2)}, u32[]{:S(2)}) collective-permute-start(bf16[4,2,5120]{2,1,0:T(2,128)(2,1)S(1)} %get-tuple-element.45), channel_id=1, source_target_pairs={{0,2},{2,0},{4,6},{6,4},{8,10},{10,8},{12,14},{14,12},{1,3},{3,1},... | collective-permute-start | bytes 245768 | tf_op jit(solution)/shard_map/ppermute | solution.py:259
  47.3 4.2 %collective-permute-start.12 = (bf16[4,2,3072]{2,1,0:T(2,128)(2,1)S(1)}, bf16[4,2,3072]{2,1,0:T(2,128)(2,1)S(1)}, u32[]{:S(2)}, u32[]{:S(2)}) collective-permute-start(bf16[4,2,3072]{2,1,0:T(2,128)(2,1)S(1)} %get-tuple-element.52), channel_id=1, source_target_pairs={{0,2},{2,0},{4,6},{6,4},{8,10},{10,8},{12,14},{14,12},{1,3},{3,1},... | collective-permute-start | bytes 147464 | tf_op jit(solution)/shard_map/ppermute | solution.py:259
  51.5 6.1 %collective-permute-start.13 = (bf16[2,3072]{1,0:T(2,128)(2,1)S(1)}, bf16[2,3072]{1,0:T(2,128)(2,1)S(1)}, u32[]{:S(2)}, u32[]{:S(2)}) collective-permute-start(bf16[2,3072]{1,0:T(2,128)(2,1)S(1)} %get-tuple-element.54), channel_id=1, source_target_pairs={{0,4},{2,6},{4,0},{6,2},{8,12},{10,14},{12,8},{14,10},{1,5},{3,7},... | collective-permute-start | bytes 36872 | tf_op jit(solution)/shard_map/ppermute | solution.py:259
  52.4 10.7 %collective-permute-start.9 = (bf16[2,5120]{1,0:T(2,128)(2,1)S(1)}, bf16[2,5120]{1,0:T(2,128)(2,1)S(1)}, u32[]{:S(2)}, u32[]{:S(2)}) collective-permute-start(bf16[2,5120]{1,0:T(2,128)(2,1)S(1)} %get-tuple-element.47), channel_id=1, source_target_pairs={{0,4},{2,6},{4,0},{6,2},{8,12},{10,14},{12,8},{14,10},{1,5},{3,7},... | collective-permute-start | bytes 61448 | tf_op jit(solution)/shard_map/ppermute | solution.py:259
  53.8 9.4 %collective-permute-start.10 = (bf16[2,5120]{1,0:T(2,128)(2,1)S(1)}, bf16[2,5120]{1,0:T(2,128)(2,1)S(1)}, u32[]{:S(2)}, u32[]{:S(2)}) collective-permute-start(bf16[2,5120]{1,0:T(2,128)(2,1)S(1)} %get-tuple-element.48), channel_id=1, source_target_pairs={{0,8},{2,10},{4,12},{6,14},{8,0},{10,2},{12,4},{14,6},{1,9},{3,11}... | collective-permute-start | bytes 61448 | tf_op jit(solution)/shard_map/ppermute | solution.py:259
  55.3 7.9 %collective-permute-start.11 = (bf16[2,5120]{1,0:T(2,128)(2,1)S(1)}, bf16[2,5120]{1,0:T(2,128)(2,1)S(1)}, u32[]{:S(2)}, u32[]{:S(2)}) collective-permute-start(bf16[2,5120]{1,0:T(2,128)(2,1)S(1)} %get-tuple-element.49), channel_id=1, source_target_pairs={{0,12},{2,14},{4,8},{6,10},{8,4},{10,6},{12,0},{14,2},{1,13},{3,15... | collective-permute-start | bytes 61448 | tf_op jit(solution)/shard_map/ppermute | solution.py:259
  56.9 4.6 %collective-permute-start.14 = (bf16[2,3072]{1,0:T(2,128)(2,1)S(1)}, bf16[2,3072]{1,0:T(2,128)(2,1)S(1)}, u32[]{:S(2)}, u32[]{:S(2)}) collective-permute-start(bf16[2,3072]{1,0:T(2,128)(2,1)S(1)} %get-tuple-element.55), channel_id=1, source_target_pairs={{0,8},{2,10},{4,12},{6,14},{8,0},{10,2},{12,4},{14,6},{1,9},{3,11}... | collective-permute-start | bytes 36872 | tf_op jit(solution)/shard_map/ppermute | solution.py:259
  57.7 5.5 %collective-permute-start.15 = (bf16[2,3072]{1,0:T(2,128)(2,1)S(1)}, bf16[2,3072]{1,0:T(2,128)(2,1)S(1)}, u32[]{:S(2)}, u32[]{:S(2)}) collective-permute-start(bf16[2,3072]{1,0:T(2,128)(2,1)S(1)} %get-tuple-element.56), channel_id=1, source_target_pairs={{0,12},{2,14},{4,8},{6,10},{8,4},{10,6},{12,0},{14,2},{1,13},{3,15... | collective-permute-start | bytes 36872 | tf_op jit(solution)/shard_map/ppermute | solution.py:259

commit v2 on v0

v2 whole, which is shorter than its diff:
```python
import functools
import math

import jax
import jax.numpy as jnp
from jax import lax
from jax.experimental import pallas as pl
from jax.experimental.pallas import tpu as pltpu
from jax.sharding import PartitionSpec as P

HEADS = 128
KV_HEADS = 8
HEAD_DIM = 128
theta_base = 500000.0
F32 = jnp.float32
BF16 = jnp.bfloat16
MIB = 1 << 20
CUTS = (0, 6, 9, 9, 10, 22, 24, 24, 32)
QSTEP = 4
QOUT = pltpu.VMEM
LIM = 3
HINT = 0
JH = (0, 0)
KH = 0


def vspec():
    return pl.BlockSpec(memory_space=pltpu.VMEM)


def aspec():
    return pl.BlockSpec(memory_space=pltpu.HBM)


def near(x):
    return pltpu.with_memory_space_constraint(x, pltpu.VMEM)


def call(kernel, name, ins, outs, scratch=(), limit=4, far=0, hint=0, smem=0, after=(), behind=()):
    if after:
        inner, skip = kernel, len(after)
        kernel = lambda *refs: inner(*refs[skip:])
        ins = [*[near(x) for x in after], *ins]
    if behind:
        whole, drop, keep = kernel, len(behind), len(ins) + len(after)
        kernel = lambda *refs: whole(*refs[:keep], *refs[keep + drop :])
        ins, far = [*ins, *behind], far + drop
    if far:
        ins = [*ins[:-far], *[pltpu.with_memory_space_constraint(x, pltpu.HBM) for x in ins[-far:]]]
    specs = [pl.BlockSpec(memory_space=pltpu.SMEM)] * smem
    specs += [vspec()] * (len(ins) - smem - far) + [aspec()] * far
    return pl.pallas_call(
        kernel,
        out_shape=tuple(outs),
        in_specs=specs,
        out_specs=(vspec(),) * len(outs),
        scratch_shapes=list(scratch),
        compiler_params=pltpu.CompilerParams(vmem_limit_bytes=limit * MIB),
        cost_estimate=pl.CostEstimate(flops=hint, bytes_accessed=1000, transcendentals=0),
        name=name,
    )(*ins)


def fetched(w, lo, hi):
    return pltpu.VMEM((w.shape[0], hi - lo), BF16)


def fetches(sources, targets, spans, sems):
    return [
        pltpu.make_async_copy(src.at[:, pl.ds(lo, hi - lo)], dst, sems.at[i])
        for i, (src, dst, (lo, hi)) in enumerate(zip(sources, targets, spans))
    ]


def ahead_kernel(*refs, spans):
    n = len(spans)
    copies = fetches(refs[:n], refs[n : 2 * n], spans, refs[-1])
    for copy in copies:
        copy.start()
    for copy in copies:
        copy.wait()


def ahead(name, sources, spans, after=(), behind=(), hint=0):
    return call(
        functools.partial(ahead_kernel, spans=spans),
        name,
        sources,
        [fetched(w, lo, hi) for w, (lo, hi) in zip(sources, spans)],
        [pltpu.SemaphoreType.DMA((len(spans),))],
        limit=1,
        far=len(sources),
        hint=hint,
        after=after,
        behind=behind,
    )


def positions(token, len_ref):
    end = jnp.int32(0)
    segment = jnp.zeros_like(token)
    start = jnp.zeros_like(token)
    for i in range(len_ref.shape[0]):
        end = end + len_ref[i]
        past = token >= end
        segment = segment + past.astype(jnp.int32)
        start = start + jnp.where(past, len_ref[i], 0)
    return segment, token - start


def tables_kernel(*refs, rows, spans):
    n = len(spans)
    sources, (turn_ref, allow_ref), targets, (sems, len_ref, len_sem) = refs[: n + 1], refs[n + 1 : n + 3], refs[n + 3 : -3], refs[-3:]
    lengths = pltpu.make_async_copy(sources[0], len_ref, len_sem)
    lengths.start()
    copies = fetches(sources[1:], targets, spans, sems)
    for copy in copies:
        copy.start()
    me = lax.axis_index("wide")
    total, dim = turn_ref.shape[1:]

    def owner(row, base):
        return rows * jnp.bitwise_xor(row // rows, base) + lax.rem(row, rows)

    shape = (total, dim)
    power = lax.rem(lax.broadcasted_iota(jnp.int32, shape, 1), dim // 2).astype(F32)
    freq = jnp.exp(power * F32(-2.0 * math.log(theta_base) / dim))
    lengths.wait()
    row = lax.broadcasted_iota(jnp.int32, shape, 0)
    lane = lax.broadcasted_iota(jnp.int32, shape, 1)
    for i, base in enumerate((me, me // 2)):
        angle = positions(owner(row, base), len_ref)[1].astype(F32) * freq
        sine = jnp.sin(angle)
        turn_ref[2 * i] = jnp.cos(angle)
        turn_ref[2 * i + 1] = jnp.where(lane < dim // 2, -sine, sine)
    shape = allow_ref.shape
    query = owner(lax.rem(lax.broadcasted_iota(jnp.int32, shape, 0), total), me)
    key = owner(lax.broadcasted_iota(jnp.int32, shape, 1), me // 2)
    same = positions(query, len_ref)[0] == positions(key, len_ref)[0]
    allow_ref[...] = jnp.where(same & (key <= query), 1.0, 0.0).astype(F32)
    for copy in copies:
        copy.wait()


def join_kernel(a_ref, b_ref, o_ref):
    n = a_ref.shape[0]
    o_ref[:n] = a_ref[...]
    o_ref[n:] = b_ref[...]


def keyval_kernel(a_ref, b_ref, w_ref, *refs, order, spans):
    n = len(spans)
    sources, (x_out, keep_ref, give_ref), targets = refs[:n], refs[n : n + 3], refs[n + 3 : 2 * n + 3]
    x32, sems = refs[2 * n + 3 :]
    copies = fetches(sources, targets, spans, sems)
    for copy in copies:
        copy.start()
    count, rows = a_ref.shape[:2]
    for i in range(count):
        for base, ref in ((order[i], a_ref), (order[count + i], b_ref)):
            x32[rows * base : rows * (base + 1), :] = ref[i].astype(F32)
    x_out[...] = x32[...].astype(BF16)
    part = jnp.dot(x_out[...], w_ref[...], preferred_element_type=F32)
    width = keep_ref.shape[1]
    left, right = part[:, :width], part[:, width:]
    low = lax.axis_index("narrow") == 0
    keep_ref[...] = jnp.where(low, left, right)
    give_ref[...] = jnp.where(low, right, left)
    for copy in copies:
        copy.wait()


def pair_kernel(mine_ref, other_ref, out_ref):
    out_ref[...] = (mine_ref[...] + other_ref[...]).astype(BF16)


def multiply(x_ref, w_ref, out, at, lo=0, hi=None):
    width = (w_ref.shape[1] if hi is None else hi) - lo
    step = math.gcd(math.gcd(width, 512), lo)

    @pl.loop(0, width // step)
    def _(j):
        cols = pl.ds(pl.multiple_of(lo + j * step, step), step)
        part = jnp.dot(x_ref[...], w_ref[:, cols], preferred_element_type=F32)
        out[:, pl.ds(pl.multiple_of(at + j * step, step), step)] = part


def query_kernel(x_ref, w_ref, head_ref, *refs, spans):
    n = len(spans)
    sources, q_out, targets, sems = refs[:n], refs[n], refs[n + 1 : -1], refs[-1]
    copies = fetches(sources, targets, spans, sems)
    for copy in copies:
        copy.start()
    width = head_ref.shape[1]
    q_out[:, :width] = head_ref[...].astype(F32)
    multiply(x_ref, w_ref, q_out, width)
    for copy in copies:
        copy.wait()


def attend(mine_ref, other_ref, turn_ref, allow_ref, att):
    total, dim = turn_ref.shape[1:]
    low = lax.axis_index("narrow") == 0
    mine, other = mine_ref[:, :dim], other_ref[:, :dim]
    keys, values = jnp.where(low, mine, other), jnp.where(low, other, mine)
    summed = mine_ref[:, dim:] + other_ref[:, dim:]
    values = jnp.concatenate([values[total // 2 :], values[: total // 2]], axis=0).astype(BF16)

    def rotate(u, i):
        return (u * turn_ref[i] + pltpu.roll(u, dim // 2, 1) * turn_ref[i + 1]).astype(BF16)

    keys = rotate(keys, 2)
    heads = summed.shape[1] // dim
    stack = jnp.concatenate([rotate(summed[:, dim * h : dim * (h + 1)], 0) for h in range(heads)], axis=0)
    scores = lax.dot_general(stack, keys, (((1,), (1,)), ((), ())), preferred_element_type=F32)
    scores = scores / F32(math.sqrt(dim))
    scores = jnp.where(allow_ref[...] > 0, scores, F32(-1e30))
    weights = jnp.exp(scores - jnp.max(scores, axis=1, keepdims=True))
    probs = (weights / jnp.sum(weights, axis=1, keepdims=True)).astype(BF16)
    mixed = jnp.dot(probs, values, preferred_element_type=F32).astype(BF16)
    for h in range(heads):
        att[:, dim * h : dim * (h + 1)] = mixed[total * h : total * (h + 1), :]


def part_out(acc, keep_ref, send_ref):
    pieces = 2 * keep_ref.shape[0]
    rows = acc.shape[0] // pieces
    for s in range(0, pieces, 2):
        keep_ref[s // 2] = acc[rows * s : rows * (s + 1), :]
        send_ref[s // 2] = acc[rows * (s + 1) : rows * (s + 2), :].astype(BF16)


def output_kernel(*refs, first, parts, own, spans):
    n = len(spans)
    if first:
        head, refs = refs[:4], refs[4:]
    else:
        att, refs = refs[0], refs[1:]
    w_refs, refs = refs[:parts], refs[parts:]
    w_far = None
    if n or own:
        w_far, refs = refs[0], refs[1:]
    if first:
        att, refs = refs[0], refs[1:]
    keep_ref, send_ref, targets, refs = refs[0], refs[1], refs[2 : 2 + n], refs[2 + n :]
    acc, sems, mine = refs[0], refs[1], refs[2:]
    copies = fetches([w_far] * (len(own) + n), [*mine, *targets], [*own, *spans], sems)
    for copy in copies:
        copy.start()
    if first:
        attend(*head, att)
    at = 0
    for w_ref in w_refs:
        multiply(att, w_ref, acc, at)
        at += w_ref.shape[1]
    for copy, w_ref in zip(copies, mine):
        copy.wait()
        multiply(att, w_ref, acc, at)
        at += w_ref.shape[1]
    part_out(acc, keep_ref, send_ref)
    for copy in copies[len(own) :]:
        copy.wait()


def near_sum_kernel(*refs, parts):
    at = 0
    outs = refs[2 * parts :]
    for p in range(parts):
        keep_ref, got_ref = refs[2 * p : 2 * p + 2]
        width = keep_ref.shape[2]
        for k in range(keep_ref.shape[0]):
            part = keep_ref[k] + got_ref[k].astype(F32)
            outs[k][:, at : at + width] = part.astype(outs[k].dtype)
        at += width


def total_kernel(*refs):
    total = refs[0][...]
    for r in refs[1:-1]:
        total = total + r[...].astype(F32)
    refs[-1][...] = total.astype(BF16)


def swap(x, axis, size, bit):
    return lax.ppermute(x, axis, [(i, i ^ bit) for i in range(size)])


def shaped(*shape, dtype=F32):
    return jax.ShapeDtypeStruct(shape, dtype)


def plain_positions(lengths, total):
    index = jnp.arange(total, dtype=jnp.int32)
    ends = jnp.cumsum(lengths)
    past = index[:, None] >= ends[None, :]
    segment = jnp.sum(past.astype(jnp.int32), axis=1)
    offset = index - jnp.sum(jnp.where(past, lengths[None, :], 0), axis=1)
    return segment, offset


def plain_rotate(values, offset):
    half = values.shape[-1] // 2
    freq = theta_base ** (-(jnp.arange(half, dtype=F32) * 2.0) / values.shape[-1])
    angle = offset.astype(F32)[:, None] * freq[None, :]
    cosine = jnp.cos(angle)[:, None, :]
    sine = jnp.sin(angle)[:, None, :]
    first, second = values[..., :half], values[..., half:]
    return jnp.concatenate([first * cosine - second * sine, second * cosine + first * sine], axis=-1)


def plain_attend(query, keys, values, segment):
    total = query.shape[0]
    scores = jnp.einsum("qhd,khd->hqk", query, keys, preferred_element_type=F32) / jnp.sqrt(F32(query.shape[-1]))
    index = jnp.arange(total, dtype=jnp.int32)
    allowed = (segment[:, None] == segment[None, :]) & (index[None, :] <= index[:, None])
    scores = jnp.where(allowed[None], scores, F32(-1e30))
    weights = jnp.exp(scores - jnp.max(scores, axis=-1, keepdims=True))
    probs = (weights / jnp.sum(weights, axis=-1, keepdims=True)).astype(BF16)
    return jnp.einsum("hqk,khd->qhd", probs, values, preferred_element_type=F32).astype(BF16)


def plain(tokens, lengths, w_query, w_keyval, w_out):
    q_cols = w_query.shape[1]
    heads = q_cols // HEAD_DIM
    piece = lax.all_gather(tokens, "wide", axis=0, tiled=True)
    query_part = jnp.dot(piece, w_query, preferred_element_type=F32)
    keyval_part = jnp.dot(piece, w_keyval, preferred_element_type=F32)
    total = piece.shape[0]
    query = lax.psum(query_part, "narrow")
    summed = lax.psum(keyval_part, "narrow").astype(BF16)
    keyval = lax.all_gather(summed, "wide", axis=1, tiled=True)
    segment, offset = plain_positions(lengths, total)
    kv_width = KV_HEADS * HEAD_DIM
    keys = plain_rotate(keyval[:, :kv_width].astype(F32).reshape(total, KV_HEADS, HEAD_DIM), offset).astype(BF16)
    values = keyval[:, kv_width:].reshape(total, KV_HEADS, HEAD_DIM)
    head_ids = lax.axis_index("wide") * heads + jnp.arange(heads, dtype=jnp.int32)
    kv_ids = head_ids // (HEADS // KV_HEADS)
    query_rot = plain_rotate(query.reshape(total, -1, HEAD_DIM), offset).astype(BF16)
    attended = plain_attend(query_rot, jnp.take(keys, kv_ids, axis=1), jnp.take(values, kv_ids, axis=1), segment)
    mixed = lax.psum_scatter(
        jnp.dot(attended.reshape(total, -1), w_out, preferred_element_type=F32), "wide", scatter_dimension=0, tiled=True
    )
    return mixed.astype(BF16)


def local(tokens, lengths, w_query, w_keyval, w_out):
    wide = lax.axis_size("wide")
    rows, depth = tokens.shape
    total = rows * wide
    kv_cols, q_cols, out_cols = w_keyval.shape[1], w_query.shape[1], w_out.shape[1]
    heads = q_cols // HEAD_DIM

    bits = [1 << b for b in reversed(range(wide.bit_length() - 1))]
    o_cuts = [out_cols * k // 32 for k in CUTS]
    x, order, o_near = tokens[None], [0], []
    for i, bit in enumerate(bits):
        other = swap(x, "wide", wide, bit)
        w = None
        span = (o_cuts[i], o_cuts[i + 1])
        if i == 0:
            spans = [span] if span[1] > span[0] else []
            turn, allow, *pieces = call(
                functools.partial(tables_kernel, rows=rows, spans=spans),
                "tables",
                [lengths, *[w_out for _ in spans]],
                [shaped(4, total, HEAD_DIM), shaped(heads * total, total)] + [fetched(w_out, *s) for s in spans],
                [pltpu.SemaphoreType.DMA((1,)), pltpu.SMEM(lengths.shape, jnp.int32), pltpu.SemaphoreType.DMA],
                limit=2,
                far=1 + len(spans),
                hint=HINT,
            )
            o_near += pieces
            w = turn
        elif span[1] > span[0]:
            (w,) = ahead("ahead%d" % i, [w_out], [span], after=[x])
            o_near.append(w)
        order = order + [s ^ bit for s in order]
        if i < len(bits) - 1:
            (x,) = call(join_kernel, "join%d" % i, [x, other], [shaped(2 * x.shape[0], rows, depth, dtype=BF16)], limit=2, after=[] if w is None else [w], hint=JH[i])
    x, keep, give = call(
        functools.partial(keyval_kernel, order=order, spans=[]),
        "keyval",
        [x, other, near(w_keyval)],
        [shaped(total, depth, dtype=BF16)] + [shaped(total, HEAD_DIM)] * 2,
        [pltpu.VMEM((total, depth), F32), pltpu.SemaphoreType.DMA((1,))],
        limit=4,
        hint=KH,
        after=[o_near[-1]],
    )

    half = wide // 2
    given = swap(give, "narrow", 2, 1)
    (head,) = call(pair_kernel, "pair", [keep, given], [shaped(total, HEAD_DIM, dtype=BF16)], limit=1)
    routes = [(2 * s + n, 2 * ((2 * s + n) % wide) + s // half) for s in range(wide) for n in range(2)]
    sent = head
    head = lax.ppermute(head, ("wide", "narrow"), routes)
    if o_cuts[4] > o_cuts[3]:
        (w,) = ahead("ahead3", [w_out], [(o_cuts[3], o_cuts[4])], after=[sent])
        o_near.append(w)
    unit = out_cols * QSTEP // 32
    spans = [(lo, min(lo + unit, o_cuts[5])) for lo in range(o_cuts[4], o_cuts[5], unit)]
    q, *pieces = call(
        functools.partial(query_kernel, spans=spans),
        "query",
        [x, near(w_query), head] + [w_out] * len(spans),
        [QOUT((total, q_cols + HEAD_DIM), F32)] + [fetched(w_out, *span) for span in spans],
        [pltpu.SemaphoreType.DMA((len(spans),))],
        limit=2,
        far=len(spans),
        after=o_near[-1:],
    )
    o_near += pieces
    other = swap(q, "narrow", 2, 1)
    if o_cuts[6] > o_cuts[5]:
        (w,) = ahead("ahead4", [w_out], [(o_cuts[5], o_cuts[6])], after=[q])
        o_near.append(w)

    def output(name, head, weights, own, spans):
        own_cols = [hi - lo for lo, hi in own]
        width = sum(w.shape[1] for w in weights) + sum(own_cols)
        return call(
            functools.partial(output_kernel, first=len(head) > 1, parts=len(weights), own=own, spans=spans),
            name,
            [*head, *[near(w) for w in weights], *([w_out] if own or spans else [])],
            ([shaped(total, q_cols, dtype=BF16)] if len(head) > 1 else [])
            + [shaped(wide // 2, rows, width), shaped(wide // 2, rows, width, dtype=BF16)]
            + [fetched(w_out, *span) for span in spans],
            [pltpu.VMEM((total, width), F32), pltpu.SemaphoreType.DMA((max(1, len(own) + len(spans)),))]
            + [pltpu.VMEM((w_out.shape[0], cols), BF16) for cols in own_cols],
            limit=LIM,
            far=1 if own or spans else 0,
        )

    att, keep0, send0, o2 = output(
        "output0",
        [q, other, turn, allow],
        o_near,
        [span for span in [(o_cuts[6], o_cuts[7])] if span[1] > span[0]],
        [(o_cuts[7], o_cuts[8])],
    )
    got0 = swap(send0, "wide", wide, 1)
    keep1, send1 = output("output1", [att], [o2], [], [])
    got1 = swap(send1, "wide", wide, 1)
    mine, *others = call(
        functools.partial(near_sum_kernel, parts=2),
        "pairs",
        [keep0, got0, keep1, got1],
        [shaped(rows, out_cols)] + [shaped(rows, out_cols, dtype=BF16)] * (half - 1),
        limit=1,
    )
    back = {k: swap(others[k - 1], "wide", wide, 2 * k) for k in reversed(range(1, half))}
    return call(total_kernel, "total", [mine] + [back[k] for k in range(1, half)], [shaped(rows, out_cols, dtype=BF16)], limit=1)[0]


def solution(mesh):
    in_specs = (
        P(("groups", "wide"), "narrow"),
        P("groups"),
        P("narrow", "wide"),
        P("narrow", "wide"),
        P("wide", "narrow"),
    )
    out_specs = P(("groups", "wide"), "narrow")
    body = local if mesh.shape["wide"] == KV_HEADS and mesh.shape["narrow"] == 2 else plain
    return jax.shard_map(body, mesh=mesh, in_specs=in_specs, out_specs=out_specs, check_vma=False)
```

time: 160 us -> 54.5 us (0.34)
  blocking collectives: 111 us -> 0 us
  matrix products: 29 us -> 0 us
  Pallas kernels: 0 us -> 21.4 us
  starting transfers between devices: 0.01 us -> 16.3 us
  between operations: 14.2 us -> 0.22 us
  waiting for transfers between devices: 0.04 us -> 14 us
  other arithmetic: 1.82 us -> 0.01 us
    all_gather x2 -> x0, blocking collectives: 63.4 us -> none  [the longest x1 32.9 us: local(): piece = lax.all_gather(tokens, 'wide', axis=0, tiled=True)]
    unnamed x1 -> x0, blocking collectives: 44.4 us -> none
    dot_general x4 -> x0, matrix products: 28.7 us -> none  [the longest x1 12.8 us: local(): jnp.dot(attended, w_out, preferred_element_type=jnp.float32)]
    pallas_call x0 -> x13, Pallas kernels: none -> 21.4 us  [call(): pl.pallas_call(kernel, out_shape=tuple(outs), in_specs=specs, out_specs=(...]
    ppermute x0 -> x11, starting transfers between devices: none -> 16.3 us  [the longest x10 15.5 us: swap(): return lax.ppermute(x, axis, [(i, i ^ bit) for i in range(size)])]
    ppermute x0 -> x11, waiting for transfers between devices: none -> 14 us  [the longest x10 13.9 us: swap(): return lax.ppermute(x, axis, [(i, i ^ bit) for i in range(size)])]
    psum x1 -> x0, blocking collectives: 3.37 us -> none  [local(): summed = lax.psum(keyval_part, 'narrow').astype(jnp.bfloat16)]
    unnamed x7 -> x20, local copies, waits for them, and re-layouts: 0.71 us -> 2.5 us
  transfers between devices with their start and end apart: 1 -> 11, of which waited for: 0 -> 6; matrix products, arithmetic and copies ran while one was open for 3% -> 0% of each run, Pallas kernels for 0% -> 18%
where the time goes in v2:
time: 54.5 us; the launch traced here: 54.4 us
  Pallas kernels  21.4 us (39%)
  starting transfers between devices  16.3 us (30%)
  waiting for transfers between devices  14 us (26%)
  local copies, waits for them, and re-layouts  2.5 us (5%)
    pallas_call x13, Pallas kernels, call(): pl.pallas_call(kernel, out_shape=tuple(outs), in_specs=specs, out_specs=(...  21.4 us
    ppermute x10, starting transfers between devices, swap(): return lax.ppermute(x, axis, [(i, i ^ bit) for i in range(size)])  15.5 us
    ppermute x10, waiting for transfers between devices, swap(): return lax.ppermute(x, axis, [(i, i ^ bit) for i in range(size)])  13.9 us
    unnamed x20, local copies, waits for them, and re-layouts  2.5 us
  transfers between devices with their start and end apart: 11, of which 6 were waited for; matrix products, arithmetic and copies ran while one was open for 0% of the time, Pallas kernels for 18%

profile of v2, /device:TPU:0, one launch (start us, length us, event | category | flops | bytes accessed | tf_op | source)
XLA Modules:
  0.0 54.4 jit_solution(10907940727495385696)
XLA Ops:
  0.0 4.0 %collective-permute-start = (bf16[1,2,8192]{2,1,0:T(2,128)(2,1)}, bf16[1,2,8192]{2,1,0:T(2,128)(2,1)S(1)}, u32[]{:S(2)}, u32[]{:S(2)}) collective-permute-start(bf16[1,2,8192]{2,1,0:T(2,128)(2,1)} %bitcast.3), channel_id=1, source_target_pairs={{0,8},{2,10},{4,12},{6,14},{8,0},{10,2},{12,4},{14,6},{1,9},{3,11}... | collective-permute-start | bytes 98312 | tf_op jit(solution)/shard_map/ppermute | solution.py:285
  4.0 2.8 %tables.1 = (f32[4,16,128]{2,1,0:T(8,128)S(1)}, f32[256,16]{1,0:T(8,128)S(1)}, bf16[2048,1536]{1,0:T(8,128)(2,1)S(1)}) custom-call(s32[4]{0:T(128)} %refs_0_.1, bf16[2048,8192]{1,0:T(8,128)(2,1)} %refs_11_.1), custom_call_target="tpu_custom_call" | custom-call | bytes 1000 | tf_op jit(solution)/shard_map/tables/pallas_call | solution.py:52
  6.9 1.6 %collective-permute-start.1 = (bf16[2,2,8192]{2,1,0:T(2,128)(2,1)S(1)}, bf16[2,2,8192]{2,1,0:T(2,128)(2,1)S(1)}, u32[]{:S(2)}, u32[]{:S(2)}) collective-permute-start(bf16[2,2,8192]{2,1,0:T(2,128)(2,1)S(1)} %join0.1.refs_0_.refs_1_), channel_id=1, source_target_pairs={{0,4},{2,6},{4,0},{6,2},{8,12},{10,14},{12,8},{14,10},{1,5},{3,7},... | collective-permute-start | bytes 196616 | tf_op jit(solution)/shard_map/ppermute | solution.py:285
  8.6 2.1 %ahead1.1.refs_0_.refs_5_ = bf16[2048,768]{1,0:T(8,128)(2,1)S(1)} custom-call(bf16[2,2,8192]{2,1,0:T(2,128)(2,1)S(1)} %join0.1.refs_0_.refs_1_, bf16[2048,8192]{1,0:T(8,128)(2,1)} %refs_11_.1), custom_call_target="tpu_custom_call" | custom-call | bytes 1000 | tf_op jit(solution)/shard_map/ahead1/pallas_call | solution.py:52
  11.2 1.6 %collective-permute-start.2 = (bf16[4,2,8192]{2,1,0:T(2,128)(2,1)S(1)}, bf16[4,2,8192]{2,1,0:T(2,128)(2,1)S(1)}, u32[]{:S(2)}, u32[]{:S(2)}) collective-permute-start(bf16[4,2,8192]{2,1,0:T(2,128)(2,1)S(1)} %join1.1.refs_1_), channel_id=1, source_target_pairs={{0,2},{2,0},{4,6},{6,4},{8,10},{10,8},{12,14},{14,12},{1,3},{3,1},... | collective-permute-start | bytes 393224 | tf_op jit(solution)/shard_map/ppermute | solution.py:285
  12.8 3.4 %collective-permute-done.2.refs_2_ = bf16[4,2,8192]{2,1,0:T(2,128)(2,1)S(1)} collective-permute-done((bf16[4,2,8192]{2,1,0:T(2,128)(2,1)S(1)}, bf16[4,2,8192]{2,1,0:T(2,128)(2,1)S(1)}, u32[]{:S(2)}, u32[]{:S(2)}) %collective-permute-start.2) | collective-permute-done | bytes 131104 | tf_op jit(solution)/shard_map/ppermute | solution.py:285
  16.3 0.7 %keyval.1 = (bf16[16,8192]{1,0:T(8,128)(2,1)S(1)}, f32[16,128]{1,0:T(8,128)S(1)}, f32[16,128]{1,0:T(8,128)S(1)}) custom-call(bf16[2048,768]{1,0:T(8,128)(2,1)S(1)} %ahead1.1.refs_0_.refs_5_, bf16[4,2,8192]{2,1,0:T(2,128)(2,1)S(1)} %join1.1.refs_1_, bf16[4,2,8192]{2,1,0:T(2,128)(2,1)S(1)} %collective-permute-done.2.refs_2_, bf16[8192,256]{1,0:T(8,128)(2,1)S(1)} %copy-done), custom_call_target="tpu_custom_call" | custom-call | bytes 1000 | tf_op jit(solution)/shard_map/keyval/pallas_call | solution.py:52
  17.1 1.2 %collective-permute-done.3.other_ref = f32[16,128]{1,0:T(8,128)S(1)} collective-permute-done((f32[16,128]{1,0:T(8,128)S(1)}, f32[16,128]{1,0:T(8,128)S(1)}, u32[]{:S(2)}, u32[]{:S(2)}) %collective-permute-start.3) | collective-permute-done | bytes 8224 | tf_op jit(solution)/shard_map/ppermute | solution.py:285
  18.3 0.8 %collective-permute-start.4 = (bf16[16,128]{1,0:T(8,128)(2,1)S(1)}, bf16[16,128]{1,0:T(8,128)(2,1)S(1)}, u32[]{:S(2)}, u32[]{:S(2)}) collective-permute-start(bf16[16,128]{1,0:T(8,128)(2,1)S(1)} %pair.1.refs_0_), channel_id=1, source_target_pairs={{0,0},{1,2},{2,4},{3,6},{4,8},{5,10},{6,12},{7,14},{8,1},{9,3},{10... | collective-permute-start | bytes 12296 | tf_op jit(solution)/shard_map/ppermute | solution.py:396
  19.1 1.6 %ahead3.1.refs_0_.refs_6_ = bf16[2048,256]{1,0:T(8,128)(2,1)S(1)} custom-call(bf16[16,128]{1,0:T(8,128)(2,1)S(1)} %pair.1.refs_0_, bf16[2048,8192]{1,0:T(8,128)(2,1)} %refs_11_.1), custom_call_target="tpu_custom_call" | custom-call | bytes 1000 | tf_op jit(solution)/shard_map/ahead3/pallas_call | solution.py:52
  20.8 1.3 %slice-done.6 = s8[4194304]{0:T(1024)(128)(4,1)S(1)} async-done(((s8[33554432]{0:T(1024)(128)(4,1)}), s8[4194304]{0:T(1024)(128)(4,1)S(1)}, s32[]{:S(2)}) %slice-start.6) | async-done | bytes 4194328
  22.1 1.2 %slice-done.7 = s8[4194304]{0:T(1024)(128)(4,1)S(1)} async-done(((s8[33554432]{0:T(1024)(128)(4,1)}), s8[4194304]{0:T(1024)(128)(4,1)S(1)}, s32[]{:S(2)}) %slice-start.7) | async-done | bytes 4194328
  23.3 4.8 %query.1 = (f32[16,2176]{1,0:T(8,128)S(1)}, bf16[2048,1024]{1,0:T(8,128)(2,1)S(1)}, bf16[2048,1024]{1,0:T(8,128)(2,1)S(1)}, bf16[2048,1024]{1,0:T(8,128)(2,1)S(1)}) custom-call(bf16[2048,256]{1,0:T(8,128)(2,1)S(1)} %ahead3.1.refs_0_.refs_6_, bf16[16,8192]{1,0:T(8,128)(2,1)S(1)} %get-tuple-element.28.refs_1_, bf16[8192,2048]{1,0:T(8,128)(2,1)S(1)} %bitcast.2, ...), custom_call_target="tpu_custom_call" | custom-call | bytes 1000 | tf_op jit(solution)/shard_map/query/pallas_call | solution.py:52
  28.1 1.5 %collective-permute-start.5 = (f32[16,2176]{1,0:T(8,128)S(1)}, f32[16,2176]{1,0:T(8,128)S(1)}, u32[]{:S(2)}, u32[]{:S(2)}) collective-permute-start(f32[16,2176]{1,0:T(8,128)S(1)} %get-tuple-element.29.refs_0_), channel_id=1, source_target_pairs={{0,1},{1,0},{2,3},{3,2},{4,5},{5,4},{6,7},{7,6},{8,9},{9,8},{10,11... | collective-permute-start | bytes 417800 | tf_op jit(solution)/shard_map/ppermute | solution.py:285
  29.6 1.6 %ahead4.1.refs_10_ = bf16[2048,512]{1,0:T(8,128)(2,1)S(1)} custom-call(f32[16,2176]{1,0:T(8,128)S(1)} %get-tuple-element.29.refs_0_, bf16[2048,8192]{1,0:T(8,128)(2,1)} %refs_11_.1), custom_call_target="tpu_custom_call" | custom-call | bytes 1000 | tf_op jit(solution)/shard_map/ahead4/pallas_call | solution.py:52
  31.2 5.4 %output0.1 = (bf16[16,2048]{1,0:T(8,128)(2,1)S(1)}, f32[4,2,6144]{2,1,0:T(2,128)S(1)}, bf16[4,2,6144]{2,1,0:T(2,128)(2,1)S(1)}, bf16[2048,2048]{1,0:T(8,128)(2,1)S(1)}) custom-call(f32[16,2176]{1,0:T(8,128)S(1)} %get-tuple-element.29.refs_0_, f32[16,2176]{1,0:T(8,128)S(1)} %collective-permute-done.5.refs_1_, ...), custom_call_target="tpu_custom_call" | custom-call | bytes 1000 | tf_op jit(solution)/shard_map/output0/pallas_call | solution.py:52
  36.7 1.9 %collective-permute-start.6 = (bf16[4,2,6144]{2,1,0:T(2,128)(2,1)S(1)}, bf16[4,2,6144]{2,1,0:T(2,128)(2,1)S(1)}, u32[]{:S(2)}, u32[]{:S(2)}) collective-permute-start(bf16[4,2,6144]{2,1,0:T(2,128)(2,1)S(1)} %get-tuple-element.36), channel_id=1, source_target_pairs={{0,2},{2,0},{4,6},{6,4},{8,10},{10,8},{12,14},{14,12},{1,3},{3,1},... | collective-permute-start | bytes 294920 | tf_op jit(solution)/shard_map/ppermute | solution.py:285
  38.6 1.6 %output1.1 = (f32[4,2,2048]{2,1,0:T(2,128)S(1)}, bf16[4,2,2048]{2,1,0:T(2,128)(2,1)S(1)}) custom-call(bf16[16,2048]{1,0:T(8,128)(2,1)S(1)} %get-tuple-element.37.refs_0_, bf16[2048,2048]{1,0:T(8,128)(2,1)S(1)} %get-tuple-element.38.refs_1_), custom_call_target="tpu_custom_call" | custom-call | bytes 1000 | tf_op jit(solution)/shard_map/output1/pallas_call | solution.py:52
  40.4 3.7 %collective-permute-done.7.refs_3_ = bf16[4,2,2048]{2,1,0:T(2,128)(2,1)S(1)} collective-permute-done((bf16[4,2,2048]{2,1,0:T(2,128)(2,1)S(1)}, bf16[4,2,2048]{2,1,0:T(2,128)(2,1)S(1)}, u32[]{:S(2)}, u32[]{:S(2)}) %collective-permute-start.7) | collective-permute-done | bytes 32800 | tf_op jit(solution)/shard_map/ppermute | solution.py:285
  44.3 0.9 %collective-permute-start.8 = (bf16[2,8192]{1,0:T(2,128)(2,1)S(1)}, bf16[2,8192]{1,0:T(2,128)(2,1)S(1)}, u32[]{:S(2)}, u32[]{:S(2)}) collective-permute-start(bf16[2,8192]{1,0:T(2,128)(2,1)S(1)} %get-tuple-element.42), channel_id=1, source_target_pairs={{0,4},{2,6},{4,0},{6,2},{8,12},{10,14},{12,8},{14,10},{1,5},{3,7},... | collective-permute-start | bytes 98312 | tf_op jit(solution)/shard_map/ppermute | solution.py:285
  45.2 2.8 %collective-permute-start.9 = (bf16[2,8192]{1,0:T(2,128)(2,1)S(1)}, bf16[2,8192]{1,0:T(2,128)(2,1)S(1)}, u32[]{:S(2)}, u32[]{:S(2)}) collective-permute-start(bf16[2,8192]{1,0:T(2,128)(2,1)S(1)} %get-tuple-element.43), channel_id=1, source_target_pairs={{0,8},{2,10},{4,12},{6,14},{8,0},{10,2},{12,4},{14,6},{1,9},{3,11}... | collective-permute-start | bytes 98312 | tf_op jit(solution)/shard_map/ppermute | solution.py:285
  48.0 0.7 %collective-permute-start.10 = (bf16[2,8192]{1,0:T(2,128)(2,1)S(1)}, bf16[2,8192]{1,0:T(2,128)(2,1)S(1)}, u32[]{:S(2)}, u32[]{:S(2)}) collective-permute-start(bf16[2,8192]{1,0:T(2,128)(2,1)S(1)} %get-tuple-element.44), channel_id=1, source_target_pairs={{0,12},{2,14},{4,8},{6,10},{8,4},{10,6},{12,0},{14,2},{1,13},{3,15... | collective-permute-start | bytes 98312 | tf_op jit(solution)/shard_map/ppermute | solution.py:285
  48.7 1.5 %collective-permute-done.9.refs_2_ = bf16[2,8192]{1,0:T(2,128)(2,1)S(1)} collective-permute-done((bf16[2,8192]{1,0:T(2,128)(2,1)S(1)}, bf16[2,8192]{1,0:T(2,128)(2,1)S(1)}, u32[]{:S(2)}, u32[]{:S(2)}) %collective-permute-start.9) | collective-permute-done | bytes 32800 | tf_op jit(solution)/shard_map/ppermute | solution.py:285
  50.2 3.5 %collective-permute-done.10.refs_3_ = bf16[2,8192]{1,0:T(2,128)(2,1)S(1)} collective-permute-done((bf16[2,8192]{1,0:T(2,128)(2,1)S(1)}, bf16[2,8192]{1,0:T(2,128)(2,1)S(1)}, u32[]{:S(2)}, u32[]{:S(2)}) %collective-permute-start.10) | collective-permute-done | bytes 32800 | tf_op jit(solution)/shard_map/ppermute | solution.py:285
  (32 shorter events, 1.8 us)
Async XLA Ops:
  0.0 6.9 %copy-start.1 = (bf16[2,8192]{1,0:T(2,128)(2,1)S(1)}, bf16[2,8192]{1,0:T(2,128)(2,1)}, u32[]{:S(2)}) copy-start(bf16[2,8192]{1,0:T(2,128)(2,1)} %param.5) | copy-start | bytes 98308
  0.0 6.9 %collective-permute-start = (bf16[1,2,8192]{2,1,0:T(2,128)(2,1)}, bf16[1,2,8192]{2,1,0:T(2,128)(2,1)S(1)}, u32[]{:S(2)}, u32[]{:S(2)}) collective-permute-start(bf16[1,2,8192]{2,1,0:T(2,128)(2,1)} %bitcast.3), channel_id=1, source_target_pairs={{0,8},{2,10},{4,12},{6,14},{8,0},{10,2},{12,4},{14,6},{1,9},{3,11}... | collective-permute-start | bytes 98312 | tf_op jit(solution)/shard_map/ppermute | solution.py:285
  6.9 4.3 %collective-permute-start.1 = (bf16[2,2,8192]{2,1,0:T(2,128)(2,1)S(1)}, bf16[2,2,8192]{2,1,0:T(2,128)(2,1)S(1)}, u32[]{:S(2)}, u32[]{:S(2)}) collective-permute-start(bf16[2,2,8192]{2,1,0:T(2,128)(2,1)S(1)} %join0.1.refs_0_.refs_1_), channel_id=1, source_target_pairs={{0,4},{2,6},{4,0},{6,2},{8,12},{10,14},{12,8},{14,10},{1,5},{3,7},... | collective-permute-start | bytes 196616 | tf_op jit(solution)/shard_map/ppermute | solution.py:285
  8.5 7.8 %copy-start = (bf16[8192,256]{1,0:T(8,128)(2,1)S(1)}, bf16[8192,256]{1,0:T(8,128)(2,1)}, u32[]{:S(2)}) copy-start(bf16[8192,256]{1,0:T(8,128)(2,1)} %refs_3_.1) | copy-start | bytes 12582916
  8.5 12.2 %slice-start = ((s8[33554432]{0:T(1024)(128)(4,1)}), s8[4194304]{0:T(1024)(128)(4,1)S(1)}, s32[]{:S(2)}) async-start(s8[33554432]{0:T(1024)(128)(4,1)} %bitcast.1), calls=%async_computation | async-start | bytes 8388608
  8.5 12.2 %slice-start.1 = ((s8[33554432]{0:T(1024)(128)(4,1)}), s8[4194304]{0:T(1024)(128)(4,1)S(1)}, s32[]{:S(2)}) async-start(s8[33554432]{0:T(1024)(128)(4,1)} %bitcast.1), calls=%async_computation.1 | async-start | bytes 8388608
  8.5 12.2 %slice-start.2 = ((s8[33554432]{0:T(1024)(128)(4,1)}), s8[4194304]{0:T(1024)(128)(4,1)S(1)}, s32[]{:S(2)}) async-start(s8[33554432]{0:T(1024)(128)(4,1)} %bitcast.1), calls=%async_computation.2 | async-start | bytes 8388608
  8.5 12.2 %slice-start.3 = ((s8[33554432]{0:T(1024)(128)(4,1)}), s8[4194304]{0:T(1024)(128)(4,1)S(1)}, s32[]{:S(2)}) async-start(s8[33554432]{0:T(1024)(128)(4,1)} %bitcast.1), calls=%async_computation.3 | async-start | bytes 8388608
  11.2 9.5 %slice-start.4 = ((s8[33554432]{0:T(1024)(128)(4,1)}), s8[4194304]{0:T(1024)(128)(4,1)S(1)}, s32[]{:S(2)}) async-start(s8[33554432]{0:T(1024)(128)(4,1)} %bitcast.1), calls=%async_computation.4 | async-start | bytes 8388608
  11.2 5.0 %collective-permute-start.2 = (bf16[4,2,8192]{2,1,0:T(2,128)(2,1)S(1)}, bf16[4,2,8192]{2,1,0:T(2,128)(2,1)S(1)}, u32[]{:S(2)}, u32[]{:S(2)}) collective-permute-start(bf16[4,2,8192]{2,1,0:T(2,128)(2,1)S(1)} %join1.1.refs_1_), channel_id=1, source_target_pairs={{0,2},{2,0},{4,6},{6,4},{8,10},{10,8},{12,14},{14,12},{1,3},{3,1},... | collective-permute-start | bytes 393224 | tf_op jit(solution)/shard_map/ppermute | solution.py:285
  17.0 1.2 %collective-permute-start.3 = (f32[16,128]{1,0:T(8,128)S(1)}, f32[16,128]{1,0:T(8,128)S(1)}, u32[]{:S(2)}, u32[]{:S(2)}) collective-permute-start(f32[16,128]{1,0:T(8,128)S(1)} %get-tuple-element.27), channel_id=1, source_target_pairs={{0,1},{1,0},{2,3},{3,2},{4,5},{5,4},{6,7},{7,6},{8,9},{9,8},{10,11... | collective-permute-start | bytes 24584 | tf_op jit(solution)/shard_map/ppermute | solution.py:285
  18.3 2.5 %slice-start.5 = ((s8[33554432]{0:T(1024)(128)(4,1)}), s8[4194304]{0:T(1024)(128)(4,1)S(1)}, s32[]{:S(2)}) async-start(s8[33554432]{0:T(1024)(128)(4,1)} %bitcast.1), calls=%async_computation.5 | async-start | bytes 8388608
  18.3 3.8 %slice-start.6 = ((s8[33554432]{0:T(1024)(128)(4,1)}), s8[4194304]{0:T(1024)(128)(4,1)S(1)}, s32[]{:S(2)}) async-start(s8[33554432]{0:T(1024)(128)(4,1)} %bitcast.1), calls=%async_computation.6 | async-start | bytes 8388608
  18.3 5.0 %slice-start.7 = ((s8[33554432]{0:T(1024)(128)(4,1)}), s8[4194304]{0:T(1024)(128)(4,1)S(1)}, s32[]{:S(2)}) async-start(s8[33554432]{0:T(1024)(128)(4,1)} %bitcast.1), calls=%async_computation.7 | async-start | bytes 8388608
  18.3 2.4 %collective-permute-start.4 = (bf16[16,128]{1,0:T(8,128)(2,1)S(1)}, bf16[16,128]{1,0:T(8,128)(2,1)S(1)}, u32[]{:S(2)}, u32[]{:S(2)}) collective-permute-start(bf16[16,128]{1,0:T(8,128)(2,1)S(1)} %pair.1.refs_0_), channel_id=1, source_target_pairs={{0,0},{1,2},{2,4},{3,6},{4,8},{5,10},{6,12},{7,14},{8,1},{9,3},{10... | collective-permute-start | bytes 12296 | tf_op jit(solution)/shard_map/ppermute | solution.py:396
  28.1 3.2 %collective-permute-start.5 = (f32[16,2176]{1,0:T(8,128)S(1)}, f32[16,2176]{1,0:T(8,128)S(1)}, u32[]{:S(2)}, u32[]{:S(2)}) collective-permute-start(f32[16,2176]{1,0:T(8,128)S(1)} %get-tuple-element.29.refs_0_), channel_id=1, source_target_pairs={{0,1},{1,0},{2,3},{3,2},{4,5},{5,4},{6,7},{7,6},{8,9},{9,8},{10,11... | collective-permute-start | bytes 417800 | tf_op jit(solution)/shard_map/ppermute | solution.py:285
  36.7 7.5 %collective-permute-start.6 = (bf16[4,2,6144]{2,1,0:T(2,128)(2,1)S(1)}, bf16[4,2,6144]{2,1,0:T(2,128)(2,1)S(1)}, u32[]{:S(2)}, u32[]{:S(2)}) collective-permute-start(bf16[4,2,6144]{2,1,0:T(2,128)(2,1)S(1)} %get-tuple-element.36), channel_id=1, source_target_pairs={{0,2},{2,0},{4,6},{6,4},{8,10},{10,8},{12,14},{14,12},{1,3},{3,1},... | collective-permute-start | bytes 294920 | tf_op jit(solution)/shard_map/ppermute | solution.py:285
  40.2 4.0 %collective-permute-start.7 = (bf16[4,2,2048]{2,1,0:T(2,128)(2,1)S(1)}, bf16[4,2,2048]{2,1,0:T(2,128)(2,1)S(1)}, u32[]{:S(2)}, u32[]{:S(2)}) collective-permute-start(bf16[4,2,2048]{2,1,0:T(2,128)(2,1)S(1)} %get-tuple-element.40), channel_id=1, source_target_pairs={{0,2},{2,0},{4,6},{6,4},{8,10},{10,8},{12,14},{14,12},{1,3},{3,1},... | collective-permute-start | bytes 98312 | tf_op jit(solution)/shard_map/ppermute | solution.py:285
  44.3 4.5 %collective-permute-start.8 = (bf16[2,8192]{1,0:T(2,128)(2,1)S(1)}, bf16[2,8192]{1,0:T(2,128)(2,1)S(1)}, u32[]{:S(2)}, u32[]{:S(2)}) collective-permute-start(bf16[2,8192]{1,0:T(2,128)(2,1)S(1)} %get-tuple-element.42), channel_id=1, source_target_pairs={{0,4},{2,6},{4,0},{6,2},{8,12},{10,14},{12,8},{14,10},{1,5},{3,7},... | collective-permute-start | bytes 98312 | tf_op jit(solution)/shard_map/ppermute | solution.py:285
  45.2 5.0 %collective-permute-start.9 = (bf16[2,8192]{1,0:T(2,128)(2,1)S(1)}, bf16[2,8192]{1,0:T(2,128)(2,1)S(1)}, u32[]{:S(2)}, u32[]{:S(2)}) collective-permute-start(bf16[2,8192]{1,0:T(2,128)(2,1)S(1)} %get-tuple-element.43), channel_id=1, source_target_pairs={{0,8},{2,10},{4,12},{6,14},{8,0},{10,2},{12,4},{14,6},{1,9},{3,11}... | collective-permute-start | bytes 98312 | tf_op jit(solution)/shard_map/ppermute | solution.py:285
  48.0 5.7 %collective-permute-start.10 = (bf16[2,8192]{1,0:T(2,128)(2,1)S(1)}, bf16[2,8192]{1,0:T(2,128)(2,1)S(1)}, u32[]{:S(2)}, u32[]{:S(2)}) collective-permute-start(bf16[2,8192]{1,0:T(2,128)(2,1)S(1)} %get-tuple-element.44), channel_id=1, source_target_pairs={{0,12},{2,14},{4,8},{6,10},{8,4},{10,6},{12,0},{14,2},{1,13},{3,15... | collective-permute-start | bytes 98312 | tf_op jit(solution)/shard_map/ppermute | solution.py:285

commit v3 on v2

--- a/solution.py
+++ b/solution.py
@@ -15,7 +15,7 @@
 F32 = jnp.float32
 BF16 = jnp.bfloat16
 MIB = 1 << 20
-CUTS = (0, 6, 9, 9, 10, 22, 24, 24, 32)
+CUTS = (0, 6, 6, 9, 10, 22, 24, 24, 32)
 QSTEP = 4
 QOUT = pltpu.VMEM
 LIM = 3
@@ -142,10 +142,9 @@
         copy.wait()
 
 
-def join_kernel(a_ref, b_ref, o_ref):
-    n = a_ref.shape[0]
-    o_ref[:n] = a_ref[...]
-    o_ref[n:] = b_ref[...]
+def join_kernel(*refs):
+    for i, ref in enumerate(refs[:-1]):
+        refs[-1][i] = ref[...]
 
 
 def keyval_kernel(a_ref, b_ref, w_ref, *refs, order, spans):
@@ -350,33 +349,30 @@
     kv_cols, q_cols, out_cols = w_keyval.shape[1], w_query.shape[1], w_out.shape[1]
     heads = q_cols // HEAD_DIM
 
-    bits = [1 << b for b in reversed(range(wide.bit_length() - 1))]
     o_cuts = [out_cols * k // 32 for k in CUTS]
-    x, order, o_near = tokens[None], [0], []
-    for i, bit in enumerate(bits):
-        other = swap(x, "wide", wide, bit)
-        w = None
-        span = (o_cuts[i], o_cuts[i + 1])
-        if i == 0:
-            spans = [span] if span[1] > span[0] else []
-            turn, allow, *pieces = call(
-                functools.partial(tables_kernel, rows=rows, spans=spans),
-                "tables",
-                [lengths, *[w_out for _ in spans]],
-                [shaped(4, total, HEAD_DIM), shaped(heads * total, total)] + [fetched(w_out, *s) for s in spans],
-                [pltpu.SemaphoreType.DMA((1,)), pltpu.SMEM(lengths.shape, jnp.int32), pltpu.SemaphoreType.DMA],
-                limit=2,
-                far=1 + len(spans),
-                hint=HINT,
-            )
-            o_near += pieces
-            w = turn
-        elif span[1] > span[0]:
-            (w,) = ahead("ahead%d" % i, [w_out], [span], after=[x])
-            o_near.append(w)
-        order = order + [s ^ bit for s in order]
-        if i < len(bits) - 1:
-            (x,) = call(join_kernel, "join%d" % i, [x, other], [shaped(2 * x.shape[0], rows, depth, dtype=BF16)], limit=2, after=[] if w is None else [w], hint=JH[i])
+    o_near, spans = [], [(o_cuts[0], o_cuts[1])]
+    along = list(reversed(range(2, wide, 2)))
+    others = [swap(tokens, "wide", wide, bit) for bit in along]
+    turn, allow, w = call(
+        functools.partial(tables_kernel, rows=rows, spans=spans),
+        "tables",
+        [lengths, w_out],
+        [shaped(4, total, HEAD_DIM), shaped(heads * total, total)] + [fetched(w_out, *s) for s in spans],
+        [pltpu.SemaphoreType.DMA((1,)), pltpu.SMEM(lengths.shape, jnp.int32), pltpu.SemaphoreType.DMA],
+        limit=2,
+        far=2,
+        hint=HINT,
+    )
+    o_near.append(w)
+    order = [*along, 0]
+    (x,) = call(
+        join_kernel, "join", [*others, tokens], [shaped(len(order), rows, depth, dtype=BF16)], limit=2, after=[turn], hint=JH[0]
+    )
+    order = order + [s ^ 1 for s in order]
+    other = swap(x, "wide", wide, 1)
+    if o_cuts[3] > o_cuts[1]:
+        (w,) = ahead("ahead1", [w_out], [(o_cuts[1], o_cuts[3])], after=[x])
+        o_near.append(w)
     x, keep, give = call(
         functools.partial(keyval_kernel, order=order, spans=[]),
         "keyval",
@@ -449,7 +445,7 @@
         limit=1,
     )
     back = {k: swap(others[k - 1], "wide", wide, 2 * k) for k in reversed(range(1, half))}
-    return call(total_kernel, "total", [mine] + [back[k] for k in range(1, half)], [shaped(rows, out_cols, dtype=BF16)], limit=1)[0]
+    return call(total_kernel, "total", [mine] + [back[k] for k in reversed(range(1, half))], [shaped(rows, out_cols, dtype=BF16)], limit=1)[0]
 
 
 def solution(mesh):

time: 54.5 us -> 50.5 us (0.927)
  waiting for transfers between devices: 14 us -> 9.84 us
  starting transfers between devices: 16.3 us -> 14.7 us
  local copies, waits for them, and re-layouts: 2.5 us -> 3.75 us
    ppermute x10 -> x11, waiting for transfers between devices: 13.9 us -> 9.83 us  [swap(): return lax.ppermute(x, axis, [(i, i ^ bit) for i in range(size)])]
    ppermute x10 -> x11, starting transfers between devices: 15.5 us -> 14 us  [swap(): return lax.ppermute(x, axis, [(i, i ^ bit) for i in range(size)])]
    unnamed x20, local copies, waits for them, and re-layouts: 2.5 us -> 3.75 us
    pallas_call x13 -> x12, Pallas kernels: 21.4 us -> 21.8 us  [call(): pl.pallas_call(kernel, out_shape=tuple(outs), in_specs=specs, out_specs=(...]
  transfers between devices with their start and end apart: 11 -> 12, of which waited for: 6 -> 6; matrix products, arithmetic and copies ran while one was open for 0% -> 0% of each run, Pallas kernels for 18% -> 20%
where the time goes in v3:
time: 50.5 us; the launch traced here: 50.4 us
  Pallas kernels  21.8 us (43%)
  starting transfers between devices  14.7 us (29%)
  waiting for transfers between devices  9.84 us (19%)
  local copies, waits for them, and re-layouts  3.75 us (7%)
    pallas_call x12, Pallas kernels, call(): pl.pallas_call(kernel, out_shape=tuple(outs), in_specs=specs, out_specs=(...  21.8 us
    ppermute x11, starting transfers between devices, swap(): return lax.ppermute(x, axis, [(i, i ^ bit) for i in range(size)])  14 us
    ppermute x11, waiting for transfers between devices, swap(): return lax.ppermute(x, axis, [(i, i ^ bit) for i in range(size)])  9.83 us
    unnamed x20, local copies, waits for them, and re-layouts  3.75 us
  transfers between devices with their start and end apart: 12, of which 6 were waited for; matrix products, arithmetic and copies ran while one was open for 0% of the time, Pallas kernels for 20%

profile of v3, /device:TPU:0, one launch (start us, length us, event | category | flops | bytes accessed | tf_op | source)
XLA Modules:
  0.0 50.4 jit_solution(765596785041959691)
XLA Ops:
  0.0 4.0 %collective-permute-start.1 = (bf16[2,8192]{1,0:T(2,128)(2,1)}, bf16[2,8192]{1,0:T(2,128)(2,1)S(1)}, u32[]{:S(2)}, u32[]{:S(2)}) collective-permute-start(bf16[2,8192]{1,0:T(2,128)(2,1)} %refs_4_.2), channel_id=1, source_target_pairs={{0,8},{2,10},{4,12},{6,14},{8,0},{10,2},{12,4},{14,6},{1,9},{3,11}... | collective-permute-start | bytes 98312 | tf_op jit(solution)/shard_map/ppermute | solution.py:284
  4.0 1.3 %collective-permute-start = (bf16[2,8192]{1,0:T(2,128)(2,1)}, bf16[2,8192]{1,0:T(2,128)(2,1)S(1)}, u32[]{:S(2)}, u32[]{:S(2)}) collective-permute-start(bf16[2,8192]{1,0:T(2,128)(2,1)} %refs_4_.2), channel_id=1, source_target_pairs={{0,12},{2,14},{4,8},{6,10},{8,4},{10,6},{12,0},{14,2},{1,13},{3,15... | collective-permute-start | bytes 98312 | tf_op jit(solution)/shard_map/ppermute | solution.py:284
  5.6 2.8 %tables.1 = (f32[4,16,128]{2,1,0:T(8,128)S(1)}, f32[256,16]{1,0:T(8,128)S(1)}, bf16[2048,1536]{1,0:T(8,128)(2,1)S(1)}) custom-call(s32[4]{0:T(128)} %refs_0_.1, bf16[2048,8192]{1,0:T(8,128)(2,1)} %refs_11_.1), custom_call_target="tpu_custom_call" | custom-call | bytes 1000 | tf_op jit(solution)/shard_map/tables/pallas_call | solution.py:52
  8.4 1.5 %collective-permute-done.refs_1_ = bf16[2,8192]{1,0:T(2,128)(2,1)S(1)} collective-permute-done((bf16[2,8192]{1,0:T(2,128)(2,1)}, bf16[2,8192]{1,0:T(2,128)(2,1)S(1)}, u32[]{:S(2)}, u32[]{:S(2)}) %collective-permute-start) | collective-permute-done | bytes 32800 | tf_op jit(solution)/shard_map/ppermute | solution.py:284
  10.0 1.6 %collective-permute-start.3 = (bf16[4,2,8192]{2,1,0:T(2,128)(2,1)S(1)}, bf16[4,2,8192]{2,1,0:T(2,128)(2,1)S(1)}, u32[]{:S(2)}, u32[]{:S(2)}) collective-permute-start(bf16[4,2,8192]{2,1,0:T(2,128)(2,1)S(1)} %join.1.refs_0_.refs_1_), channel_id=1, source_target_pairs={{0,2},{2,0},{4,6},{6,4},{8,10},{10,8},{12,14},{14,12},{1,3},{3,1},... | collective-permute-start | bytes 393224 | tf_op jit(solution)/shard_map/ppermute | solution.py:284
  11.6 2.1 %ahead1.1.refs_0_.refs_5_ = bf16[2048,768]{1,0:T(8,128)(2,1)S(1)} custom-call(bf16[4,2,8192]{2,1,0:T(2,128)(2,1)S(1)} %join.1.refs_0_.refs_1_, bf16[2048,8192]{1,0:T(8,128)(2,1)} %refs_11_.1), custom_call_target="tpu_custom_call" | custom-call | bytes 1000 | tf_op jit(solution)/shard_map/ahead1/pallas_call | solution.py:52
  13.7 1.4 %collective-permute-done.3.refs_2_ = bf16[4,2,8192]{2,1,0:T(2,128)(2,1)S(1)} collective-permute-done((bf16[4,2,8192]{2,1,0:T(2,128)(2,1)S(1)}, bf16[4,2,8192]{2,1,0:T(2,128)(2,1)S(1)}, u32[]{:S(2)}, u32[]{:S(2)}) %collective-permute-start.3) | collective-permute-done | bytes 131104 | tf_op jit(solution)/shard_map/ppermute | solution.py:284
  15.0 0.7 %keyval.1 = (bf16[16,8192]{1,0:T(8,128)(2,1)S(1)}, f32[16,128]{1,0:T(8,128)S(1)}, f32[16,128]{1,0:T(8,128)S(1)}) custom-call(bf16[2048,768]{1,0:T(8,128)(2,1)S(1)} %ahead1.1.refs_0_.refs_5_, bf16[4,2,8192]{2,1,0:T(2,128)(2,1)S(1)} %join.1.refs_0_.refs_1_, bf16[4,2,8192]{2,1,0:T(2,128)(2,1)S(1)} %collective-permute-done.3.refs_2_, bf16[8192,256]{1,0:T(8,128)(2,1)S(1)} %copy-done), custom_call_target="tpu_custom_call" | custom-call | bytes 1000 | tf_op jit(solution)/shard_map/keyval/pallas_call | solution.py:52
  15.8 1.2 %collective-permute-done.4.other_ref = f32[16,128]{1,0:T(8,128)S(1)} collective-permute-done((f32[16,128]{1,0:T(8,128)S(1)}, f32[16,128]{1,0:T(8,128)S(1)}, u32[]{:S(2)}, u32[]{:S(2)}) %collective-permute-start.4) | collective-permute-done | bytes 8224 | tf_op jit(solution)/shard_map/ppermute | solution.py:284
  17.0 0.8 %collective-permute-start.5 = (bf16[16,128]{1,0:T(8,128)(2,1)S(1)}, bf16[16,128]{1,0:T(8,128)(2,1)S(1)}, u32[]{:S(2)}, u32[]{:S(2)}) collective-permute-start(bf16[16,128]{1,0:T(8,128)(2,1)S(1)} %pair.1.refs_0_), channel_id=1, source_target_pairs={{0,0},{1,2},{2,4},{3,6},{4,8},{5,10},{6,12},{7,14},{8,1},{9,3},{10... | collective-permute-start | bytes 12296 | tf_op jit(solution)/shard_map/ppermute | solution.py:392
  17.8 2.1 %ahead3.1.refs_0_.refs_6_ = bf16[2048,256]{1,0:T(8,128)(2,1)S(1)} custom-call(bf16[16,128]{1,0:T(8,128)(2,1)S(1)} %pair.1.refs_0_, bf16[2048,8192]{1,0:T(8,128)(2,1)} %refs_11_.1), custom_call_target="tpu_custom_call" | custom-call | bytes 1000 | tf_op jit(solution)/shard_map/ahead3/pallas_call | solution.py:52
  20.0 1.3 %slice-done.5 = s8[4194304]{0:T(1024)(128)(4,1)S(1)} async-done(((s8[33554432]{0:T(1024)(128)(4,1)}), s8[4194304]{0:T(1024)(128)(4,1)S(1)}, s32[]{:S(2)}) %slice-start.5) | async-done | bytes 4194328
  21.3 1.2 %slice-done.6 = s8[4194304]{0:T(1024)(128)(4,1)S(1)} async-done(((s8[33554432]{0:T(1024)(128)(4,1)}), s8[4194304]{0:T(1024)(128)(4,1)S(1)}, s32[]{:S(2)}) %slice-start.6) | async-done | bytes 4194328
  22.5 1.2 %slice-done.7 = s8[4194304]{0:T(1024)(128)(4,1)S(1)} async-done(((s8[33554432]{0:T(1024)(128)(4,1)}), s8[4194304]{0:T(1024)(128)(4,1)S(1)}, s32[]{:S(2)}) %slice-start.7) | async-done | bytes 4194328
  23.7 4.8 %query.1 = (f32[16,2176]{1,0:T(8,128)S(1)}, bf16[2048,1024]{1,0:T(8,128)(2,1)S(1)}, bf16[2048,1024]{1,0:T(8,128)(2,1)S(1)}, bf16[2048,1024]{1,0:T(8,128)(2,1)S(1)}) custom-call(bf16[2048,256]{1,0:T(8,128)(2,1)S(1)} %ahead3.1.refs_0_.refs_6_, bf16[16,8192]{1,0:T(8,128)(2,1)S(1)} %get-tuple-element.28.refs_1_, bf16[8192,2048]{1,0:T(8,128)(2,1)S(1)} %bitcast.1, ...), custom_call_target="tpu_custom_call" | custom-call | bytes 1000 | tf_op jit(solution)/shard_map/query/pallas_call | solution.py:52
  28.6 1.6 %ahead4.1.refs_10_ = bf16[2048,512]{1,0:T(8,128)(2,1)S(1)} custom-call(f32[16,2176]{1,0:T(8,128)S(1)} %get-tuple-element.29.refs_0_, bf16[2048,8192]{1,0:T(8,128)(2,1)} %refs_11_.1), custom_call_target="tpu_custom_call" | custom-call | bytes 1000 | tf_op jit(solution)/shard_map/ahead4/pallas_call | solution.py:52
  30.2 5.4 %output0.1 = (bf16[16,2048]{1,0:T(8,128)(2,1)S(1)}, f32[4,2,6144]{2,1,0:T(2,128)S(1)}, bf16[4,2,6144]{2,1,0:T(2,128)(2,1)S(1)}, bf16[2048,2048]{1,0:T(8,128)(2,1)S(1)}) custom-call(f32[16,2176]{1,0:T(8,128)S(1)} %get-tuple-element.29.refs_0_, f32[16,2176]{1,0:T(8,128)S(1)} %collective-permute-done.6.refs_1_, ...), custom_call_target="tpu_custom_call" | custom-call | bytes 1000 | tf_op jit(solution)/shard_map/output0/pallas_call | solution.py:52
  35.6 1.6 %collective-permute-start.7 = (bf16[4,2,6144]{2,1,0:T(2,128)(2,1)S(1)}, bf16[4,2,6144]{2,1,0:T(2,128)(2,1)S(1)}, u32[]{:S(2)}, u32[]{:S(2)}) collective-permute-start(bf16[4,2,6144]{2,1,0:T(2,128)(2,1)S(1)} %get-tuple-element.36), channel_id=1, source_target_pairs={{0,2},{2,0},{4,6},{6,4},{8,10},{10,8},{12,14},{14,12},{1,3},{3,1},... | collective-permute-start | bytes 294920 | tf_op jit(solution)/shard_map/ppermute | solution.py:284
  37.2 1.6 %output1.1 = (f32[4,2,2048]{2,1,0:T(2,128)S(1)}, bf16[4,2,2048]{2,1,0:T(2,128)(2,1)S(1)}) custom-call(bf16[16,2048]{1,0:T(8,128)(2,1)S(1)} %get-tuple-element.37.refs_0_, bf16[2048,2048]{1,0:T(8,128)(2,1)S(1)} %get-tuple-element.38.refs_1_), custom_call_target="tpu_custom_call" | custom-call | bytes 1000 | tf_op jit(solution)/shard_map/output1/pallas_call | solution.py:52
  39.4 3.4 %collective-permute-done.8.refs_3_ = bf16[4,2,2048]{2,1,0:T(2,128)(2,1)S(1)} collective-permute-done((bf16[4,2,2048]{2,1,0:T(2,128)(2,1)S(1)}, bf16[4,2,2048]{2,1,0:T(2,128)(2,1)S(1)}, u32[]{:S(2)}, u32[]{:S(2)}) %collective-permute-start.8) | collective-permute-done | bytes 32800 | tf_op jit(solution)/shard_map/ppermute | solution.py:284
  42.9 2.0 %collective-permute-start.9 = (bf16[2,8192]{1,0:T(2,128)(2,1)S(1)}, bf16[2,8192]{1,0:T(2,128)(2,1)S(1)}, u32[]{:S(2)}, u32[]{:S(2)}) collective-permute-start(bf16[2,8192]{1,0:T(2,128)(2,1)S(1)} %get-tuple-element.42), channel_id=1, source_target_pairs={{0,12},{2,14},{4,8},{6,10},{8,4},{10,6},{12,0},{14,2},{1,13},{3,15... | collective-permute-start | bytes 98312 | tf_op jit(solution)/shard_map/ppermute | solution.py:284
  44.9 2.4 %collective-permute-start.11 = (bf16[2,8192]{1,0:T(2,128)(2,1)S(1)}, bf16[2,8192]{1,0:T(2,128)(2,1)S(1)}, u32[]{:S(2)}, u32[]{:S(2)}) collective-permute-start(bf16[2,8192]{1,0:T(2,128)(2,1)S(1)} %get-tuple-element.44), channel_id=1, source_target_pairs={{0,4},{2,6},{4,0},{6,2},{8,12},{10,14},{12,8},{14,10},{1,5},{3,7},... | collective-permute-start | bytes 98312 | tf_op jit(solution)/shard_map/ppermute | solution.py:284
  47.3 1.3 %collective-permute-done.9.refs_1_ = bf16[2,8192]{1,0:T(2,128)(2,1)S(1)} collective-permute-done((bf16[2,8192]{1,0:T(2,128)(2,1)S(1)}, bf16[2,8192]{1,0:T(2,128)(2,1)S(1)}, u32[]{:S(2)}, u32[]{:S(2)}) %collective-permute-start.9) | collective-permute-done | bytes 32800 | tf_op jit(solution)/shard_map/ppermute | solution.py:284
  48.7 1.1 %collective-permute-done.10.refs_2_ = bf16[2,8192]{1,0:T(2,128)(2,1)S(1)} collective-permute-done((bf16[2,8192]{1,0:T(2,128)(2,1)S(1)}, bf16[2,8192]{1,0:T(2,128)(2,1)S(1)}, u32[]{:S(2)}, u32[]{:S(2)}) %collective-permute-start.10) | collective-permute-done | bytes 32800 | tf_op jit(solution)/shard_map/ppermute | solution.py:284
  (33 shorter events, 1.8 us)
Async XLA Ops:
  0.0 10.0 %copy-start.1 = (bf16[2,8192]{1,0:T(2,128)(2,1)S(1)}, bf16[2,8192]{1,0:T(2,128)(2,1)}, u32[]{:S(2)}) copy-start(bf16[2,8192]{1,0:T(2,128)(2,1)} %refs_4_.2) | copy-start | bytes 98308
  0.0 8.4 %collective-permute-start.1 = (bf16[2,8192]{1,0:T(2,128)(2,1)}, bf16[2,8192]{1,0:T(2,128)(2,1)S(1)}, u32[]{:S(2)}, u32[]{:S(2)}) collective-permute-start(bf16[2,8192]{1,0:T(2,128)(2,1)} %refs_4_.2), channel_id=1, source_target_pairs={{0,8},{2,10},{4,12},{6,14},{8,0},{10,2},{12,4},{14,6},{1,9},{3,11}... | collective-permute-start | bytes 98312 | tf_op jit(solution)/shard_map/ppermute | solution.py:284
  4.0 5.9 %collective-permute-start = (bf16[2,8192]{1,0:T(2,128)(2,1)}, bf16[2,8192]{1,0:T(2,128)(2,1)S(1)}, u32[]{:S(2)}, u32[]{:S(2)}) collective-permute-start(bf16[2,8192]{1,0:T(2,128)(2,1)} %refs_4_.2), channel_id=1, source_target_pairs={{0,12},{2,14},{4,8},{6,10},{8,4},{10,6},{12,0},{14,2},{1,13},{3,15... | collective-permute-start | bytes 98312 | tf_op jit(solution)/shard_map/ppermute | solution.py:284
  5.4 4.6 %collective-permute-start.2 = (bf16[2,8192]{1,0:T(2,128)(2,1)}, bf16[2,8192]{1,0:T(2,128)(2,1)S(1)}, u32[]{:S(2)}, u32[]{:S(2)}) collective-permute-start(bf16[2,8192]{1,0:T(2,128)(2,1)} %refs_4_.2), channel_id=1, source_target_pairs={{0,4},{2,6},{4,0},{6,2},{8,12},{10,14},{12,8},{14,10},{1,5},{3,7},... | collective-permute-start | bytes 98312 | tf_op jit(solution)/shard_map/ppermute | solution.py:284
  10.0 5.0 %copy-start = (bf16[8192,256]{1,0:T(8,128)(2,1)S(1)}, bf16[8192,256]{1,0:T(8,128)(2,1)}, u32[]{:S(2)}) copy-start(bf16[8192,256]{1,0:T(8,128)(2,1)} %refs_3_.1) | copy-start | bytes 12582916
  10.0 5.0 %collective-permute-start.3 = (bf16[4,2,8192]{2,1,0:T(2,128)(2,1)S(1)}, bf16[4,2,8192]{2,1,0:T(2,128)(2,1)S(1)}, u32[]{:S(2)}, u32[]{:S(2)}) collective-permute-start(bf16[4,2,8192]{2,1,0:T(2,128)(2,1)S(1)} %join.1.refs_0_.refs_1_), channel_id=1, source_target_pairs={{0,2},{2,0},{4,6},{6,4},{8,10},{10,8},{12,14},{14,12},{1,3},{3,1},... | collective-permute-start | bytes 393224 | tf_op jit(solution)/shard_map/ppermute | solution.py:284
  11.6 8.3 %slice-start = ((s8[33554432]{0:T(1024)(128)(4,1)}), s8[4194304]{0:T(1024)(128)(4,1)S(1)}, s32[]{:S(2)}) async-start(s8[33554432]{0:T(1024)(128)(4,1)} %bitcast), calls=%async_computation | async-start | bytes 8388608
  11.6 8.3 %slice-start.1 = ((s8[33554432]{0:T(1024)(128)(4,1)}), s8[4194304]{0:T(1024)(128)(4,1)S(1)}, s32[]{:S(2)}) async-start(s8[33554432]{0:T(1024)(128)(4,1)} %bitcast), calls=%async_computation.1 | async-start | bytes 8388608
  11.6 8.3 %slice-start.2 = ((s8[33554432]{0:T(1024)(128)(4,1)}), s8[4194304]{0:T(1024)(128)(4,1)S(1)}, s32[]{:S(2)}) async-start(s8[33554432]{0:T(1024)(128)(4,1)} %bitcast), calls=%async_computation.2 | async-start | bytes 8388608
  11.6 8.3 %slice-start.3 = ((s8[33554432]{0:T(1024)(128)(4,1)}), s8[4194304]{0:T(1024)(128)(4,1)S(1)}, s32[]{:S(2)}) async-start(s8[33554432]{0:T(1024)(128)(4,1)} %bitcast), calls=%async_computation.3 | async-start | bytes 8388608
  13.7 6.3 %slice-start.4 = ((s8[33554432]{0:T(1024)(128)(4,1)}), s8[4194304]{0:T(1024)(128)(4,1)S(1)}, s32[]{:S(2)}) async-start(s8[33554432]{0:T(1024)(128)(4,1)} %bitcast), calls=%async_computation.4 | async-start | bytes 8388608
  15.8 1.2 %collective-permute-start.4 = (f32[16,128]{1,0:T(8,128)S(1)}, f32[16,128]{1,0:T(8,128)S(1)}, u32[]{:S(2)}, u32[]{:S(2)}) collective-permute-start(f32[16,128]{1,0:T(8,128)S(1)} %get-tuple-element.27), channel_id=1, source_target_pairs={{0,1},{1,0},{2,3},{3,2},{4,5},{5,4},{6,7},{7,6},{8,9},{9,8},{10,11... | collective-permute-start | bytes 24584 | tf_op jit(solution)/shard_map/ppermute | solution.py:284
  17.0 4.3 %slice-start.5 = ((s8[33554432]{0:T(1024)(128)(4,1)}), s8[4194304]{0:T(1024)(128)(4,1)S(1)}, s32[]{:S(2)}) async-start(s8[33554432]{0:T(1024)(128)(4,1)} %bitcast), calls=%async_computation.5 | async-start | bytes 8388608
  17.0 5.5 %slice-start.6 = ((s8[33554432]{0:T(1024)(128)(4,1)}), s8[4194304]{0:T(1024)(128)(4,1)S(1)}, s32[]{:S(2)}) async-start(s8[33554432]{0:T(1024)(128)(4,1)} %bitcast), calls=%async_computation.6 | async-start | bytes 8388608
  17.0 6.6 %slice-start.7 = ((s8[33554432]{0:T(1024)(128)(4,1)}), s8[4194304]{0:T(1024)(128)(4,1)S(1)}, s32[]{:S(2)}) async-start(s8[33554432]{0:T(1024)(128)(4,1)} %bitcast), calls=%async_computation.7 | async-start | bytes 8388608
  17.0 2.9 %collective-permute-start.5 = (bf16[16,128]{1,0:T(8,128)(2,1)S(1)}, bf16[16,128]{1,0:T(8,128)(2,1)S(1)}, u32[]{:S(2)}, u32[]{:S(2)}) collective-permute-start(bf16[16,128]{1,0:T(8,128)(2,1)S(1)} %pair.1.refs_0_), channel_id=1, source_target_pairs={{0,0},{1,2},{2,4},{3,6},{4,8},{5,10},{6,12},{7,14},{8,1},{9,3},{10... | collective-permute-start | bytes 12296 | tf_op jit(solution)/shard_map/ppermute | solution.py:392
  28.5 1.7 %collective-permute-start.6 = (f32[16,2176]{1,0:T(8,128)S(1)}, f32[16,2176]{1,0:T(8,128)S(1)}, u32[]{:S(2)}, u32[]{:S(2)}) collective-permute-start(f32[16,2176]{1,0:T(8,128)S(1)} %get-tuple-element.29.refs_0_), channel_id=1, source_target_pairs={{0,1},{1,0},{2,3},{3,2},{4,5},{5,4},{6,7},{7,6},{8,9},{9,8},{10,11... | collective-permute-start | bytes 417800 | tf_op jit(solution)/shard_map/ppermute | solution.py:284
  35.6 7.2 %collective-permute-start.7 = (bf16[4,2,6144]{2,1,0:T(2,128)(2,1)S(1)}, bf16[4,2,6144]{2,1,0:T(2,128)(2,1)S(1)}, u32[]{:S(2)}, u32[]{:S(2)}) collective-permute-start(bf16[4,2,6144]{2,1,0:T(2,128)(2,1)S(1)} %get-tuple-element.36), channel_id=1, source_target_pairs={{0,2},{2,0},{4,6},{6,4},{8,10},{10,8},{12,14},{14,12},{1,3},{3,1},... | collective-permute-start | bytes 294920 | tf_op jit(solution)/shard_map/ppermute | solution.py:284
  38.8 4.0 %collective-permute-start.8 = (bf16[4,2,2048]{2,1,0:T(2,128)(2,1)S(1)}, bf16[4,2,2048]{2,1,0:T(2,128)(2,1)S(1)}, u32[]{:S(2)}, u32[]{:S(2)}) collective-permute-start(bf16[4,2,2048]{2,1,0:T(2,128)(2,1)S(1)} %get-tuple-element.40), channel_id=1, source_target_pairs={{0,2},{2,0},{4,6},{6,4},{8,10},{10,8},{12,14},{14,12},{1,3},{3,1},... | collective-permute-start | bytes 98312 | tf_op jit(solution)/shard_map/ppermute | solution.py:284
  42.9 5.8 %collective-permute-start.9 = (bf16[2,8192]{1,0:T(2,128)(2,1)S(1)}, bf16[2,8192]{1,0:T(2,128)(2,1)S(1)}, u32[]{:S(2)}, u32[]{:S(2)}) collective-permute-start(bf16[2,8192]{1,0:T(2,128)(2,1)S(1)} %get-tuple-element.42), channel_id=1, source_target_pairs={{0,12},{2,14},{4,8},{6,10},{8,4},{10,6},{12,0},{14,2},{1,13},{3,15... | collective-permute-start | bytes 98312 | tf_op jit(solution)/shard_map/ppermute | solution.py:284
  44.9 4.8 %collective-permute-start.10 = (bf16[2,8192]{1,0:T(2,128)(2,1)S(1)}, bf16[2,8192]{1,0:T(2,128)(2,1)S(1)}, u32[]{:S(2)}, u32[]{:S(2)}) collective-permute-start(bf16[2,8192]{1,0:T(2,128)(2,1)S(1)} %get-tuple-element.43), channel_id=1, source_target_pairs={{0,8},{2,10},{4,12},{6,14},{8,0},{10,2},{12,4},{14,6},{1,9},{3,11}... | collective-permute-start | bytes 98312 | tf_op jit(solution)/shard_map/ppermute | solution.py:284
  44.9 4.8 %collective-permute-start.11 = (bf16[2,8192]{1,0:T(2,128)(2,1)S(1)}, bf16[2,8192]{1,0:T(2,128)(2,1)S(1)}, u32[]{:S(2)}, u32[]{:S(2)}) collective-permute-start(bf16[2,8192]{1,0:T(2,128)(2,1)S(1)} %get-tuple-element.44), channel_id=1, source_target_pairs={{0,4},{2,6},{4,0},{6,2},{8,12},{10,14},{12,8},{14,10},{1,5},{3,7},... | collective-permute-start | bytes 98312 | tf_op jit(solution)/shard_map/ppermute | solution.py:284

commit v4 on v3

--- a/solution.py
+++ b/solution.py
@@ -15,10 +15,10 @@
 F32 = jnp.float32
 BF16 = jnp.bfloat16
 MIB = 1 << 20
-CUTS = (0, 6, 6, 9, 10, 22, 24, 24, 32)
+CUTS = (0, 4, 4, 4, 5, 18, 20, 20, 32)
 QSTEP = 4
 QOUT = pltpu.VMEM
-LIM = 3
+LIM = 6
 HINT = 0
 JH = (0, 0)
 KH = 0
@@ -184,17 +184,22 @@
         out[:, pl.ds(pl.multiple_of(at + j * step, step), step)] = part
 
 
-def query_kernel(x_ref, w_ref, head_ref, *refs, spans):
+def query_kernel(x_ref, w_ref, *refs, spans):
     n = len(spans)
     sources, q_out, targets, sems = refs[:n], refs[n], refs[n + 1 : -1], refs[-1]
     copies = fetches(sources, targets, spans, sems)
     for copy in copies:
         copy.start()
-    width = head_ref.shape[1]
-    q_out[:, :width] = head_ref[...].astype(F32)
-    multiply(x_ref, w_ref, q_out, width)
-    for copy in copies:
-        copy.wait()
+    multiply(x_ref, w_ref, q_out, 0)
+    for copy in copies:
+        copy.wait()
+
+
+def pack_kernel(*refs):
+    at = 0
+    for ref in refs[:-1]:
+        refs[-1][:, at : at + ref.shape[1]] = ref[...].astype(F32)
+        at += ref.shape[1]
 
 
 def attend(mine_ref, other_ref, turn_ref, allow_ref, att):
@@ -386,26 +391,26 @@
 
     half = wide // 2
     given = swap(give, "narrow", 2, 1)
-    (head,) = call(pair_kernel, "pair", [keep, given], [shaped(total, HEAD_DIM, dtype=BF16)], limit=1)
+    (w,) = ahead("ahead3", [w_out], [(o_cuts[3], o_cuts[4])], after=[keep])
+    o_near.append(w)
+    (head,) = call(pair_kernel, "pair", [keep, given], [shaped(total, HEAD_DIM, dtype=BF16)], limit=1, after=[w])
     routes = [(2 * s + n, 2 * ((2 * s + n) % wide) + s // half) for s in range(wide) for n in range(2)]
     sent = head
     head = lax.ppermute(head, ("wide", "narrow"), routes)
-    if o_cuts[4] > o_cuts[3]:
-        (w,) = ahead("ahead3", [w_out], [(o_cuts[3], o_cuts[4])], after=[sent])
-        o_near.append(w)
     unit = out_cols * QSTEP // 32
     spans = [(lo, min(lo + unit, o_cuts[5])) for lo in range(o_cuts[4], o_cuts[5], unit)]
     q, *pieces = call(
         functools.partial(query_kernel, spans=spans),
         "query",
-        [x, near(w_query), head] + [w_out] * len(spans),
-        [QOUT((total, q_cols + HEAD_DIM), F32)] + [fetched(w_out, *span) for span in spans],
+        [x, near(w_query)] + [w_out] * len(spans),
+        [shaped(total, q_cols)] + [fetched(w_out, *span) for span in spans],
         [pltpu.SemaphoreType.DMA((len(spans),))],
         limit=2,
         far=len(spans),
-        after=o_near[-1:],
+        after=[sent],
     )
     o_near += pieces
+    (q,) = call(pack_kernel, "pack", [head, q], [shaped(total, HEAD_DIM + q_cols)], limit=1)
     other = swap(q, "narrow", 2, 1)
     if o_cuts[6] > o_cuts[5]:
         (w,) = ahead("ahead4", [w_out], [(o_cuts[5], o_cuts[6])], after=[q])

time: 50.5 us -> 48.7 us (0.964)
  Pallas kernels: 21.8 us -> 19.1 us
  waiting for transfers between devices: 9.84 us -> 11.4 us
  local copies, waits for them, and re-layouts: 3.75 us -> 3.05 us
    pallas_call x12, Pallas kernels: 21.8 us -> 19.1 us  [call(): pl.pallas_call(kernel, out_shape=tuple(outs), in_specs=specs, out_specs=(...]
    ppermute x11, waiting for transfers between devices: 9.83 us -> 11.4 us  [swap(): return lax.ppermute(x, axis, [(i, i ^ bit) for i in range(size)])]
    unnamed x20, local copies, waits for them, and re-layouts: 3.75 us -> 3.05 us
  transfers between devices with their start and end apart: 12 -> 12, of which waited for: 6 -> 5; matrix products, arithmetic and copies ran while one was open for 0% -> 0% of each run, Pallas kernels for 20% -> 27%
where the time goes in v4:
time: 48.7 us; the launch traced here: 48.5 us
  Pallas kernels  19.1 us (39%)
  starting transfers between devices  14.8 us (30%)
  waiting for transfers between devices  11.4 us (23%)
  local copies, waits for them, and re-layouts  3.05 us (6%)
    pallas_call x12, Pallas kernels, call(): pl.pallas_call(kernel, out_shape=tuple(outs), in_specs=specs, out_specs=(...  19.1 us
    ppermute x11, starting transfers between devices, swap(): return lax.ppermute(x, axis, [(i, i ^ bit) for i in range(size)])  14 us
    ppermute x11, waiting for transfers between devices, swap(): return lax.ppermute(x, axis, [(i, i ^ bit) for i in range(size)])  11.4 us
    unnamed x20, local copies, waits for them, and re-layouts  3.05 us
  transfers between devices with their start and end apart: 12, of which 5 were waited for; matrix products, arithmetic and copies ran while one was open for 0% of the time, Pallas kernels for 27%

profile of v4, /device:TPU:0, one launch (start us, length us, event | category | flops | bytes accessed | tf_op | source)
XLA Modules:
  0.0 48.5 jit_solution(10941283656873695721)
XLA Ops:
  0.0 4.0 %collective-permute-start.1 = (bf16[2,8192]{1,0:T(2,128)(2,1)}, bf16[2,8192]{1,0:T(2,128)(2,1)S(1)}, u32[]{:S(2)}, u32[]{:S(2)}) collective-permute-start(bf16[2,8192]{1,0:T(2,128)(2,1)} %refs_4_.2), channel_id=1, source_target_pairs={{0,8},{2,10},{4,12},{6,14},{8,0},{10,2},{12,4},{14,6},{1,9},{3,11}... | collective-permute-start | bytes 98312 | tf_op jit(solution)/shard_map/ppermute | solution.py:289
  4.0 1.3 %collective-permute-start = (bf16[2,8192]{1,0:T(2,128)(2,1)}, bf16[2,8192]{1,0:T(2,128)(2,1)S(1)}, u32[]{:S(2)}, u32[]{:S(2)}) collective-permute-start(bf16[2,8192]{1,0:T(2,128)(2,1)} %refs_4_.2), channel_id=1, source_target_pairs={{0,12},{2,14},{4,8},{6,10},{8,4},{10,6},{12,0},{14,2},{1,13},{3,15... | collective-permute-start | bytes 98312 | tf_op jit(solution)/shard_map/ppermute | solution.py:289
  5.6 2.4 %tables.1 = (f32[4,16,128]{2,1,0:T(8,128)S(1)}, f32[256,16]{1,0:T(8,128)S(1)}, bf16[2048,1024]{1,0:T(8,128)(2,1)S(1)}) custom-call(s32[4]{0:T(128)} %refs_0_.1, bf16[2048,8192]{1,0:T(8,128)(2,1)} %refs_11_.1), custom_call_target="tpu_custom_call" | custom-call | bytes 1000 | tf_op jit(solution)/shard_map/tables/pallas_call | solution.py:52
  8.0 2.0 %collective-permute-done.refs_1_ = bf16[2,8192]{1,0:T(2,128)(2,1)S(1)} collective-permute-done((bf16[2,8192]{1,0:T(2,128)(2,1)}, bf16[2,8192]{1,0:T(2,128)(2,1)S(1)}, u32[]{:S(2)}, u32[]{:S(2)}) %collective-permute-start) | collective-permute-done | bytes 32800 | tf_op jit(solution)/shard_map/ppermute | solution.py:289
  10.0 1.6 %collective-permute-start.3 = (bf16[4,2,8192]{2,1,0:T(2,128)(2,1)S(1)}, bf16[4,2,8192]{2,1,0:T(2,128)(2,1)S(1)}, u32[]{:S(2)}, u32[]{:S(2)}) collective-permute-start(bf16[4,2,8192]{2,1,0:T(2,128)(2,1)S(1)} %join.1.refs_1_), channel_id=1, source_target_pairs={{0,2},{2,0},{4,6},{6,4},{8,10},{10,8},{12,14},{14,12},{1,3},{3,1},... | collective-permute-start | bytes 393224 | tf_op jit(solution)/shard_map/ppermute | solution.py:289
  11.6 3.4 %collective-permute-done.3.refs_2_ = bf16[4,2,8192]{2,1,0:T(2,128)(2,1)S(1)} collective-permute-done((bf16[4,2,8192]{2,1,0:T(2,128)(2,1)S(1)}, bf16[4,2,8192]{2,1,0:T(2,128)(2,1)S(1)}, u32[]{:S(2)}, u32[]{:S(2)}) %collective-permute-start.3) | collective-permute-done | bytes 131104 | tf_op jit(solution)/shard_map/ppermute | solution.py:289
  15.0 0.7 %keyval.1 = (bf16[16,8192]{1,0:T(8,128)(2,1)S(1)}, f32[16,128]{1,0:T(8,128)S(1)}, f32[16,128]{1,0:T(8,128)S(1)}) custom-call(bf16[2048,1024]{1,0:T(8,128)(2,1)S(1)} %get-tuple-element.26.refs_0_.refs_4_, bf16[4,2,8192]{2,1,0:T(2,128)(2,1)S(1)} %join.1.refs_1_, bf16[4,2,8192]{2,1,0:T(2,128)(2,1)S(1)} %collective-permute-done.3.refs_2_, ...), custom_call_target="tpu_custom_call" | custom-call | bytes 1000 | tf_op jit(solution)/shard_map/keyval/pallas_call | solution.py:52
  15.9 1.6 %ahead3.1.refs_0_.refs_5_ = bf16[2048,256]{1,0:T(8,128)(2,1)S(1)} custom-call(f32[16,128]{1,0:T(8,128)S(1)} %get-tuple-element.28.refs_0_.refs_1_, bf16[2048,8192]{1,0:T(8,128)(2,1)} %refs_11_.1), custom_call_target="tpu_custom_call" | custom-call | bytes 1000 | tf_op jit(solution)/shard_map/ahead3/pallas_call | solution.py:52
  17.5 0.8 %collective-permute-start.5 = (bf16[16,128]{1,0:T(8,128)(2,1)S(1)}, bf16[16,128]{1,0:T(8,128)(2,1)S(1)}, u32[]{:S(2)}, u32[]{:S(2)}) collective-permute-start(bf16[16,128]{1,0:T(8,128)(2,1)S(1)} %pair.1.refs_0_), channel_id=1, source_target_pairs={{0,0},{1,2},{2,4},{3,6},{4,8},{5,10},{6,12},{7,14},{8,1},{9,3},{10... | collective-permute-start | bytes 12296 | tf_op jit(solution)/shard_map/ppermute | solution.py:399
  18.4 0.6 %slice-done.5 = s8[4194304]{0:T(1024)(128)(4,1)S(1)} async-done(((s8[33554432]{0:T(1024)(128)(4,1)}), s8[4194304]{0:T(1024)(128)(4,1)S(1)}, s32[]{:S(2)}) %slice-start.5) | async-done | bytes 4194328
  19.0 1.2 %slice-done.6 = s8[4194304]{0:T(1024)(128)(4,1)S(1)} async-done(((s8[33554432]{0:T(1024)(128)(4,1)}), s8[4194304]{0:T(1024)(128)(4,1)S(1)}, s32[]{:S(2)}) %slice-start.6) | async-done | bytes 4194328
  20.2 1.2 %slice-done.7 = s8[4194304]{0:T(1024)(128)(4,1)S(1)} async-done(((s8[33554432]{0:T(1024)(128)(4,1)}), s8[4194304]{0:T(1024)(128)(4,1)S(1)}, s32[]{:S(2)}) %slice-start.7) | async-done | bytes 4194328
  21.4 5.0 %query.1 = (f32[16,2048]{1,0:T(8,128)S(1)}, bf16[2048,1024]{1,0:T(8,128)(2,1)S(1)}, bf16[2048,1024]{1,0:T(8,128)(2,1)S(1)}, bf16[2048,1024]{1,0:T(8,128)(2,1)S(1)}, bf16[2048,256]{1,0:T(8,128)(2,1)S(1)}) custom-call(bf16[16,128]{1,0:T(8,128)(2,1)S(1)} %pair.1.refs_0_, bf16[16,8192]{1,0:T(8,128)(2,1)S(1)} %get-tuple-element.30.refs_1_, ...), custom_call_target="tpu_custom_call" | custom-call | bytes 1000 | tf_op jit(solution)/shard_map/query/pallas_call | solution.py:52
  26.5 1.6 %ahead4.1.refs_10_ = bf16[2048,512]{1,0:T(8,128)(2,1)S(1)} custom-call(f32[16,2176]{1,0:T(8,128)S(1)} %pack.1.refs_0_, bf16[2048,8192]{1,0:T(8,128)(2,1)} %refs_11_.1), custom_call_target="tpu_custom_call" | custom-call | bytes 1000 | tf_op jit(solution)/shard_map/ahead4/pallas_call | solution.py:52
  28.1 4.6 %output0.1 = (bf16[16,2048]{1,0:T(8,128)(2,1)S(1)}, f32[4,2,5120]{2,1,0:T(2,128)S(1)}, bf16[4,2,5120]{2,1,0:T(2,128)(2,1)S(1)}, bf16[2048,3072]{1,0:T(8,128)(2,1)S(1)}) custom-call(f32[16,2176]{1,0:T(8,128)S(1)} %pack.1.refs_0_, f32[16,2176]{1,0:T(8,128)S(1)} %collective-permute-done.6.refs_1_, f32[4,16,128]{2,1,0:T(8,128)S(1)} %get-tuple-element.27.refs_0_.refs_2_, ...), custom_call_target="tpu_custom_call" | custom-call | bytes 1000 | tf_op jit(solution)/shard_map/output0/pallas_call | solution.py:52
  32.8 1.6 %collective-permute-start.7 = (bf16[4,2,5120]{2,1,0:T(2,128)(2,1)S(1)}, bf16[4,2,5120]{2,1,0:T(2,128)(2,1)S(1)}, u32[]{:S(2)}, u32[]{:S(2)}) collective-permute-start(bf16[4,2,5120]{2,1,0:T(2,128)(2,1)S(1)} %get-tuple-element.38), channel_id=1, source_target_pairs={{0,2},{2,0},{4,6},{6,4},{8,10},{10,8},{12,14},{14,12},{1,3},{3,1},... | collective-permute-start | bytes 245768 | tf_op jit(solution)/shard_map/ppermute | solution.py:289
  34.3 2.4 %output1.1 = (f32[4,2,3072]{2,1,0:T(2,128)S(1)}, bf16[4,2,3072]{2,1,0:T(2,128)(2,1)S(1)}) custom-call(bf16[16,2048]{1,0:T(8,128)(2,1)S(1)} %get-tuple-element.39.refs_0_, bf16[2048,3072]{1,0:T(8,128)(2,1)S(1)} %get-tuple-element.40.refs_1_), custom_call_target="tpu_custom_call" | custom-call | bytes 1000 | tf_op jit(solution)/shard_map/output1/pallas_call | solution.py:52
  36.7 0.6 %collective-permute-start.8 = (bf16[4,2,3072]{2,1,0:T(2,128)(2,1)S(1)}, bf16[4,2,3072]{2,1,0:T(2,128)(2,1)S(1)}, u32[]{:S(2)}, u32[]{:S(2)}) collective-permute-start(bf16[4,2,3072]{2,1,0:T(2,128)(2,1)S(1)} %get-tuple-element.42), channel_id=1, source_target_pairs={{0,2},{2,0},{4,6},{6,4},{8,10},{10,8},{12,14},{14,12},{1,3},{3,1},... | collective-permute-start | bytes 147464 | tf_op jit(solution)/shard_map/ppermute | solution.py:289
  37.3 3.6 %collective-permute-done.8.refs_3_ = bf16[4,2,3072]{2,1,0:T(2,128)(2,1)S(1)} collective-permute-done((bf16[4,2,3072]{2,1,0:T(2,128)(2,1)S(1)}, bf16[4,2,3072]{2,1,0:T(2,128)(2,1)S(1)}, u32[]{:S(2)}, u32[]{:S(2)}) %collective-permute-start.8) | collective-permute-done | bytes 49184 | tf_op jit(solution)/shard_map/ppermute | solution.py:289
  41.0 2.1 %collective-permute-start.9 = (bf16[2,8192]{1,0:T(2,128)(2,1)S(1)}, bf16[2,8192]{1,0:T(2,128)(2,1)S(1)}, u32[]{:S(2)}, u32[]{:S(2)}) collective-permute-start(bf16[2,8192]{1,0:T(2,128)(2,1)S(1)} %get-tuple-element.44), channel_id=1, source_target_pairs={{0,12},{2,14},{4,8},{6,10},{8,4},{10,6},{12,0},{14,2},{1,13},{3,15... | collective-permute-start | bytes 98312 | tf_op jit(solution)/shard_map/ppermute | solution.py:289
  43.6 1.8 %collective-permute-start.11 = (bf16[2,8192]{1,0:T(2,128)(2,1)S(1)}, bf16[2,8192]{1,0:T(2,128)(2,1)S(1)}, u32[]{:S(2)}, u32[]{:S(2)}) collective-permute-start(bf16[2,8192]{1,0:T(2,128)(2,1)S(1)} %get-tuple-element.46), channel_id=1, source_target_pairs={{0,4},{2,6},{4,0},{6,2},{8,12},{10,14},{12,8},{14,10},{1,5},{3,7},... | collective-permute-start | bytes 98312 | tf_op jit(solution)/shard_map/ppermute | solution.py:289
  45.4 1.6 %collective-permute-done.9.refs_1_ = bf16[2,8192]{1,0:T(2,128)(2,1)S(1)} collective-permute-done((bf16[2,8192]{1,0:T(2,128)(2,1)S(1)}, bf16[2,8192]{1,0:T(2,128)(2,1)S(1)}, u32[]{:S(2)}, u32[]{:S(2)}) %collective-permute-start.9) | collective-permute-done | bytes 32800 | tf_op jit(solution)/shard_map/ppermute | solution.py:289
  47.0 0.9 %collective-permute-done.10.refs_2_ = bf16[2,8192]{1,0:T(2,128)(2,1)S(1)} collective-permute-done((bf16[2,8192]{1,0:T(2,128)(2,1)S(1)}, bf16[2,8192]{1,0:T(2,128)(2,1)S(1)}, u32[]{:S(2)}, u32[]{:S(2)}) %collective-permute-start.10) | collective-permute-done | bytes 32800 | tf_op jit(solution)/shard_map/ppermute | solution.py:289
  47.9 0.7 %total.1 = bf16[2,8192]{1,0:T(2,128)(2,1)} custom-call(f32[2,8192]{1,0:T(2,128)S(1)} %get-tuple-element.43.refs_0_, bf16[2,8192]{1,0:T(2,128)(2,1)S(1)} %collective-permute-done.9.refs_1_, bf16[2,8192]{1,0:T(2,128)(2,1)S(1)} %collective-permute-done.10.refs_2_, bf16[2,8192]{1,0:T(2,128)(2,1)S(1)} %collective-permute-done.11.refs_3_), custom_call_target="tpu_custom_call" | custom-call | bytes 1000 | tf_op jit(solution)/shard_map/total/pallas_call | solution.py:52
  (33 shorter events, 1.1 us)
Async XLA Ops:
  0.0 10.0 %copy-start.1 = (bf16[2,8192]{1,0:T(2,128)(2,1)S(1)}, bf16[2,8192]{1,0:T(2,128)(2,1)}, u32[]{:S(2)}) copy-start(bf16[2,8192]{1,0:T(2,128)(2,1)} %refs_4_.2) | copy-start | bytes 98308
  0.0 15.0 %copy-start = (bf16[8192,256]{1,0:T(8,128)(2,1)S(1)}, bf16[8192,256]{1,0:T(8,128)(2,1)}, u32[]{:S(2)}) copy-start(bf16[8192,256]{1,0:T(8,128)(2,1)} %refs_3_.2) | copy-start | bytes 12582916
  0.0 8.0 %collective-permute-start.1 = (bf16[2,8192]{1,0:T(2,128)(2,1)}, bf16[2,8192]{1,0:T(2,128)(2,1)S(1)}, u32[]{:S(2)}, u32[]{:S(2)}) collective-permute-start(bf16[2,8192]{1,0:T(2,128)(2,1)} %refs_4_.2), channel_id=1, source_target_pairs={{0,8},{2,10},{4,12},{6,14},{8,0},{10,2},{12,4},{14,6},{1,9},{3,11}... | collective-permute-start | bytes 98312 | tf_op jit(solution)/shard_map/ppermute | solution.py:289
  4.0 5.9 %collective-permute-start = (bf16[2,8192]{1,0:T(2,128)(2,1)}, bf16[2,8192]{1,0:T(2,128)(2,1)S(1)}, u32[]{:S(2)}, u32[]{:S(2)}) collective-permute-start(bf16[2,8192]{1,0:T(2,128)(2,1)} %refs_4_.2), channel_id=1, source_target_pairs={{0,12},{2,14},{4,8},{6,10},{8,4},{10,6},{12,0},{14,2},{1,13},{3,15... | collective-permute-start | bytes 98312 | tf_op jit(solution)/shard_map/ppermute | solution.py:289
  5.4 4.6 %collective-permute-start.2 = (bf16[2,8192]{1,0:T(2,128)(2,1)}, bf16[2,8192]{1,0:T(2,128)(2,1)S(1)}, u32[]{:S(2)}, u32[]{:S(2)}) collective-permute-start(bf16[2,8192]{1,0:T(2,128)(2,1)} %refs_4_.2), channel_id=1, source_target_pairs={{0,4},{2,6},{4,0},{6,2},{8,12},{10,14},{12,8},{14,10},{1,5},{3,7},... | collective-permute-start | bytes 98312 | tf_op jit(solution)/shard_map/ppermute | solution.py:289
  5.6 12.7 %slice-start = ((s8[33554432]{0:T(1024)(128)(4,1)}), s8[4194304]{0:T(1024)(128)(4,1)S(1)}, s32[]{:S(2)}) async-start(s8[33554432]{0:T(1024)(128)(4,1)} %bitcast), calls=%async_computation | async-start | bytes 8388608
  5.6 12.7 %slice-start.1 = ((s8[33554432]{0:T(1024)(128)(4,1)}), s8[4194304]{0:T(1024)(128)(4,1)S(1)}, s32[]{:S(2)}) async-start(s8[33554432]{0:T(1024)(128)(4,1)} %bitcast), calls=%async_computation.1 | async-start | bytes 8388608
  5.6 12.7 %slice-start.2 = ((s8[33554432]{0:T(1024)(128)(4,1)}), s8[4194304]{0:T(1024)(128)(4,1)S(1)}, s32[]{:S(2)}) async-start(s8[33554432]{0:T(1024)(128)(4,1)} %bitcast), calls=%async_computation.2 | async-start | bytes 8388608
  5.6 12.8 %slice-start.3 = ((s8[33554432]{0:T(1024)(128)(4,1)}), s8[4194304]{0:T(1024)(128)(4,1)S(1)}, s32[]{:S(2)}) async-start(s8[33554432]{0:T(1024)(128)(4,1)} %bitcast), calls=%async_computation.3 | async-start | bytes 8388608
  10.0 5.0 %collective-permute-start.3 = (bf16[4,2,8192]{2,1,0:T(2,128)(2,1)S(1)}, bf16[4,2,8192]{2,1,0:T(2,128)(2,1)S(1)}, u32[]{:S(2)}, u32[]{:S(2)}) collective-permute-start(bf16[4,2,8192]{2,1,0:T(2,128)(2,1)S(1)} %join.1.refs_1_), channel_id=1, source_target_pairs={{0,2},{2,0},{4,6},{6,4},{8,10},{10,8},{12,14},{14,12},{1,3},{3,1},... | collective-permute-start | bytes 393224 | tf_op jit(solution)/shard_map/ppermute | solution.py:289
  15.0 3.4 %slice-start.4 = ((s8[33554432]{0:T(1024)(128)(4,1)}), s8[4194304]{0:T(1024)(128)(4,1)S(1)}, s32[]{:S(2)}) async-start(s8[33554432]{0:T(1024)(128)(4,1)} %bitcast), calls=%async_computation.4 | async-start | bytes 8388608
  15.8 1.8 %collective-permute-start.4 = (f32[16,128]{1,0:T(8,128)S(1)}, f32[16,128]{1,0:T(8,128)S(1)}, u32[]{:S(2)}, u32[]{:S(2)}) collective-permute-start(f32[16,128]{1,0:T(8,128)S(1)} %get-tuple-element.29), channel_id=1, source_target_pairs={{0,1},{1,0},{2,3},{3,2},{4,5},{5,4},{6,7},{7,6},{8,9},{9,8},{10,11... | collective-permute-start | bytes 24584 | tf_op jit(solution)/shard_map/ppermute | solution.py:289
  15.8 3.2 %slice-start.5 = ((s8[33554432]{0:T(1024)(128)(4,1)}), s8[4194304]{0:T(1024)(128)(4,1)S(1)}, s32[]{:S(2)}) async-start(s8[33554432]{0:T(1024)(128)(4,1)} %bitcast), calls=%async_computation.5 | async-start | bytes 8388608
  15.8 4.4 %slice-start.6 = ((s8[33554432]{0:T(1024)(128)(4,1)}), s8[4194304]{0:T(1024)(128)(4,1)S(1)}, s32[]{:S(2)}) async-start(s8[33554432]{0:T(1024)(128)(4,1)} %bitcast), calls=%async_computation.6 | async-start | bytes 8388608
  15.9 5.6 %slice-start.7 = ((s8[33554432]{0:T(1024)(128)(4,1)}), s8[4194304]{0:T(1024)(128)(4,1)S(1)}, s32[]{:S(2)}) async-start(s8[33554432]{0:T(1024)(128)(4,1)} %bitcast), calls=%async_computation.7 | async-start | bytes 8388608
  17.5 8.8 %collective-permute-start.5 = (bf16[16,128]{1,0:T(8,128)(2,1)S(1)}, bf16[16,128]{1,0:T(8,128)(2,1)S(1)}, u32[]{:S(2)}, u32[]{:S(2)}) collective-permute-start(bf16[16,128]{1,0:T(8,128)(2,1)S(1)} %pair.1.refs_0_), channel_id=1, source_target_pairs={{0,0},{1,2},{2,4},{3,6},{4,8},{5,10},{6,12},{7,14},{8,1},{9,3},{10... | collective-permute-start | bytes 12296 | tf_op jit(solution)/shard_map/ppermute | solution.py:399
  26.4 1.7 %collective-permute-start.6 = (f32[16,2176]{1,0:T(8,128)S(1)}, f32[16,2176]{1,0:T(8,128)S(1)}, u32[]{:S(2)}, u32[]{:S(2)}) collective-permute-start(f32[16,2176]{1,0:T(8,128)S(1)} %pack.1.refs_0_), channel_id=1, source_target_pairs={{0,1},{1,0},{2,3},{3,2},{4,5},{5,4},{6,7},{7,6},{8,9},{9,8},{10,11... | collective-permute-start | bytes 417800 | tf_op jit(solution)/shard_map/ppermute | solution.py:289
  32.8 8.1 %collective-permute-start.7 = (bf16[4,2,5120]{2,1,0:T(2,128)(2,1)S(1)}, bf16[4,2,5120]{2,1,0:T(2,128)(2,1)S(1)}, u32[]{:S(2)}, u32[]{:S(2)}) collective-permute-start(bf16[4,2,5120]{2,1,0:T(2,128)(2,1)S(1)} %get-tuple-element.38), channel_id=1, source_target_pairs={{0,2},{2,0},{4,6},{6,4},{8,10},{10,8},{12,14},{14,12},{1,3},{3,1},... | collective-permute-start | bytes 245768 | tf_op jit(solution)/shard_map/ppermute | solution.py:289
  36.7 4.2 %collective-permute-start.8 = (bf16[4,2,3072]{2,1,0:T(2,128)(2,1)S(1)}, bf16[4,2,3072]{2,1,0:T(2,128)(2,1)S(1)}, u32[]{:S(2)}, u32[]{:S(2)}) collective-permute-start(bf16[4,2,3072]{2,1,0:T(2,128)(2,1)S(1)} %get-tuple-element.42), channel_id=1, source_target_pairs={{0,2},{2,0},{4,6},{6,4},{8,10},{10,8},{12,14},{14,12},{1,3},{3,1},... | collective-permute-start | bytes 147464 | tf_op jit(solution)/shard_map/ppermute | solution.py:289
  41.0 6.0 %collective-permute-start.9 = (bf16[2,8192]{1,0:T(2,128)(2,1)S(1)}, bf16[2,8192]{1,0:T(2,128)(2,1)S(1)}, u32[]{:S(2)}, u32[]{:S(2)}) collective-permute-start(bf16[2,8192]{1,0:T(2,128)(2,1)S(1)} %get-tuple-element.44), channel_id=1, source_target_pairs={{0,12},{2,14},{4,8},{6,10},{8,4},{10,6},{12,0},{14,2},{1,13},{3,15... | collective-permute-start | bytes 98312 | tf_op jit(solution)/shard_map/ppermute | solution.py:289
  43.0 4.8 %collective-permute-start.10 = (bf16[2,8192]{1,0:T(2,128)(2,1)S(1)}, bf16[2,8192]{1,0:T(2,128)(2,1)S(1)}, u32[]{:S(2)}, u32[]{:S(2)}) collective-permute-start(bf16[2,8192]{1,0:T(2,128)(2,1)S(1)} %get-tuple-element.45), channel_id=1, source_target_pairs={{0,8},{2,10},{4,12},{6,14},{8,0},{10,2},{12,4},{14,6},{1,9},{3,11}... | collective-permute-start | bytes 98312 | tf_op jit(solution)/shard_map/ppermute | solution.py:289
  43.6 4.3 %collective-permute-start.11 = (bf16[2,8192]{1,0:T(2,128)(2,1)S(1)}, bf16[2,8192]{1,0:T(2,128)(2,1)S(1)}, u32[]{:S(2)}, u32[]{:S(2)}) collective-permute-start(bf16[2,8192]{1,0:T(2,128)(2,1)S(1)} %get-tuple-element.46), channel_id=1, source_target_pairs={{0,4},{2,6},{4,0},{6,2},{8,12},{10,14},{12,8},{14,10},{1,5},{3,7},... | collective-permute-start | bytes 98312 | tf_op jit(solution)/shard_map/ppermute | solution.py:289

commit v5 on v4

--- a/solution.py
+++ b/solution.py
@@ -15,13 +15,9 @@
 F32 = jnp.float32
 BF16 = jnp.bfloat16
 MIB = 1 << 20
-CUTS = (0, 4, 4, 4, 5, 18, 20, 20, 32)
-QSTEP = 4
-QOUT = pltpu.VMEM
-LIM = 6
-HINT = 0
-JH = (0, 0)
-KH = 0
+CUTS = (0, 4, 16, 18, 24, 32)
+STEP = 4
+FILL = 9 * 10**9
 
 
 def vspec():
@@ -147,17 +143,18 @@
         refs[-1][i] = ref[...]
 
 
-def keyval_kernel(a_ref, b_ref, w_ref, *refs, order, spans):
+def keyval_kernel(*refs, order, spans):
     n = len(spans)
+    parts, w_ref, refs = refs[: len(order)], refs[len(order)], refs[len(order) + 1 :]
     sources, (x_out, keep_ref, give_ref), targets = refs[:n], refs[n : n + 3], refs[n + 3 : 2 * n + 3]
     x32, sems = refs[2 * n + 3 :]
     copies = fetches(sources, targets, spans, sems)
     for copy in copies:
         copy.start()
-    count, rows = a_ref.shape[:2]
-    for i in range(count):
-        for base, ref in ((order[i], a_ref), (order[count + i], b_ref)):
-            x32[rows * base : rows * (base + 1), :] = ref[i].astype(F32)
+    rows = parts[0].shape[1]
+    for ref, owners in zip(parts, order):
+        for i, s in enumerate(owners):
+            x32[rows * s : rows * (s + 1), :] = ref[i].astype(F32)
     x_out[...] = x32[...].astype(BF16)
     part = jnp.dot(x_out[...], w_ref[...], preferred_element_type=F32)
     width = keep_ref.shape[1]
@@ -175,7 +172,7 @@
 
 def multiply(x_ref, w_ref, out, at, lo=0, hi=None):
     width = (w_ref.shape[1] if hi is None else hi) - lo
-    step = math.gcd(math.gcd(width, 512), lo)
+    step = math.gcd(math.gcd(width, min(1024, (1 << 23) // w_ref.shape[0])), lo)
 
     @pl.loop(0, width // step)
     def _(j):
@@ -357,7 +354,7 @@
     o_cuts = [out_cols * k // 32 for k in CUTS]
     o_near, spans = [], [(o_cuts[0], o_cuts[1])]
     along = list(reversed(range(2, wide, 2)))
-    others = [swap(tokens, "wide", wide, bit) for bit in along]
+    other = swap(tokens, "wide", wide, 1)
     turn, allow, w = call(
         functools.partial(tables_kernel, rows=rows, spans=spans),
         "tables",
@@ -366,39 +363,31 @@
         [pltpu.SemaphoreType.DMA((1,)), pltpu.SMEM(lengths.shape, jnp.int32), pltpu.SemaphoreType.DMA],
         limit=2,
         far=2,
-        hint=HINT,
     )
     o_near.append(w)
-    order = [*along, 0]
-    (x,) = call(
-        join_kernel, "join", [*others, tokens], [shaped(len(order), rows, depth, dtype=BF16)], limit=2, after=[turn], hint=JH[0]
-    )
-    order = order + [s ^ 1 for s in order]
-    other = swap(x, "wide", wide, 1)
-    if o_cuts[3] > o_cuts[1]:
-        (w,) = ahead("ahead1", [w_out], [(o_cuts[1], o_cuts[3])], after=[x])
-        o_near.append(w)
+    (pair,) = call(join_kernel, "join", [tokens, other], [shaped(2, rows, depth, dtype=BF16)], limit=2, after=[turn])
+    others = [swap(pair, "wide", wide, bit) for bit in along]
+    others, along = others[::-1], along[::-1]
+    order = [[bit, bit ^ 1] for bit in [*along, 0]]
     x, keep, give = call(
         functools.partial(keyval_kernel, order=order, spans=[]),
         "keyval",
-        [x, other, near(w_keyval)],
+        [*others, pair, near(w_keyval)],
         [shaped(total, depth, dtype=BF16)] + [shaped(total, HEAD_DIM)] * 2,
         [pltpu.VMEM((total, depth), F32), pltpu.SemaphoreType.DMA((1,))],
         limit=4,
-        hint=KH,
         after=[o_near[-1]],
     )
 
     half = wide // 2
     given = swap(give, "narrow", 2, 1)
-    (w,) = ahead("ahead3", [w_out], [(o_cuts[3], o_cuts[4])], after=[keep])
-    o_near.append(w)
-    (head,) = call(pair_kernel, "pair", [keep, given], [shaped(total, HEAD_DIM, dtype=BF16)], limit=1, after=[w])
+    (mark,) = call(join_kernel, "mark", [keep], [shaped(1, total, HEAD_DIM)], limit=1, hint=FILL)
+    (head,) = call(pair_kernel, "pair", [keep, given], [shaped(total, HEAD_DIM, dtype=BF16)], limit=1, after=[mark])
     routes = [(2 * s + n, 2 * ((2 * s + n) % wide) + s // half) for s in range(wide) for n in range(2)]
     sent = head
     head = lax.ppermute(head, ("wide", "narrow"), routes)
-    unit = out_cols * QSTEP // 32
-    spans = [(lo, min(lo + unit, o_cuts[5])) for lo in range(o_cuts[4], o_cuts[5], unit)]
+    unit = out_cols * STEP // 32
+    spans = [(lo, min(lo + unit, o_cuts[2])) for lo in range(o_cuts[1], o_cuts[2], unit)]
     q, *pieces = call(
         functools.partial(query_kernel, spans=spans),
         "query",
@@ -412,9 +401,8 @@
     o_near += pieces
     (q,) = call(pack_kernel, "pack", [head, q], [shaped(total, HEAD_DIM + q_cols)], limit=1)
     other = swap(q, "narrow", 2, 1)
-    if o_cuts[6] > o_cuts[5]:
-        (w,) = ahead("ahead4", [w_out], [(o_cuts[5], o_cuts[6])], after=[q])
-        o_near.append(w)
+    (w,) = ahead("ahead", [w_out], [(o_cuts[2], o_cuts[3])], after=[q])
+    o_near.append(w)
 
     def output(name, head, weights, own, spans):
         own_cols = [hi - lo for lo, hi in own]
@@ -428,7 +416,7 @@
             + [fetched(w_out, *span) for span in spans],
             [pltpu.VMEM((total, width), F32), pltpu.SemaphoreType.DMA((max(1, len(own) + len(spans)),))]
             + [pltpu.VMEM((w_out.shape[0], cols), BF16) for cols in own_cols],
-            limit=LIM,
+            limit=8,
             far=1 if own or spans else 0,
         )
 
@@ -436,8 +424,8 @@
         "output0",
         [q, other, turn, allow],
         o_near,
-        [span for span in [(o_cuts[6], o_cuts[7])] if span[1] > span[0]],
-        [(o_cuts[7], o_cuts[8])],
+        [(o_cuts[3], o_cuts[4])],
+        [(o_cuts[4], o_cuts[5])],
     )
     got0 = swap(send0, "wide", wide, 1)
     keep1, send1 = output("output1", [att], [o2], [], [])

time: 48.7 us -> 48 us (0.986)
  Pallas kernels: 19.1 us -> 17.4 us
  waiting for transfers between devices: 11.4 us -> 11.9 us
    pallas_call x12, Pallas kernels: 19.1 us -> 17.4 us  [call(): pl.pallas_call(kernel, out_shape=tuple(outs), in_specs=specs, out_specs=(...]
  transfers between devices with their start and end apart: 12 -> 12, of which waited for: 5 -> 6; matrix products, arithmetic and copies ran while one was open for 0% -> 0% of each run, Pallas kernels for 27% -> 21%
where the time goes in v5:
time: 48 us; the launch traced here: 47.8 us
  Pallas kernels  17.4 us (36%)
  starting transfers between devices  15 us (31%)
  waiting for transfers between devices  11.9 us (25%)
  local copies, waits for them, and re-layouts  3.28 us (7%)
    pallas_call x12, Pallas kernels, call(): pl.pallas_call(kernel, out_shape=tuple(outs), in_specs=specs, out_specs=(...  17.4 us
    ppermute x11, starting transfers between devices, swap(): return lax.ppermute(x, axis, [(i, i ^ bit) for i in range(size)])  14.2 us
    ppermute x11, waiting for transfers between devices, swap(): return lax.ppermute(x, axis, [(i, i ^ bit) for i in range(size)])  11.9 us
    unnamed x20, local copies, waits for them, and re-layouts  3.28 us
  transfers between devices with their start and end apart: 12, of which 6 were waited for; matrix products, arithmetic and copies ran while one was open for 0% of the time, Pallas kernels for 21%

profile of v5, /device:TPU:0, one launch (start us, length us, event | category | flops | bytes accessed | tf_op | source)
XLA Modules:
  0.0 47.8 jit_solution(17907503894935377408)
XLA Ops:
  0.0 3.0 %collective-permute-start = (bf16[2,8192]{1,0:T(2,128)(2,1)}, bf16[2,8192]{1,0:T(2,128)(2,1)S(1)}, u32[]{:S(2)}, u32[]{:S(2)}) collective-permute-start(bf16[2,8192]{1,0:T(2,128)(2,1)} %refs_1_.4), channel_id=1, source_target_pairs={{0,2},{2,0},{4,6},{6,4},{8,10},{10,8},{12,14},{14,12},{1,3},{3,1},... | collective-permute-start | bytes 98312 | tf_op jit(solution)/shard_map/ppermute | solution.py:286
  3.0 2.4 %tables.1 = (f32[4,16,128]{2,1,0:T(8,128)S(1)}, f32[256,16]{1,0:T(8,128)S(1)}, bf16[2048,1024]{1,0:T(8,128)(2,1)S(1)}) custom-call(s32[4]{0:T(128)} %refs_0_.1, bf16[2048,8192]{1,0:T(8,128)(2,1)} %refs_9_.1), custom_call_target="tpu_custom_call" | custom-call | bytes 1000 | tf_op jit(solution)/shard_map/tables/pallas_call | solution.py:48
  5.4 3.9 %collective-permute-start.3 = (bf16[2,2,8192]{2,1,0:T(2,128)(2,1)S(1)}, bf16[2,2,8192]{2,1,0:T(2,128)(2,1)S(1)}, u32[]{:S(2)}, u32[]{:S(2)}) collective-permute-start(bf16[2,2,8192]{2,1,0:T(2,128)(2,1)S(1)} %join.1.refs_4_), channel_id=1, source_target_pairs={{0,12},{2,14},{4,8},{6,10},{8,4},{10,6},{12,0},{14,2},{1,13},{3,15... | collective-permute-start | bytes 196616 | tf_op jit(solution)/shard_map/ppermute | solution.py:286
  9.9 2.4 %collective-permute-done.3.refs_3_ = bf16[2,2,8192]{2,1,0:T(2,128)(2,1)S(1)} collective-permute-done((bf16[2,2,8192]{2,1,0:T(2,128)(2,1)S(1)}, bf16[2,2,8192]{2,1,0:T(2,128)(2,1)S(1)}, u32[]{:S(2)}, u32[]{:S(2)}) %collective-permute-start.3) | collective-permute-done | bytes 65568 | tf_op jit(solution)/shard_map/ppermute | solution.py:286
  12.3 2.2 %collective-permute-done.2.refs_2_ = bf16[2,2,8192]{2,1,0:T(2,128)(2,1)S(1)} collective-permute-done((bf16[2,2,8192]{2,1,0:T(2,128)(2,1)S(1)}, bf16[2,2,8192]{2,1,0:T(2,128)(2,1)S(1)}, u32[]{:S(2)}, u32[]{:S(2)}) %collective-permute-start.2) | collective-permute-done | bytes 65568 | tf_op jit(solution)/shard_map/ppermute | solution.py:286
  14.6 0.7 %keyval.1 = (bf16[16,8192]{1,0:T(8,128)(2,1)S(1)}, f32[16,128]{1,0:T(8,128)S(1)}, f32[16,128]{1,0:T(8,128)S(1)}) custom-call(bf16[2048,1024]{1,0:T(8,128)(2,1)S(1)} %get-tuple-element.25.refs_0_.refs_4_, bf16[2,2,8192]{2,1,0:T(2,128)(2,1)S(1)} %collective-permute-done.1.refs_1_, bf16[2,2,8192]{2,1,0:T(2,128)(2,1)S(1)} %collective-permute-done.2.refs_2_, ...), custom_call_target="tpu_custom_call" | custom-call | bytes 1000 | tf_op jit(solution)/shard_map/keyval/pallas_call | solution.py:48
  15.4 1.1 %collective-permute-done.4.refs_2_ = f32[16,128]{1,0:T(8,128)S(1)} collective-permute-done((f32[16,128]{1,0:T(8,128)S(1)}, f32[16,128]{1,0:T(8,128)S(1)}, u32[]{:S(2)}, u32[]{:S(2)}) %collective-permute-start.4) | collective-permute-done | bytes 8224 | tf_op jit(solution)/shard_map/ppermute | solution.py:286
  16.5 0.8 %collective-permute-start.5 = (bf16[16,128]{1,0:T(8,128)(2,1)S(1)}, bf16[16,128]{1,0:T(8,128)(2,1)S(1)}, u32[]{:S(2)}, u32[]{:S(2)}) collective-permute-start(bf16[16,128]{1,0:T(8,128)(2,1)S(1)} %pair.1.refs_0_), channel_id=1, source_target_pairs={{0,0},{1,2},{2,4},{3,6},{4,8},{5,10},{6,12},{7,14},{8,1},{9,3},{10... | collective-permute-start | bytes 12296 | tf_op jit(solution)/shard_map/ppermute | solution.py:388
  17.4 0.8 %slice-done.5 = s8[4194304]{0:T(1024)(128)(4,1)S(1)} async-done(((s8[33554432]{0:T(1024)(128)(4,1)}), s8[4194304]{0:T(1024)(128)(4,1)S(1)}, s32[]{:S(2)}) %slice-start.5) | async-done | bytes 4194328
  18.2 1.2 %slice-done.6 = s8[4194304]{0:T(1024)(128)(4,1)S(1)} async-done(((s8[33554432]{0:T(1024)(128)(4,1)}), s8[4194304]{0:T(1024)(128)(4,1)S(1)}, s32[]{:S(2)}) %slice-start.6) | async-done | bytes 4194328
  19.4 1.2 %slice-done.7 = s8[4194304]{0:T(1024)(128)(4,1)S(1)} async-done(((s8[33554432]{0:T(1024)(128)(4,1)}), s8[4194304]{0:T(1024)(128)(4,1)S(1)}, s32[]{:S(2)}) %slice-start.7) | async-done | bytes 4194328
  20.6 4.7 %query.1 = (f32[16,2048]{1,0:T(8,128)S(1)}, bf16[2048,1024]{1,0:T(8,128)(2,1)S(1)}, bf16[2048,1024]{1,0:T(8,128)(2,1)S(1)}, bf16[2048,1024]{1,0:T(8,128)(2,1)S(1)}) custom-call(bf16[16,128]{1,0:T(8,128)(2,1)S(1)} %pair.1.refs_0_, bf16[16,8192]{1,0:T(8,128)(2,1)S(1)} %get-tuple-element.29.refs_1_, bf16[8192,2048]{1,0:T(8,128)(2,1)S(1)} %bitcast.1, ...), custom_call_target="tpu_custom_call" | custom-call | bytes 1000 | tf_op jit(solution)/shard_map/query/pallas_call | solution.py:48
  25.5 1.6 %ahead.1.refs_8_ = bf16[2048,512]{1,0:T(8,128)(2,1)S(1)} custom-call(f32[16,2176]{1,0:T(8,128)S(1)} %pack.1.refs_0_, bf16[2048,8192]{1,0:T(8,128)(2,1)} %refs_9_.1), custom_call_target="tpu_custom_call" | custom-call | bytes 1000 | tf_op jit(solution)/shard_map/ahead/pallas_call | solution.py:48
  27.1 5.9 %output0.1 = (bf16[16,2048]{1,0:T(8,128)(2,1)S(1)}, f32[4,2,6144]{2,1,0:T(2,128)S(1)}, bf16[4,2,6144]{2,1,0:T(2,128)(2,1)S(1)}, bf16[2048,2048]{1,0:T(8,128)(2,1)S(1)}) custom-call(f32[16,2176]{1,0:T(8,128)S(1)} %pack.1.refs_0_, f32[16,2176]{1,0:T(8,128)S(1)} %collective-permute-done.6.refs_1_, f32[4,16,128]{2,1,0:T(8,128)S(1)} %get-tuple-element.26.refs_0_.refs_2_, ...), custom_call_target="tpu_custom_call" | custom-call | bytes 1000 | tf_op jit(solution)/shard_map/output0/pallas_call | solution.py:48
  32.9 1.5 %collective-permute-start.7 = (bf16[4,2,6144]{2,1,0:T(2,128)(2,1)S(1)}, bf16[4,2,6144]{2,1,0:T(2,128)(2,1)S(1)}, u32[]{:S(2)}, u32[]{:S(2)}) collective-permute-start(bf16[4,2,6144]{2,1,0:T(2,128)(2,1)S(1)} %get-tuple-element.36), channel_id=1, source_target_pairs={{0,2},{2,0},{4,6},{6,4},{8,10},{10,8},{12,14},{14,12},{1,3},{3,1},... | collective-permute-start | bytes 294920 | tf_op jit(solution)/shard_map/ppermute | solution.py:286
  34.4 1.4 %output1.1 = (f32[4,2,2048]{2,1,0:T(2,128)S(1)}, bf16[4,2,2048]{2,1,0:T(2,128)(2,1)S(1)}) custom-call(bf16[16,2048]{1,0:T(8,128)(2,1)S(1)} %get-tuple-element.37.refs_0_, bf16[2048,2048]{1,0:T(8,128)(2,1)S(1)} %get-tuple-element.38.refs_1_), custom_call_target="tpu_custom_call" | custom-call | bytes 1000 | tf_op jit(solution)/shard_map/output1/pallas_call | solution.py:48
  35.8 0.7 %collective-permute-start.8 = (bf16[4,2,2048]{2,1,0:T(2,128)(2,1)S(1)}, bf16[4,2,2048]{2,1,0:T(2,128)(2,1)S(1)}, u32[]{:S(2)}, u32[]{:S(2)}) collective-permute-start(bf16[4,2,2048]{2,1,0:T(2,128)(2,1)S(1)} %get-tuple-element.40), channel_id=1, source_target_pairs={{0,2},{2,0},{4,6},{6,4},{8,10},{10,8},{12,14},{14,12},{1,3},{3,1},... | collective-permute-start | bytes 98312 | tf_op jit(solution)/shard_map/ppermute | solution.py:286
  36.5 3.3 %collective-permute-done.8.refs_3_ = bf16[4,2,2048]{2,1,0:T(2,128)(2,1)S(1)} collective-permute-done((bf16[4,2,2048]{2,1,0:T(2,128)(2,1)S(1)}, bf16[4,2,2048]{2,1,0:T(2,128)(2,1)S(1)}, u32[]{:S(2)}, u32[]{:S(2)}) %collective-permute-start.8) | collective-permute-done | bytes 32800 | tf_op jit(solution)/shard_map/ppermute | solution.py:286
  39.9 2.2 %collective-permute-start.9 = (bf16[2,8192]{1,0:T(2,128)(2,1)S(1)}, bf16[2,8192]{1,0:T(2,128)(2,1)S(1)}, u32[]{:S(2)}, u32[]{:S(2)}) collective-permute-start(bf16[2,8192]{1,0:T(2,128)(2,1)S(1)} %get-tuple-element.42), channel_id=1, source_target_pairs={{0,12},{2,14},{4,8},{6,10},{8,4},{10,6},{12,0},{14,2},{1,13},{3,15... | collective-permute-start | bytes 98312 | tf_op jit(solution)/shard_map/ppermute | solution.py:286
  42.0 0.7 %collective-permute-start.10 = (bf16[2,8192]{1,0:T(2,128)(2,1)S(1)}, bf16[2,8192]{1,0:T(2,128)(2,1)S(1)}, u32[]{:S(2)}, u32[]{:S(2)}) collective-permute-start(bf16[2,8192]{1,0:T(2,128)(2,1)S(1)} %get-tuple-element.43), channel_id=1, source_target_pairs={{0,8},{2,10},{4,12},{6,14},{8,0},{10,2},{12,4},{14,6},{1,9},{3,11}... | collective-permute-start | bytes 98312 | tf_op jit(solution)/shard_map/ppermute | solution.py:286
  42.7 1.6 %collective-permute-start.11 = (bf16[2,8192]{1,0:T(2,128)(2,1)S(1)}, bf16[2,8192]{1,0:T(2,128)(2,1)S(1)}, u32[]{:S(2)}, u32[]{:S(2)}) collective-permute-start(bf16[2,8192]{1,0:T(2,128)(2,1)S(1)} %get-tuple-element.44), channel_id=1, source_target_pairs={{0,4},{2,6},{4,0},{6,2},{8,12},{10,14},{12,8},{14,10},{1,5},{3,7},... | collective-permute-start | bytes 98312 | tf_op jit(solution)/shard_map/ppermute | solution.py:286
  44.3 1.5 %collective-permute-done.9.refs_1_ = bf16[2,8192]{1,0:T(2,128)(2,1)S(1)} collective-permute-done((bf16[2,8192]{1,0:T(2,128)(2,1)S(1)}, bf16[2,8192]{1,0:T(2,128)(2,1)S(1)}, u32[]{:S(2)}, u32[]{:S(2)}) %collective-permute-start.9) | collective-permute-done | bytes 32800 | tf_op jit(solution)/shard_map/ppermute | solution.py:286
  45.8 1.3 %collective-permute-done.10.refs_2_ = bf16[2,8192]{1,0:T(2,128)(2,1)S(1)} collective-permute-done((bf16[2,8192]{1,0:T(2,128)(2,1)S(1)}, bf16[2,8192]{1,0:T(2,128)(2,1)S(1)}, u32[]{:S(2)}, u32[]{:S(2)}) %collective-permute-start.10) | collective-permute-done | bytes 32800 | tf_op jit(solution)/shard_map/ppermute | solution.py:286
  47.1 0.7 %total.1 = bf16[2,8192]{1,0:T(2,128)(2,1)} custom-call(f32[2,8192]{1,0:T(2,128)S(1)} %get-tuple-element.41.refs_0_, bf16[2,8192]{1,0:T(2,128)(2,1)S(1)} %collective-permute-done.9.refs_1_, bf16[2,8192]{1,0:T(2,128)(2,1)S(1)} %collective-permute-done.10.refs_2_, bf16[2,8192]{1,0:T(2,128)(2,1)S(1)} %collective-permute-done.11.refs_3_), custom_call_target="tpu_custom_call" | custom-call | bytes 1000 | tf_op jit(solution)/shard_map/total/pallas_call | solution.py:48
  (33 shorter events, 1.0 us)
Async XLA Ops:
  0.0 5.4 %copy-start.1 = (bf16[2,8192]{1,0:T(2,128)(2,1)S(1)}, bf16[2,8192]{1,0:T(2,128)(2,1)}, u32[]{:S(2)}) copy-start(bf16[2,8192]{1,0:T(2,128)(2,1)} %refs_1_.4) | copy-start | bytes 98308
  0.0 14.6 %copy-start = (bf16[8192,256]{1,0:T(8,128)(2,1)S(1)}, bf16[8192,256]{1,0:T(8,128)(2,1)}, u32[]{:S(2)}) copy-start(bf16[8192,256]{1,0:T(8,128)(2,1)} %refs_5_.2) | copy-start | bytes 12582916
  0.0 5.3 %collective-permute-start = (bf16[2,8192]{1,0:T(2,128)(2,1)}, bf16[2,8192]{1,0:T(2,128)(2,1)S(1)}, u32[]{:S(2)}, u32[]{:S(2)}) collective-permute-start(bf16[2,8192]{1,0:T(2,128)(2,1)} %refs_1_.4), channel_id=1, source_target_pairs={{0,2},{2,0},{4,6},{6,4},{8,10},{10,8},{12,14},{14,12},{1,3},{3,1},... | collective-permute-start | bytes 98312 | tf_op jit(solution)/shard_map/ppermute | solution.py:286
  3.0 14.4 %slice-start = ((s8[33554432]{0:T(1024)(128)(4,1)}), s8[4194304]{0:T(1024)(128)(4,1)S(1)}, s32[]{:S(2)}) async-start(s8[33554432]{0:T(1024)(128)(4,1)} %bitcast), calls=%async_computation | async-start | bytes 8388608
  3.0 14.4 %slice-start.1 = ((s8[33554432]{0:T(1024)(128)(4,1)}), s8[4194304]{0:T(1024)(128)(4,1)S(1)}, s32[]{:S(2)}) async-start(s8[33554432]{0:T(1024)(128)(4,1)} %bitcast), calls=%async_computation.1 | async-start | bytes 8388608
  3.0 14.4 %slice-start.2 = ((s8[33554432]{0:T(1024)(128)(4,1)}), s8[4194304]{0:T(1024)(128)(4,1)S(1)}, s32[]{:S(2)}) async-start(s8[33554432]{0:T(1024)(128)(4,1)} %bitcast), calls=%async_computation.2 | async-start | bytes 8388608
  3.0 14.4 %slice-start.3 = ((s8[33554432]{0:T(1024)(128)(4,1)}), s8[4194304]{0:T(1024)(128)(4,1)S(1)}, s32[]{:S(2)}) async-start(s8[33554432]{0:T(1024)(128)(4,1)} %bitcast), calls=%async_computation.3 | async-start | bytes 8388608
  5.4 6.9 %collective-permute-start.3 = (bf16[2,2,8192]{2,1,0:T(2,128)(2,1)S(1)}, bf16[2,2,8192]{2,1,0:T(2,128)(2,1)S(1)}, u32[]{:S(2)}, u32[]{:S(2)}) collective-permute-start(bf16[2,2,8192]{2,1,0:T(2,128)(2,1)S(1)} %join.1.refs_4_), channel_id=1, source_target_pairs={{0,12},{2,14},{4,8},{6,10},{8,4},{10,6},{12,0},{14,2},{1,13},{3,15... | collective-permute-start | bytes 196616 | tf_op jit(solution)/shard_map/ppermute | solution.py:286
  9.3 5.3 %collective-permute-start.2 = (bf16[2,2,8192]{2,1,0:T(2,128)(2,1)S(1)}, bf16[2,2,8192]{2,1,0:T(2,128)(2,1)S(1)}, u32[]{:S(2)}, u32[]{:S(2)}) collective-permute-start(bf16[2,2,8192]{2,1,0:T(2,128)(2,1)S(1)} %join.1.refs_4_), channel_id=1, source_target_pairs={{0,8},{2,10},{4,12},{6,14},{8,0},{10,2},{12,4},{14,6},{1,9},{3,11}... | collective-permute-start | bytes 196616 | tf_op jit(solution)/shard_map/ppermute | solution.py:286
  9.3 5.3 %collective-permute-start.1 = (bf16[2,2,8192]{2,1,0:T(2,128)(2,1)S(1)}, bf16[2,2,8192]{2,1,0:T(2,128)(2,1)S(1)}, u32[]{:S(2)}, u32[]{:S(2)}) collective-permute-start(bf16[2,2,8192]{2,1,0:T(2,128)(2,1)S(1)} %join.1.refs_4_), channel_id=1, source_target_pairs={{0,4},{2,6},{4,0},{6,2},{8,12},{10,14},{12,8},{14,10},{1,5},{3,7},... | collective-permute-start | bytes 196616 | tf_op jit(solution)/shard_map/ppermute | solution.py:286
  14.6 2.8 %slice-start.4 = ((s8[33554432]{0:T(1024)(128)(4,1)}), s8[4194304]{0:T(1024)(128)(4,1)S(1)}, s32[]{:S(2)}) async-start(s8[33554432]{0:T(1024)(128)(4,1)} %bitcast), calls=%async_computation.4 | async-start | bytes 8388608
  15.3 1.2 %collective-permute-start.4 = (f32[16,128]{1,0:T(8,128)S(1)}, f32[16,128]{1,0:T(8,128)S(1)}, u32[]{:S(2)}, u32[]{:S(2)}) collective-permute-start(f32[16,128]{1,0:T(8,128)S(1)} %get-tuple-element.28), channel_id=1, source_target_pairs={{0,1},{1,0},{2,3},{3,2},{4,5},{5,4},{6,7},{7,6},{8,9},{9,8},{10,11... | collective-permute-start | bytes 24584 | tf_op jit(solution)/shard_map/ppermute | solution.py:286
  15.4 2.9 %slice-start.5 = ((s8[33554432]{0:T(1024)(128)(4,1)}), s8[4194304]{0:T(1024)(128)(4,1)S(1)}, s32[]{:S(2)}) async-start(s8[33554432]{0:T(1024)(128)(4,1)} %bitcast), calls=%async_computation.5 | async-start | bytes 8388608
  15.4 4.0 %slice-start.6 = ((s8[33554432]{0:T(1024)(128)(4,1)}), s8[4194304]{0:T(1024)(128)(4,1)S(1)}, s32[]{:S(2)}) async-start(s8[33554432]{0:T(1024)(128)(4,1)} %bitcast), calls=%async_computation.6 | async-start | bytes 8388608
  15.4 5.2 %slice-start.7 = ((s8[33554432]{0:T(1024)(128)(4,1)}), s8[4194304]{0:T(1024)(128)(4,1)S(1)}, s32[]{:S(2)}) async-start(s8[33554432]{0:T(1024)(128)(4,1)} %bitcast), calls=%async_computation.7 | async-start | bytes 8388608
  16.5 8.8 %collective-permute-start.5 = (bf16[16,128]{1,0:T(8,128)(2,1)S(1)}, bf16[16,128]{1,0:T(8,128)(2,1)S(1)}, u32[]{:S(2)}, u32[]{:S(2)}) collective-permute-start(bf16[16,128]{1,0:T(8,128)(2,1)S(1)} %pair.1.refs_0_), channel_id=1, source_target_pairs={{0,0},{1,2},{2,4},{3,6},{4,8},{5,10},{6,12},{7,14},{8,1},{9,3},{10... | collective-permute-start | bytes 12296 | tf_op jit(solution)/shard_map/ppermute | solution.py:388
  25.4 1.7 %collective-permute-start.6 = (f32[16,2176]{1,0:T(8,128)S(1)}, f32[16,2176]{1,0:T(8,128)S(1)}, u32[]{:S(2)}, u32[]{:S(2)}) collective-permute-start(f32[16,2176]{1,0:T(8,128)S(1)} %pack.1.refs_0_), channel_id=1, source_target_pairs={{0,1},{1,0},{2,3},{3,2},{4,5},{5,4},{6,7},{7,6},{8,9},{9,8},{10,11... | collective-permute-start | bytes 417800 | tf_op jit(solution)/shard_map/ppermute | solution.py:286
  32.9 6.8 %collective-permute-start.7 = (bf16[4,2,6144]{2,1,0:T(2,128)(2,1)S(1)}, bf16[4,2,6144]{2,1,0:T(2,128)(2,1)S(1)}, u32[]{:S(2)}, u32[]{:S(2)}) collective-permute-start(bf16[4,2,6144]{2,1,0:T(2,128)(2,1)S(1)} %get-tuple-element.36), channel_id=1, source_target_pairs={{0,2},{2,0},{4,6},{6,4},{8,10},{10,8},{12,14},{14,12},{1,3},{3,1},... | collective-permute-start | bytes 294920 | tf_op jit(solution)/shard_map/ppermute | solution.py:286
  35.8 4.0 %collective-permute-start.8 = (bf16[4,2,2048]{2,1,0:T(2,128)(2,1)S(1)}, bf16[4,2,2048]{2,1,0:T(2,128)(2,1)S(1)}, u32[]{:S(2)}, u32[]{:S(2)}) collective-permute-start(bf16[4,2,2048]{2,1,0:T(2,128)(2,1)S(1)} %get-tuple-element.40), channel_id=1, source_target_pairs={{0,2},{2,0},{4,6},{6,4},{8,10},{10,8},{12,14},{14,12},{1,3},{3,1},... | collective-permute-start | bytes 98312 | tf_op jit(solution)/shard_map/ppermute | solution.py:286
  39.9 5.9 %collective-permute-start.9 = (bf16[2,8192]{1,0:T(2,128)(2,1)S(1)}, bf16[2,8192]{1,0:T(2,128)(2,1)S(1)}, u32[]{:S(2)}, u32[]{:S(2)}) collective-permute-start(bf16[2,8192]{1,0:T(2,128)(2,1)S(1)} %get-tuple-element.42), channel_id=1, source_target_pairs={{0,12},{2,14},{4,8},{6,10},{8,4},{10,6},{12,0},{14,2},{1,13},{3,15... | collective-permute-start | bytes 98312 | tf_op jit(solution)/shard_map/ppermute | solution.py:286
  42.0 5.1 %collective-permute-start.10 = (bf16[2,8192]{1,0:T(2,128)(2,1)S(1)}, bf16[2,8192]{1,0:T(2,128)(2,1)S(1)}, u32[]{:S(2)}, u32[]{:S(2)}) collective-permute-start(bf16[2,8192]{1,0:T(2,128)(2,1)S(1)} %get-tuple-element.43), channel_id=1, source_target_pairs={{0,8},{2,10},{4,12},{6,14},{8,0},{10,2},{12,4},{14,6},{1,9},{3,11}... | collective-permute-start | bytes 98312 | tf_op jit(solution)/shard_map/ppermute | solution.py:286
  42.7 4.4 %collective-permute-start.11 = (bf16[2,8192]{1,0:T(2,128)(2,1)S(1)}, bf16[2,8192]{1,0:T(2,128)(2,1)S(1)}, u32[]{:S(2)}, u32[]{:S(2)}) collective-permute-start(bf16[2,8192]{1,0:T(2,128)(2,1)S(1)} %get-tuple-element.44), channel_id=1, source_target_pairs={{0,4},{2,6},{4,0},{6,2},{8,12},{10,14},{12,8},{14,10},{1,5},{3,7},... | collective-permute-start | bytes 98312 | tf_op jit(solution)/shard_map/ppermute | solution.py:286

commit v6 on v5

--- a/solution.py
+++ b/solution.py
@@ -15,7 +15,7 @@
 F32 = jnp.float32
 BF16 = jnp.bfloat16
 MIB = 1 << 20
-CUTS = (0, 4, 16, 18, 24, 32)
+CUTS = (0, 4, 16, 18, 24, 30, 32)
 STEP = 4
 FILL = 9 * 10**9
 
@@ -428,7 +428,7 @@
         [(o_cuts[4], o_cuts[5])],
     )
     got0 = swap(send0, "wide", wide, 1)
-    keep1, send1 = output("output1", [att], [o2], [], [])
+    keep1, send1 = output("output1", [att], [o2], [(o_cuts[5], o_cuts[6])], [])
     got1 = swap(send1, "wide", wide, 1)
     mine, *others = call(
         functools.partial(near_sum_kernel, parts=2),

time: 48 us -> 47.6 us (level)
  transfers between devices with their start and end apart: 12 -> 12, of which waited for: 6 -> 6; matrix products, arithmetic and copies ran while one was open for 0% -> 0% of each run, Pallas kernels for 21% -> 23%
where the time goes in v6:
time: 47.6 us; the launch traced here: 47.4 us
  Pallas kernels  17.1 us (36%)
  starting transfers between devices  15 us (32%)
  waiting for transfers between devices  11.9 us (25%)
  local copies, waits for them, and re-layouts  3.28 us (7%)
    pallas_call x12, Pallas kernels, call(): pl.pallas_call(kernel, out_shape=tuple(outs), in_specs=specs, out_specs=(...  17.1 us
    ppermute x11, starting transfers between devices, swap(): return lax.ppermute(x, axis, [(i, i ^ bit) for i in range(size)])  14.2 us
    ppermute x11, waiting for transfers between devices, swap(): return lax.ppermute(x, axis, [(i, i ^ bit) for i in range(size)])  11.9 us
    unnamed x20, local copies, waits for them, and re-layouts  3.28 us
  transfers between devices with their start and end apart: 12, of which 6 were waited for; matrix products, arithmetic and copies ran while one was open for 0% of the time, Pallas kernels for 23%

profile of v6, /device:TPU:0, one launch (start us, length us, event | category | flops | bytes accessed | tf_op | source)
XLA Modules:
  0.0 47.4 jit_solution(16220342536997426491)
XLA Ops:
  0.0 3.0 %collective-permute-start = (bf16[2,8192]{1,0:T(2,128)(2,1)}, bf16[2,8192]{1,0:T(2,128)(2,1)S(1)}, u32[]{:S(2)}, u32[]{:S(2)}) collective-permute-start(bf16[2,8192]{1,0:T(2,128)(2,1)} %refs_1_.4), channel_id=1, source_target_pairs={{0,2},{2,0},{4,6},{6,4},{8,10},{10,8},{12,14},{14,12},{1,3},{3,1},... | collective-permute-start | bytes 98312 | tf_op jit(solution)/shard_map/ppermute | solution.py:286
  3.0 2.4 %tables.1 = (f32[4,16,128]{2,1,0:T(8,128)S(1)}, f32[256,16]{1,0:T(8,128)S(1)}, bf16[2048,1024]{1,0:T(8,128)(2,1)S(1)}) custom-call(s32[4]{0:T(128)} %refs_0_.1, bf16[2048,8192]{1,0:T(8,128)(2,1)} %refs_2_.3), custom_call_target="tpu_custom_call" | custom-call | bytes 1000 | tf_op jit(solution)/shard_map/tables/pallas_call | solution.py:48
  5.4 3.9 %collective-permute-start.3 = (bf16[2,2,8192]{2,1,0:T(2,128)(2,1)S(1)}, bf16[2,2,8192]{2,1,0:T(2,128)(2,1)S(1)}, u32[]{:S(2)}, u32[]{:S(2)}) collective-permute-start(bf16[2,2,8192]{2,1,0:T(2,128)(2,1)S(1)} %join.1.refs_4_), channel_id=1, source_target_pairs={{0,12},{2,14},{4,8},{6,10},{8,4},{10,6},{12,0},{14,2},{1,13},{3,15... | collective-permute-start | bytes 196616 | tf_op jit(solution)/shard_map/ppermute | solution.py:286
  9.9 2.4 %collective-permute-done.3.refs_3_ = bf16[2,2,8192]{2,1,0:T(2,128)(2,1)S(1)} collective-permute-done((bf16[2,2,8192]{2,1,0:T(2,128)(2,1)S(1)}, bf16[2,2,8192]{2,1,0:T(2,128)(2,1)S(1)}, u32[]{:S(2)}, u32[]{:S(2)}) %collective-permute-start.3) | collective-permute-done | bytes 65568 | tf_op jit(solution)/shard_map/ppermute | solution.py:286
  12.3 2.2 %collective-permute-done.2.refs_2_ = bf16[2,2,8192]{2,1,0:T(2,128)(2,1)S(1)} collective-permute-done((bf16[2,2,8192]{2,1,0:T(2,128)(2,1)S(1)}, bf16[2,2,8192]{2,1,0:T(2,128)(2,1)S(1)}, u32[]{:S(2)}, u32[]{:S(2)}) %collective-permute-start.2) | collective-permute-done | bytes 65568 | tf_op jit(solution)/shard_map/ppermute | solution.py:286
  14.6 0.7 %keyval.1 = (bf16[16,8192]{1,0:T(8,128)(2,1)S(1)}, f32[16,128]{1,0:T(8,128)S(1)}, f32[16,128]{1,0:T(8,128)S(1)}) custom-call(bf16[2048,1024]{1,0:T(8,128)(2,1)S(1)} %get-tuple-element.25.refs_0_.refs_4_, bf16[2,2,8192]{2,1,0:T(2,128)(2,1)S(1)} %collective-permute-done.1.refs_1_, bf16[2,2,8192]{2,1,0:T(2,128)(2,1)S(1)} %collective-permute-done.2.refs_2_, ...), custom_call_target="tpu_custom_call" | custom-call | bytes 1000 | tf_op jit(solution)/shard_map/keyval/pallas_call | solution.py:48
  15.4 1.1 %collective-permute-done.4.refs_2_ = f32[16,128]{1,0:T(8,128)S(1)} collective-permute-done((f32[16,128]{1,0:T(8,128)S(1)}, f32[16,128]{1,0:T(8,128)S(1)}, u32[]{:S(2)}, u32[]{:S(2)}) %collective-permute-start.4) | collective-permute-done | bytes 8224 | tf_op jit(solution)/shard_map/ppermute | solution.py:286
  16.5 0.8 %collective-permute-start.5 = (bf16[16,128]{1,0:T(8,128)(2,1)S(1)}, bf16[16,128]{1,0:T(8,128)(2,1)S(1)}, u32[]{:S(2)}, u32[]{:S(2)}) collective-permute-start(bf16[16,128]{1,0:T(8,128)(2,1)S(1)} %pair.1.refs_0_), channel_id=1, source_target_pairs={{0,0},{1,2},{2,4},{3,6},{4,8},{5,10},{6,12},{7,14},{8,1},{9,3},{10... | collective-permute-start | bytes 12296 | tf_op jit(solution)/shard_map/ppermute | solution.py:388
  17.4 0.9 %slice-done.5 = s8[4194304]{0:T(1024)(128)(4,1)S(1)} async-done(((s8[33554432]{0:T(1024)(128)(4,1)}), s8[4194304]{0:T(1024)(128)(4,1)S(1)}, s32[]{:S(2)}) %slice-start.5) | async-done | bytes 4194328
  18.2 1.2 %slice-done.6 = s8[4194304]{0:T(1024)(128)(4,1)S(1)} async-done(((s8[33554432]{0:T(1024)(128)(4,1)}), s8[4194304]{0:T(1024)(128)(4,1)S(1)}, s32[]{:S(2)}) %slice-start.6) | async-done | bytes 4194328
  19.4 1.2 %slice-done.7 = s8[4194304]{0:T(1024)(128)(4,1)S(1)} async-done(((s8[33554432]{0:T(1024)(128)(4,1)}), s8[4194304]{0:T(1024)(128)(4,1)S(1)}, s32[]{:S(2)}) %slice-start.7) | async-done | bytes 4194328
  20.6 4.7 %query.1 = (f32[16,2048]{1,0:T(8,128)S(1)}, bf16[2048,1024]{1,0:T(8,128)(2,1)S(1)}, bf16[2048,1024]{1,0:T(8,128)(2,1)S(1)}, bf16[2048,1024]{1,0:T(8,128)(2,1)S(1)}) custom-call(bf16[16,128]{1,0:T(8,128)(2,1)S(1)} %pair.1.refs_0_, bf16[16,8192]{1,0:T(8,128)(2,1)S(1)} %get-tuple-element.29.refs_1_, bf16[8192,2048]{1,0:T(8,128)(2,1)S(1)} %bitcast.1, ...), custom_call_target="tpu_custom_call" | custom-call | bytes 1000 | tf_op jit(solution)/shard_map/query/pallas_call | solution.py:48
  25.5 1.6 %ahead.1.refs_8_ = bf16[2048,512]{1,0:T(8,128)(2,1)S(1)} custom-call(f32[16,2176]{1,0:T(8,128)S(1)} %pack.1.refs_0_, bf16[2048,8192]{1,0:T(8,128)(2,1)} %refs_2_.3), custom_call_target="tpu_custom_call" | custom-call | bytes 1000 | tf_op jit(solution)/shard_map/ahead/pallas_call | solution.py:48
  27.1 4.9 %output0.1 = (bf16[16,2048]{1,0:T(8,128)(2,1)S(1)}, f32[4,2,6144]{2,1,0:T(2,128)S(1)}, bf16[4,2,6144]{2,1,0:T(2,128)(2,1)S(1)}, bf16[2048,1536]{1,0:T(8,128)(2,1)S(1)}) custom-call(f32[16,2176]{1,0:T(8,128)S(1)} %pack.1.refs_0_, f32[16,2176]{1,0:T(8,128)S(1)} %collective-permute-done.6.refs_1_, f32[4,16,128]{2,1,0:T(8,128)S(1)} %get-tuple-element.26.refs_0_.refs_2_, ...), custom_call_target="tpu_custom_call" | custom-call | bytes 1000 | tf_op jit(solution)/shard_map/output0/pallas_call | solution.py:48
  32.0 1.5 %collective-permute-start.7 = (bf16[4,2,6144]{2,1,0:T(2,128)(2,1)S(1)}, bf16[4,2,6144]{2,1,0:T(2,128)(2,1)S(1)}, u32[]{:S(2)}, u32[]{:S(2)}) collective-permute-start(bf16[4,2,6144]{2,1,0:T(2,128)(2,1)S(1)} %get-tuple-element.36), channel_id=1, source_target_pairs={{0,2},{2,0},{4,6},{6,4},{8,10},{10,8},{12,14},{14,12},{1,3},{3,1},... | collective-permute-start | bytes 294920 | tf_op jit(solution)/shard_map/ppermute | solution.py:286
  33.5 2.0 %output1.1 = (f32[4,2,2048]{2,1,0:T(2,128)S(1)}, bf16[4,2,2048]{2,1,0:T(2,128)(2,1)S(1)}) custom-call(bf16[16,2048]{1,0:T(8,128)(2,1)S(1)} %get-tuple-element.37.refs_0_, bf16[2048,1536]{1,0:T(8,128)(2,1)S(1)} %get-tuple-element.38.refs_1_, bf16[2048,8192]{1,0:T(8,128)(2,1)} %refs_2_.3), custom_call_target="tpu_custom_call" | custom-call | bytes 1000 | tf_op jit(solution)/shard_map/output1/pallas_call | solution.py:48
  35.5 0.7 %collective-permute-start.8 = (bf16[4,2,2048]{2,1,0:T(2,128)(2,1)S(1)}, bf16[4,2,2048]{2,1,0:T(2,128)(2,1)S(1)}, u32[]{:S(2)}, u32[]{:S(2)}) collective-permute-start(bf16[4,2,2048]{2,1,0:T(2,128)(2,1)S(1)} %get-tuple-element.40), channel_id=1, source_target_pairs={{0,2},{2,0},{4,6},{6,4},{8,10},{10,8},{12,14},{14,12},{1,3},{3,1},... | collective-permute-start | bytes 98312 | tf_op jit(solution)/shard_map/ppermute | solution.py:286
  36.1 3.3 %collective-permute-done.8.refs_3_ = bf16[4,2,2048]{2,1,0:T(2,128)(2,1)S(1)} collective-permute-done((bf16[4,2,2048]{2,1,0:T(2,128)(2,1)S(1)}, bf16[4,2,2048]{2,1,0:T(2,128)(2,1)S(1)}, u32[]{:S(2)}, u32[]{:S(2)}) %collective-permute-start.8) | collective-permute-done | bytes 32800 | tf_op jit(solution)/shard_map/ppermute | solution.py:286
  39.5 2.2 %collective-permute-start.9 = (bf16[2,8192]{1,0:T(2,128)(2,1)S(1)}, bf16[2,8192]{1,0:T(2,128)(2,1)S(1)}, u32[]{:S(2)}, u32[]{:S(2)}) collective-permute-start(bf16[2,8192]{1,0:T(2,128)(2,1)S(1)} %get-tuple-element.42), channel_id=1, source_target_pairs={{0,12},{2,14},{4,8},{6,10},{8,4},{10,6},{12,0},{14,2},{1,13},{3,15... | collective-permute-start | bytes 98312 | tf_op jit(solution)/shard_map/ppermute | solution.py:286
  41.7 0.7 %collective-permute-start.10 = (bf16[2,8192]{1,0:T(2,128)(2,1)S(1)}, bf16[2,8192]{1,0:T(2,128)(2,1)S(1)}, u32[]{:S(2)}, u32[]{:S(2)}) collective-permute-start(bf16[2,8192]{1,0:T(2,128)(2,1)S(1)} %get-tuple-element.43), channel_id=1, source_target_pairs={{0,8},{2,10},{4,12},{6,14},{8,0},{10,2},{12,4},{14,6},{1,9},{3,11}... | collective-permute-start | bytes 98312 | tf_op jit(solution)/shard_map/ppermute | solution.py:286
  42.4 1.6 %collective-permute-start.11 = (bf16[2,8192]{1,0:T(2,128)(2,1)S(1)}, bf16[2,8192]{1,0:T(2,128)(2,1)S(1)}, u32[]{:S(2)}, u32[]{:S(2)}) collective-permute-start(bf16[2,8192]{1,0:T(2,128)(2,1)S(1)} %get-tuple-element.44), channel_id=1, source_target_pairs={{0,4},{2,6},{4,0},{6,2},{8,12},{10,14},{12,8},{14,10},{1,5},{3,7},... | collective-permute-start | bytes 98312 | tf_op jit(solution)/shard_map/ppermute | solution.py:286
  44.0 1.5 %collective-permute-done.9.refs_1_ = bf16[2,8192]{1,0:T(2,128)(2,1)S(1)} collective-permute-done((bf16[2,8192]{1,0:T(2,128)(2,1)S(1)}, bf16[2,8192]{1,0:T(2,128)(2,1)S(1)}, u32[]{:S(2)}, u32[]{:S(2)}) %collective-permute-start.9) | collective-permute-done | bytes 32800 | tf_op jit(solution)/shard_map/ppermute | solution.py:286
  45.5 1.3 %collective-permute-done.10.refs_2_ = bf16[2,8192]{1,0:T(2,128)(2,1)S(1)} collective-permute-done((bf16[2,8192]{1,0:T(2,128)(2,1)S(1)}, bf16[2,8192]{1,0:T(2,128)(2,1)S(1)}, u32[]{:S(2)}, u32[]{:S(2)}) %collective-permute-start.10) | collective-permute-done | bytes 32800 | tf_op jit(solution)/shard_map/ppermute | solution.py:286
  46.8 0.7 %total.1 = bf16[2,8192]{1,0:T(2,128)(2,1)} custom-call(f32[2,8192]{1,0:T(2,128)S(1)} %get-tuple-element.41.refs_0_, bf16[2,8192]{1,0:T(2,128)(2,1)S(1)} %collective-permute-done.9.refs_1_, bf16[2,8192]{1,0:T(2,128)(2,1)S(1)} %collective-permute-done.10.refs_2_, bf16[2,8192]{1,0:T(2,128)(2,1)S(1)} %collective-permute-done.11.refs_3_), custom_call_target="tpu_custom_call" | custom-call | bytes 1000 | tf_op jit(solution)/shard_map/total/pallas_call | solution.py:48
  (33 shorter events, 1.0 us)
Async XLA Ops:
  0.0 5.4 %copy-start.1 = (bf16[2,8192]{1,0:T(2,128)(2,1)S(1)}, bf16[2,8192]{1,0:T(2,128)(2,1)}, u32[]{:S(2)}) copy-start(bf16[2,8192]{1,0:T(2,128)(2,1)} %refs_1_.4) | copy-start | bytes 98308
  0.0 14.6 %copy-start = (bf16[8192,256]{1,0:T(8,128)(2,1)S(1)}, bf16[8192,256]{1,0:T(8,128)(2,1)}, u32[]{:S(2)}) copy-start(bf16[8192,256]{1,0:T(8,128)(2,1)} %refs_5_.2) | copy-start | bytes 12582916
  0.0 5.3 %collective-permute-start = (bf16[2,8192]{1,0:T(2,128)(2,1)}, bf16[2,8192]{1,0:T(2,128)(2,1)S(1)}, u32[]{:S(2)}, u32[]{:S(2)}) collective-permute-start(bf16[2,8192]{1,0:T(2,128)(2,1)} %refs_1_.4), channel_id=1, source_target_pairs={{0,2},{2,0},{4,6},{6,4},{8,10},{10,8},{12,14},{14,12},{1,3},{3,1},... | collective-permute-start | bytes 98312 | tf_op jit(solution)/shard_map/ppermute | solution.py:286
  3.0 14.4 %slice-start = ((s8[33554432]{0:T(1024)(128)(4,1)}), s8[4194304]{0:T(1024)(128)(4,1)S(1)}, s32[]{:S(2)}) async-start(s8[33554432]{0:T(1024)(128)(4,1)} %bitcast), calls=%async_computation | async-start | bytes 8388608
  3.0 14.4 %slice-start.1 = ((s8[33554432]{0:T(1024)(128)(4,1)}), s8[4194304]{0:T(1024)(128)(4,1)S(1)}, s32[]{:S(2)}) async-start(s8[33554432]{0:T(1024)(128)(4,1)} %bitcast), calls=%async_computation.1 | async-start | bytes 8388608
  3.0 14.4 %slice-start.2 = ((s8[33554432]{0:T(1024)(128)(4,1)}), s8[4194304]{0:T(1024)(128)(4,1)S(1)}, s32[]{:S(2)}) async-start(s8[33554432]{0:T(1024)(128)(4,1)} %bitcast), calls=%async_computation.2 | async-start | bytes 8388608
  3.0 14.4 %slice-start.3 = ((s8[33554432]{0:T(1024)(128)(4,1)}), s8[4194304]{0:T(1024)(128)(4,1)S(1)}, s32[]{:S(2)}) async-start(s8[33554432]{0:T(1024)(128)(4,1)} %bitcast), calls=%async_computation.3 | async-start | bytes 8388608
  5.4 6.9 %collective-permute-start.3 = (bf16[2,2,8192]{2,1,0:T(2,128)(2,1)S(1)}, bf16[2,2,8192]{2,1,0:T(2,128)(2,1)S(1)}, u32[]{:S(2)}, u32[]{:S(2)}) collective-permute-start(bf16[2,2,8192]{2,1,0:T(2,128)(2,1)S(1)} %join.1.refs_4_), channel_id=1, source_target_pairs={{0,12},{2,14},{4,8},{6,10},{8,4},{10,6},{12,0},{14,2},{1,13},{3,15... | collective-permute-start | bytes 196616 | tf_op jit(solution)/shard_map/ppermute | solution.py:286
  9.3 5.3 %collective-permute-start.2 = (bf16[2,2,8192]{2,1,0:T(2,128)(2,1)S(1)}, bf16[2,2,8192]{2,1,0:T(2,128)(2,1)S(1)}, u32[]{:S(2)}, u32[]{:S(2)}) collective-permute-start(bf16[2,2,8192]{2,1,0:T(2,128)(2,1)S(1)} %join.1.refs_4_), channel_id=1, source_target_pairs={{0,8},{2,10},{4,12},{6,14},{8,0},{10,2},{12,4},{14,6},{1,9},{3,11}... | collective-permute-start | bytes 196616 | tf_op jit(solution)/shard_map/ppermute | solution.py:286
  9.3 5.3 %collective-permute-start.1 = (bf16[2,2,8192]{2,1,0:T(2,128)(2,1)S(1)}, bf16[2,2,8192]{2,1,0:T(2,128)(2,1)S(1)}, u32[]{:S(2)}, u32[]{:S(2)}) collective-permute-start(bf16[2,2,8192]{2,1,0:T(2,128)(2,1)S(1)} %join.1.refs_4_), channel_id=1, source_target_pairs={{0,4},{2,6},{4,0},{6,2},{8,12},{10,14},{12,8},{14,10},{1,5},{3,7},... | collective-permute-start | bytes 196616 | tf_op jit(solution)/shard_map/ppermute | solution.py:286
  14.6 2.8 %slice-start.4 = ((s8[33554432]{0:T(1024)(128)(4,1)}), s8[4194304]{0:T(1024)(128)(4,1)S(1)}, s32[]{:S(2)}) async-start(s8[33554432]{0:T(1024)(128)(4,1)} %bitcast), calls=%async_computation.4 | async-start | bytes 8388608
  15.3 1.2 %collective-permute-start.4 = (f32[16,128]{1,0:T(8,128)S(1)}, f32[16,128]{1,0:T(8,128)S(1)}, u32[]{:S(2)}, u32[]{:S(2)}) collective-permute-start(f32[16,128]{1,0:T(8,128)S(1)} %get-tuple-element.28), channel_id=1, source_target_pairs={{0,1},{1,0},{2,3},{3,2},{4,5},{5,4},{6,7},{7,6},{8,9},{9,8},{10,11... | collective-permute-start | bytes 24584 | tf_op jit(solution)/shard_map/ppermute | solution.py:286
  15.4 2.9 %slice-start.5 = ((s8[33554432]{0:T(1024)(128)(4,1)}), s8[4194304]{0:T(1024)(128)(4,1)S(1)}, s32[]{:S(2)}) async-start(s8[33554432]{0:T(1024)(128)(4,1)} %bitcast), calls=%async_computation.5 | async-start | bytes 8388608
  15.4 4.0 %slice-start.6 = ((s8[33554432]{0:T(1024)(128)(4,1)}), s8[4194304]{0:T(1024)(128)(4,1)S(1)}, s32[]{:S(2)}) async-start(s8[33554432]{0:T(1024)(128)(4,1)} %bitcast), calls=%async_computation.6 | async-start | bytes 8388608
  15.4 5.2 %slice-start.7 = ((s8[33554432]{0:T(1024)(128)(4,1)}), s8[4194304]{0:T(1024)(128)(4,1)S(1)}, s32[]{:S(2)}) async-start(s8[33554432]{0:T(1024)(128)(4,1)} %bitcast), calls=%async_computation.7 | async-start | bytes 8388608
  16.5 8.8 %collective-permute-start.5 = (bf16[16,128]{1,0:T(8,128)(2,1)S(1)}, bf16[16,128]{1,0:T(8,128)(2,1)S(1)}, u32[]{:S(2)}, u32[]{:S(2)}) collective-permute-start(bf16[16,128]{1,0:T(8,128)(2,1)S(1)} %pair.1.refs_0_), channel_id=1, source_target_pairs={{0,0},{1,2},{2,4},{3,6},{4,8},{5,10},{6,12},{7,14},{8,1},{9,3},{10... | collective-permute-start | bytes 12296 | tf_op jit(solution)/shard_map/ppermute | solution.py:388
  25.4 1.7 %collective-permute-start.6 = (f32[16,2176]{1,0:T(8,128)S(1)}, f32[16,2176]{1,0:T(8,128)S(1)}, u32[]{:S(2)}, u32[]{:S(2)}) collective-permute-start(f32[16,2176]{1,0:T(8,128)S(1)} %pack.1.refs_0_), channel_id=1, source_target_pairs={{0,1},{1,0},{2,3},{3,2},{4,5},{5,4},{6,7},{7,6},{8,9},{9,8},{10,11... | collective-permute-start | bytes 417800 | tf_op jit(solution)/shard_map/ppermute | solution.py:286
  32.0 7.5 %collective-permute-start.7 = (bf16[4,2,6144]{2,1,0:T(2,128)(2,1)S(1)}, bf16[4,2,6144]{2,1,0:T(2,128)(2,1)S(1)}, u32[]{:S(2)}, u32[]{:S(2)}) collective-permute-start(bf16[4,2,6144]{2,1,0:T(2,128)(2,1)S(1)} %get-tuple-element.36), channel_id=1, source_target_pairs={{0,2},{2,0},{4,6},{6,4},{8,10},{10,8},{12,14},{14,12},{1,3},{3,1},... | collective-permute-start | bytes 294920 | tf_op jit(solution)/shard_map/ppermute | solution.py:286
  35.5 4.0 %collective-permute-start.8 = (bf16[4,2,2048]{2,1,0:T(2,128)(2,1)S(1)}, bf16[4,2,2048]{2,1,0:T(2,128)(2,1)S(1)}, u32[]{:S(2)}, u32[]{:S(2)}) collective-permute-start(bf16[4,2,2048]{2,1,0:T(2,128)(2,1)S(1)} %get-tuple-element.40), channel_id=1, source_target_pairs={{0,2},{2,0},{4,6},{6,4},{8,10},{10,8},{12,14},{14,12},{1,3},{3,1},... | collective-permute-start | bytes 98312 | tf_op jit(solution)/shard_map/ppermute | solution.py:286
  39.5 5.9 %collective-permute-start.9 = (bf16[2,8192]{1,0:T(2,128)(2,1)S(1)}, bf16[2,8192]{1,0:T(2,128)(2,1)S(1)}, u32[]{:S(2)}, u32[]{:S(2)}) collective-permute-start(bf16[2,8192]{1,0:T(2,128)(2,1)S(1)} %get-tuple-element.42), channel_id=1, source_target_pairs={{0,12},{2,14},{4,8},{6,10},{8,4},{10,6},{12,0},{14,2},{1,13},{3,15... | collective-permute-start | bytes 98312 | tf_op jit(solution)/shard_map/ppermute | solution.py:286
  41.7 5.1 %collective-permute-start.10 = (bf16[2,8192]{1,0:T(2,128)(2,1)S(1)}, bf16[2,8192]{1,0:T(2,128)(2,1)S(1)}, u32[]{:S(2)}, u32[]{:S(2)}) collective-permute-start(bf16[2,8192]{1,0:T(2,128)(2,1)S(1)} %get-tuple-element.43), channel_id=1, source_target_pairs={{0,8},{2,10},{4,12},{6,14},{8,0},{10,2},{12,4},{14,6},{1,9},{3,11}... | collective-permute-start | bytes 98312 | tf_op jit(solution)/shard_map/ppermute | solution.py:286
  42.4 4.4 %collective-permute-start.11 = (bf16[2,8192]{1,0:T(2,128)(2,1)S(1)}, bf16[2,8192]{1,0:T(2,128)(2,1)S(1)}, u32[]{:S(2)}, u32[]{:S(2)}) collective-permute-start(bf16[2,8192]{1,0:T(2,128)(2,1)S(1)} %get-tuple-element.44), channel_id=1, source_target_pairs={{0,4},{2,6},{4,0},{6,2},{8,12},{10,14},{12,8},{14,10},{1,5},{3,7},... | collective-permute-start | bytes 98312 | tf_op jit(solution)/shard_map/ppermute | solution.py:286

commit v7 on v6

--- a/solution.py
+++ b/solution.py
@@ -130,8 +130,8 @@
         turn_ref[2 * i] = jnp.cos(angle)
         turn_ref[2 * i + 1] = jnp.where(lane < dim // 2, -sine, sine)
     shape = allow_ref.shape
-    query = owner(lax.rem(lax.broadcasted_iota(jnp.int32, shape, 0), total), me)
-    key = owner(lax.broadcasted_iota(jnp.int32, shape, 1), me // 2)
+    query = owner(lax.rem(lax.broadcasted_iota(jnp.int32, shape, 1), total), me)
+    key = owner(lax.broadcasted_iota(jnp.int32, shape, 0), me // 2)
     same = positions(query, len_ref)[0] == positions(key, len_ref)[0]
     allow_ref[...] = jnp.where(same & (key <= query), 1.0, 0.0).astype(F32)
     for copy in copies:
@@ -213,12 +213,12 @@
     keys = rotate(keys, 2)
     heads = summed.shape[1] // dim
     stack = jnp.concatenate([rotate(summed[:, dim * h : dim * (h + 1)], 0) for h in range(heads)], axis=0)
-    scores = lax.dot_general(stack, keys, (((1,), (1,)), ((), ())), preferred_element_type=F32)
+    scores = lax.dot_general(keys, stack, (((1,), (1,)), ((), ())), preferred_element_type=F32)
     scores = scores / F32(math.sqrt(dim))
     scores = jnp.where(allow_ref[...] > 0, scores, F32(-1e30))
-    weights = jnp.exp(scores - jnp.max(scores, axis=1, keepdims=True))
-    probs = (weights / jnp.sum(weights, axis=1, keepdims=True)).astype(BF16)
-    mixed = jnp.dot(probs, values, preferred_element_type=F32).astype(BF16)
+    weights = jnp.exp(scores - jnp.max(scores, axis=0, keepdims=True))
+    probs = (weights / jnp.sum(weights, axis=0, keepdims=True)).astype(BF16)
+    mixed = lax.dot_general(probs, values, (((0,), (0,)), ((), ())), preferred_element_type=F32).astype(BF16)
     for h in range(heads):
         att[:, dim * h : dim * (h + 1)] = mixed[total * h : total * (h + 1), :]
 
@@ -359,7 +359,7 @@
         functools.partial(tables_kernel, rows=rows, spans=spans),
         "tables",
         [lengths, w_out],
-        [shaped(4, total, HEAD_DIM), shaped(heads * total, total)] + [fetched(w_out, *s) for s in spans],
+        [shaped(4, total, HEAD_DIM), shaped(total, heads * total)] + [fetched(w_out, *s) for s in spans],
         [pltpu.SemaphoreType.DMA((1,)), pltpu.SMEM(lengths.shape, jnp.int32), pltpu.SemaphoreType.DMA],
         limit=2,
         far=2,

time: 47.6 us -> 47.7 us (level)
  transfers between devices with their start and end apart: 12 -> 12, of which waited for: 6 -> 6; matrix products, arithmetic and copies ran while one was open for 0% -> 0% of each run, Pallas kernels for 23% -> 22%
where the time goes in v7:
time: 47.7 us; the launch traced here: 47.6 us
  Pallas kernels  17.2 us (36%)
  starting transfers between devices  15 us (31%)
  waiting for transfers between devices  11.9 us (25%)
  local copies, waits for them, and re-layouts  3.28 us (7%)
    pallas_call x12, Pallas kernels, call(): pl.pallas_call(kernel, out_shape=tuple(outs), in_specs=specs, out_specs=(...  17.2 us
    ppermute x11, starting transfers between devices, swap(): return lax.ppermute(x, axis, [(i, i ^ bit) for i in range(size)])  14.2 us
    ppermute x11, waiting for transfers between devices, swap(): return lax.ppermute(x, axis, [(i, i ^ bit) for i in range(size)])  11.9 us
    unnamed x20, local copies, waits for them, and re-layouts  3.28 us
  transfers between devices with their start and end apart: 12, of which 6 were waited for; matrix products, arithmetic and copies ran while one was open for 0% of the time, Pallas kernels for 22%

profile of v7, /device:TPU:0, one launch (start us, length us, event | category | flops | bytes accessed | tf_op | source)
XLA Modules:
  0.0 47.6 jit_solution(470596953239659560)
XLA Ops:
  0.0 3.0 %collective-permute-start = (bf16[2,8192]{1,0:T(2,128)(2,1)}, bf16[2,8192]{1,0:T(2,128)(2,1)S(1)}, u32[]{:S(2)}, u32[]{:S(2)}) collective-permute-start(bf16[2,8192]{1,0:T(2,128)(2,1)} %refs_1_.4), channel_id=1, source_target_pairs={{0,2},{2,0},{4,6},{6,4},{8,10},{10,8},{12,14},{14,12},{1,3},{3,1},... | collective-permute-start | bytes 98312 | tf_op jit(solution)/shard_map/ppermute | solution.py:286
  3.0 2.4 %tables.1 = (f32[4,16,128]{2,1,0:T(8,128)S(1)}, f32[16,256]{1,0:T(8,128)S(1)}, bf16[2048,1024]{1,0:T(8,128)(2,1)S(1)}) custom-call(s32[4]{0:T(128)} %refs_0_.1, bf16[2048,8192]{1,0:T(8,128)(2,1)} %refs_2_.3), custom_call_target="tpu_custom_call" | custom-call | bytes 1000 | tf_op jit(solution)/shard_map/tables/pallas_call | solution.py:48
  5.4 3.9 %collective-permute-start.3 = (bf16[2,2,8192]{2,1,0:T(2,128)(2,1)S(1)}, bf16[2,2,8192]{2,1,0:T(2,128)(2,1)S(1)}, u32[]{:S(2)}, u32[]{:S(2)}) collective-permute-start(bf16[2,2,8192]{2,1,0:T(2,128)(2,1)S(1)} %join.1.refs_4_), channel_id=1, source_target_pairs={{0,12},{2,14},{4,8},{6,10},{8,4},{10,6},{12,0},{14,2},{1,13},{3,15... | collective-permute-start | bytes 196616 | tf_op jit(solution)/shard_map/ppermute | solution.py:286
  9.9 2.4 %collective-permute-done.3.refs_3_ = bf16[2,2,8192]{2,1,0:T(2,128)(2,1)S(1)} collective-permute-done((bf16[2,2,8192]{2,1,0:T(2,128)(2,1)S(1)}, bf16[2,2,8192]{2,1,0:T(2,128)(2,1)S(1)}, u32[]{:S(2)}, u32[]{:S(2)}) %collective-permute-start.3) | collective-permute-done | bytes 65568 | tf_op jit(solution)/shard_map/ppermute | solution.py:286
  12.3 2.2 %collective-permute-done.2.refs_2_ = bf16[2,2,8192]{2,1,0:T(2,128)(2,1)S(1)} collective-permute-done((bf16[2,2,8192]{2,1,0:T(2,128)(2,1)S(1)}, bf16[2,2,8192]{2,1,0:T(2,128)(2,1)S(1)}, u32[]{:S(2)}, u32[]{:S(2)}) %collective-permute-start.2) | collective-permute-done | bytes 65568 | tf_op jit(solution)/shard_map/ppermute | solution.py:286
  14.6 0.7 %keyval.1 = (bf16[16,8192]{1,0:T(8,128)(2,1)S(1)}, f32[16,128]{1,0:T(8,128)S(1)}, f32[16,128]{1,0:T(8,128)S(1)}) custom-call(bf16[2048,1024]{1,0:T(8,128)(2,1)S(1)} %get-tuple-element.25.refs_0_.refs_4_, bf16[2,2,8192]{2,1,0:T(2,128)(2,1)S(1)} %collective-permute-done.1.refs_1_, bf16[2,2,8192]{2,1,0:T(2,128)(2,1)S(1)} %collective-permute-done.2.refs_2_, ...), custom_call_target="tpu_custom_call" | custom-call | bytes 1000 | tf_op jit(solution)/shard_map/keyval/pallas_call | solution.py:48
  15.4 1.1 %collective-permute-done.4.refs_2_ = f32[16,128]{1,0:T(8,128)S(1)} collective-permute-done((f32[16,128]{1,0:T(8,128)S(1)}, f32[16,128]{1,0:T(8,128)S(1)}, u32[]{:S(2)}, u32[]{:S(2)}) %collective-permute-start.4) | collective-permute-done | bytes 8224 | tf_op jit(solution)/shard_map/ppermute | solution.py:286
  16.5 0.8 %collective-permute-start.5 = (bf16[16,128]{1,0:T(8,128)(2,1)S(1)}, bf16[16,128]{1,0:T(8,128)(2,1)S(1)}, u32[]{:S(2)}, u32[]{:S(2)}) collective-permute-start(bf16[16,128]{1,0:T(8,128)(2,1)S(1)} %pair.1.refs_0_), channel_id=1, source_target_pairs={{0,0},{1,2},{2,4},{3,6},{4,8},{5,10},{6,12},{7,14},{8,1},{9,3},{10... | collective-permute-start | bytes 12296 | tf_op jit(solution)/shard_map/ppermute | solution.py:388
  17.4 0.9 %slice-done.5 = s8[4194304]{0:T(1024)(128)(4,1)S(1)} async-done(((s8[33554432]{0:T(1024)(128)(4,1)}), s8[4194304]{0:T(1024)(128)(4,1)S(1)}, s32[]{:S(2)}) %slice-start.5) | async-done | bytes 4194328
  18.2 1.2 %slice-done.6 = s8[4194304]{0:T(1024)(128)(4,1)S(1)} async-done(((s8[33554432]{0:T(1024)(128)(4,1)}), s8[4194304]{0:T(1024)(128)(4,1)S(1)}, s32[]{:S(2)}) %slice-start.6) | async-done | bytes 4194328
  19.4 1.2 %slice-done.7 = s8[4194304]{0:T(1024)(128)(4,1)S(1)} async-done(((s8[33554432]{0:T(1024)(128)(4,1)}), s8[4194304]{0:T(1024)(128)(4,1)S(1)}, s32[]{:S(2)}) %slice-start.7) | async-done | bytes 4194328
  20.6 4.7 %query.1 = (f32[16,2048]{1,0:T(8,128)S(1)}, bf16[2048,1024]{1,0:T(8,128)(2,1)S(1)}, bf16[2048,1024]{1,0:T(8,128)(2,1)S(1)}, bf16[2048,1024]{1,0:T(8,128)(2,1)S(1)}) custom-call(bf16[16,128]{1,0:T(8,128)(2,1)S(1)} %pair.1.refs_0_, bf16[16,8192]{1,0:T(8,128)(2,1)S(1)} %get-tuple-element.29.refs_1_, bf16[8192,2048]{1,0:T(8,128)(2,1)S(1)} %bitcast.1, ...), custom_call_target="tpu_custom_call" | custom-call | bytes 1000 | tf_op jit(solution)/shard_map/query/pallas_call | solution.py:48
  25.5 1.6 %ahead.1.refs_8_ = bf16[2048,512]{1,0:T(8,128)(2,1)S(1)} custom-call(f32[16,2176]{1,0:T(8,128)S(1)} %pack.1.refs_0_, bf16[2048,8192]{1,0:T(8,128)(2,1)} %refs_2_.3), custom_call_target="tpu_custom_call" | custom-call | bytes 1000 | tf_op jit(solution)/shard_map/ahead/pallas_call | solution.py:48
  27.1 5.0 %output0.1 = (bf16[16,2048]{1,0:T(8,128)(2,1)S(1)}, f32[4,2,6144]{2,1,0:T(2,128)S(1)}, bf16[4,2,6144]{2,1,0:T(2,128)(2,1)S(1)}, bf16[2048,1536]{1,0:T(8,128)(2,1)S(1)}) custom-call(f32[16,2176]{1,0:T(8,128)S(1)} %pack.1.refs_0_, f32[16,2176]{1,0:T(8,128)S(1)} %collective-permute-done.6.refs_1_, f32[4,16,128]{2,1,0:T(8,128)S(1)} %get-tuple-element.26.refs_0_.refs_2_, ...), custom_call_target="tpu_custom_call" | custom-call | bytes 1000 | tf_op jit(solution)/shard_map/output0/pallas_call | solution.py:48
  32.1 1.5 %collective-permute-start.7 = (bf16[4,2,6144]{2,1,0:T(2,128)(2,1)S(1)}, bf16[4,2,6144]{2,1,0:T(2,128)(2,1)S(1)}, u32[]{:S(2)}, u32[]{:S(2)}) collective-permute-start(bf16[4,2,6144]{2,1,0:T(2,128)(2,1)S(1)} %get-tuple-element.36), channel_id=1, source_target_pairs={{0,2},{2,0},{4,6},{6,4},{8,10},{10,8},{12,14},{14,12},{1,3},{3,1},... | collective-permute-start | bytes 294920 | tf_op jit(solution)/shard_map/ppermute | solution.py:286
  33.6 2.0 %output1.1 = (f32[4,2,2048]{2,1,0:T(2,128)S(1)}, bf16[4,2,2048]{2,1,0:T(2,128)(2,1)S(1)}) custom-call(bf16[16,2048]{1,0:T(8,128)(2,1)S(1)} %get-tuple-element.37.refs_0_, bf16[2048,1536]{1,0:T(8,128)(2,1)S(1)} %get-tuple-element.38.refs_1_, bf16[2048,8192]{1,0:T(8,128)(2,1)} %refs_2_.3), custom_call_target="tpu_custom_call" | custom-call | bytes 1000 | tf_op jit(solution)/shard_map/output1/pallas_call | solution.py:48
  35.6 0.7 %collective-permute-start.8 = (bf16[4,2,2048]{2,1,0:T(2,128)(2,1)S(1)}, bf16[4,2,2048]{2,1,0:T(2,128)(2,1)S(1)}, u32[]{:S(2)}, u32[]{:S(2)}) collective-permute-start(bf16[4,2,2048]{2,1,0:T(2,128)(2,1)S(1)} %get-tuple-element.40), channel_id=1, source_target_pairs={{0,2},{2,0},{4,6},{6,4},{8,10},{10,8},{12,14},{14,12},{1,3},{3,1},... | collective-permute-start | bytes 98312 | tf_op jit(solution)/shard_map/ppermute | solution.py:286
  36.3 3.3 %collective-permute-done.8.refs_3_ = bf16[4,2,2048]{2,1,0:T(2,128)(2,1)S(1)} collective-permute-done((bf16[4,2,2048]{2,1,0:T(2,128)(2,1)S(1)}, bf16[4,2,2048]{2,1,0:T(2,128)(2,1)S(1)}, u32[]{:S(2)}, u32[]{:S(2)}) %collective-permute-start.8) | collective-permute-done | bytes 32800 | tf_op jit(solution)/shard_map/ppermute | solution.py:286
  39.7 2.2 %collective-permute-start.9 = (bf16[2,8192]{1,0:T(2,128)(2,1)S(1)}, bf16[2,8192]{1,0:T(2,128)(2,1)S(1)}, u32[]{:S(2)}, u32[]{:S(2)}) collective-permute-start(bf16[2,8192]{1,0:T(2,128)(2,1)S(1)} %get-tuple-element.42), channel_id=1, source_target_pairs={{0,12},{2,14},{4,8},{6,10},{8,4},{10,6},{12,0},{14,2},{1,13},{3,15... | collective-permute-start | bytes 98312 | tf_op jit(solution)/shard_map/ppermute | solution.py:286
  41.8 0.7 %collective-permute-start.10 = (bf16[2,8192]{1,0:T(2,128)(2,1)S(1)}, bf16[2,8192]{1,0:T(2,128)(2,1)S(1)}, u32[]{:S(2)}, u32[]{:S(2)}) collective-permute-start(bf16[2,8192]{1,0:T(2,128)(2,1)S(1)} %get-tuple-element.43), channel_id=1, source_target_pairs={{0,8},{2,10},{4,12},{6,14},{8,0},{10,2},{12,4},{14,6},{1,9},{3,11}... | collective-permute-start | bytes 98312 | tf_op jit(solution)/shard_map/ppermute | solution.py:286
  42.5 1.6 %collective-permute-start.11 = (bf16[2,8192]{1,0:T(2,128)(2,1)S(1)}, bf16[2,8192]{1,0:T(2,128)(2,1)S(1)}, u32[]{:S(2)}, u32[]{:S(2)}) collective-permute-start(bf16[2,8192]{1,0:T(2,128)(2,1)S(1)} %get-tuple-element.44), channel_id=1, source_target_pairs={{0,4},{2,6},{4,0},{6,2},{8,12},{10,14},{12,8},{14,10},{1,5},{3,7},... | collective-permute-start | bytes 98312 | tf_op jit(solution)/shard_map/ppermute | solution.py:286
  44.1 1.5 %collective-permute-done.9.refs_1_ = bf16[2,8192]{1,0:T(2,128)(2,1)S(1)} collective-permute-done((bf16[2,8192]{1,0:T(2,128)(2,1)S(1)}, bf16[2,8192]{1,0:T(2,128)(2,1)S(1)}, u32[]{:S(2)}, u32[]{:S(2)}) %collective-permute-start.9) | collective-permute-done | bytes 32800 | tf_op jit(solution)/shard_map/ppermute | solution.py:286
  45.6 1.3 %collective-permute-done.10.refs_2_ = bf16[2,8192]{1,0:T(2,128)(2,1)S(1)} collective-permute-done((bf16[2,8192]{1,0:T(2,128)(2,1)S(1)}, bf16[2,8192]{1,0:T(2,128)(2,1)S(1)}, u32[]{:S(2)}, u32[]{:S(2)}) %collective-permute-start.10) | collective-permute-done | bytes 32800 | tf_op jit(solution)/shard_map/ppermute | solution.py:286
  46.9 0.7 %total.1 = bf16[2,8192]{1,0:T(2,128)(2,1)} custom-call(f32[2,8192]{1,0:T(2,128)S(1)} %get-tuple-element.41.refs_0_, bf16[2,8192]{1,0:T(2,128)(2,1)S(1)} %collective-permute-done.9.refs_1_, bf16[2,8192]{1,0:T(2,128)(2,1)S(1)} %collective-permute-done.10.refs_2_, bf16[2,8192]{1,0:T(2,128)(2,1)S(1)} %collective-permute-done.11.refs_3_), custom_call_target="tpu_custom_call" | custom-call | bytes 1000 | tf_op jit(solution)/shard_map/total/pallas_call | solution.py:48
  (33 shorter events, 1.0 us)
Async XLA Ops:
  0.0 5.4 %copy-start.1 = (bf16[2,8192]{1,0:T(2,128)(2,1)S(1)}, bf16[2,8192]{1,0:T(2,128)(2,1)}, u32[]{:S(2)}) copy-start(bf16[2,8192]{1,0:T(2,128)(2,1)} %refs_1_.4) | copy-start | bytes 98308
  0.0 14.6 %copy-start = (bf16[8192,256]{1,0:T(8,128)(2,1)S(1)}, bf16[8192,256]{1,0:T(8,128)(2,1)}, u32[]{:S(2)}) copy-start(bf16[8192,256]{1,0:T(8,128)(2,1)} %refs_5_.2) | copy-start | bytes 12582916
  0.0 5.3 %collective-permute-start = (bf16[2,8192]{1,0:T(2,128)(2,1)}, bf16[2,8192]{1,0:T(2,128)(2,1)S(1)}, u32[]{:S(2)}, u32[]{:S(2)}) collective-permute-start(bf16[2,8192]{1,0:T(2,128)(2,1)} %refs_1_.4), channel_id=1, source_target_pairs={{0,2},{2,0},{4,6},{6,4},{8,10},{10,8},{12,14},{14,12},{1,3},{3,1},... | collective-permute-start | bytes 98312 | tf_op jit(solution)/shard_map/ppermute | solution.py:286
  3.0 14.4 %slice-start = ((s8[33554432]{0:T(1024)(128)(4,1)}), s8[4194304]{0:T(1024)(128)(4,1)S(1)}, s32[]{:S(2)}) async-start(s8[33554432]{0:T(1024)(128)(4,1)} %bitcast), calls=%async_computation | async-start | bytes 8388608
  3.0 14.4 %slice-start.1 = ((s8[33554432]{0:T(1024)(128)(4,1)}), s8[4194304]{0:T(1024)(128)(4,1)S(1)}, s32[]{:S(2)}) async-start(s8[33554432]{0:T(1024)(128)(4,1)} %bitcast), calls=%async_computation.1 | async-start | bytes 8388608
  3.0 14.4 %slice-start.2 = ((s8[33554432]{0:T(1024)(128)(4,1)}), s8[4194304]{0:T(1024)(128)(4,1)S(1)}, s32[]{:S(2)}) async-start(s8[33554432]{0:T(1024)(128)(4,1)} %bitcast), calls=%async_computation.2 | async-start | bytes 8388608
  3.0 14.4 %slice-start.3 = ((s8[33554432]{0:T(1024)(128)(4,1)}), s8[4194304]{0:T(1024)(128)(4,1)S(1)}, s32[]{:S(2)}) async-start(s8[33554432]{0:T(1024)(128)(4,1)} %bitcast), calls=%async_computation.3 | async-start | bytes 8388608
  5.4 6.9 %collective-permute-start.3 = (bf16[2,2,8192]{2,1,0:T(2,128)(2,1)S(1)}, bf16[2,2,8192]{2,1,0:T(2,128)(2,1)S(1)}, u32[]{:S(2)}, u32[]{:S(2)}) collective-permute-start(bf16[2,2,8192]{2,1,0:T(2,128)(2,1)S(1)} %join.1.refs_4_), channel_id=1, source_target_pairs={{0,12},{2,14},{4,8},{6,10},{8,4},{10,6},{12,0},{14,2},{1,13},{3,15... | collective-permute-start | bytes 196616 | tf_op jit(solution)/shard_map/ppermute | solution.py:286
  9.3 5.3 %collective-permute-start.2 = (bf16[2,2,8192]{2,1,0:T(2,128)(2,1)S(1)}, bf16[2,2,8192]{2,1,0:T(2,128)(2,1)S(1)}, u32[]{:S(2)}, u32[]{:S(2)}) collective-permute-start(bf16[2,2,8192]{2,1,0:T(2,128)(2,1)S(1)} %join.1.refs_4_), channel_id=1, source_target_pairs={{0,8},{2,10},{4,12},{6,14},{8,0},{10,2},{12,4},{14,6},{1,9},{3,11}... | collective-permute-start | bytes 196616 | tf_op jit(solution)/shard_map/ppermute | solution.py:286
  9.3 5.3 %collective-permute-start.1 = (bf16[2,2,8192]{2,1,0:T(2,128)(2,1)S(1)}, bf16[2,2,8192]{2,1,0:T(2,128)(2,1)S(1)}, u32[]{:S(2)}, u32[]{:S(2)}) collective-permute-start(bf16[2,2,8192]{2,1,0:T(2,128)(2,1)S(1)} %join.1.refs_4_), channel_id=1, source_target_pairs={{0,4},{2,6},{4,0},{6,2},{8,12},{10,14},{12,8},{14,10},{1,5},{3,7},... | collective-permute-start | bytes 196616 | tf_op jit(solution)/shard_map/ppermute | solution.py:286
  14.6 2.8 %slice-start.4 = ((s8[33554432]{0:T(1024)(128)(4,1)}), s8[4194304]{0:T(1024)(128)(4,1)S(1)}, s32[]{:S(2)}) async-start(s8[33554432]{0:T(1024)(128)(4,1)} %bitcast), calls=%async_computation.4 | async-start | bytes 8388608
  15.3 1.2 %collective-permute-start.4 = (f32[16,128]{1,0:T(8,128)S(1)}, f32[16,128]{1,0:T(8,128)S(1)}, u32[]{:S(2)}, u32[]{:S(2)}) collective-permute-start(f32[16,128]{1,0:T(8,128)S(1)} %get-tuple-element.28), channel_id=1, source_target_pairs={{0,1},{1,0},{2,3},{3,2},{4,5},{5,4},{6,7},{7,6},{8,9},{9,8},{10,11... | collective-permute-start | bytes 24584 | tf_op jit(solution)/shard_map/ppermute | solution.py:286
  15.4 2.9 %slice-start.5 = ((s8[33554432]{0:T(1024)(128)(4,1)}), s8[4194304]{0:T(1024)(128)(4,1)S(1)}, s32[]{:S(2)}) async-start(s8[33554432]{0:T(1024)(128)(4,1)} %bitcast), calls=%async_computation.5 | async-start | bytes 8388608
  15.4 4.0 %slice-start.6 = ((s8[33554432]{0:T(1024)(128)(4,1)}), s8[4194304]{0:T(1024)(128)(4,1)S(1)}, s32[]{:S(2)}) async-start(s8[33554432]{0:T(1024)(128)(4,1)} %bitcast), calls=%async_computation.6 | async-start | bytes 8388608
  15.4 5.2 %slice-start.7 = ((s8[33554432]{0:T(1024)(128)(4,1)}), s8[4194304]{0:T(1024)(128)(4,1)S(1)}, s32[]{:S(2)}) async-start(s8[33554432]{0:T(1024)(128)(4,1)} %bitcast), calls=%async_computation.7 | async-start | bytes 8388608
  16.5 8.8 %collective-permute-start.5 = (bf16[16,128]{1,0:T(8,128)(2,1)S(1)}, bf16[16,128]{1,0:T(8,128)(2,1)S(1)}, u32[]{:S(2)}, u32[]{:S(2)}) collective-permute-start(bf16[16,128]{1,0:T(8,128)(2,1)S(1)} %pair.1.refs_0_), channel_id=1, source_target_pairs={{0,0},{1,2},{2,4},{3,6},{4,8},{5,10},{6,12},{7,14},{8,1},{9,3},{10... | collective-permute-start | bytes 12296 | tf_op jit(solution)/shard_map/ppermute | solution.py:388
  25.4 1.7 %collective-permute-start.6 = (f32[16,2176]{1,0:T(8,128)S(1)}, f32[16,2176]{1,0:T(8,128)S(1)}, u32[]{:S(2)}, u32[]{:S(2)}) collective-permute-start(f32[16,2176]{1,0:T(8,128)S(1)} %pack.1.refs_0_), channel_id=1, source_target_pairs={{0,1},{1,0},{2,3},{3,2},{4,5},{5,4},{6,7},{7,6},{8,9},{9,8},{10,11... | collective-permute-start | bytes 417800 | tf_op jit(solution)/shard_map/ppermute | solution.py:286
  32.1 7.5 %collective-permute-start.7 = (bf16[4,2,6144]{2,1,0:T(2,128)(2,1)S(1)}, bf16[4,2,6144]{2,1,0:T(2,128)(2,1)S(1)}, u32[]{:S(2)}, u32[]{:S(2)}) collective-permute-start(bf16[4,2,6144]{2,1,0:T(2,128)(2,1)S(1)} %get-tuple-element.36), channel_id=1, source_target_pairs={{0,2},{2,0},{4,6},{6,4},{8,10},{10,8},{12,14},{14,12},{1,3},{3,1},... | collective-permute-start | bytes 294920 | tf_op jit(solution)/shard_map/ppermute | solution.py:286
  35.6 4.0 %collective-permute-start.8 = (bf16[4,2,2048]{2,1,0:T(2,128)(2,1)S(1)}, bf16[4,2,2048]{2,1,0:T(2,128)(2,1)S(1)}, u32[]{:S(2)}, u32[]{:S(2)}) collective-permute-start(bf16[4,2,2048]{2,1,0:T(2,128)(2,1)S(1)} %get-tuple-element.40), channel_id=1, source_target_pairs={{0,2},{2,0},{4,6},{6,4},{8,10},{10,8},{12,14},{14,12},{1,3},{3,1},... | collective-permute-start | bytes 98312 | tf_op jit(solution)/shard_map/ppermute | solution.py:286
  39.7 5.9 %collective-permute-start.9 = (bf16[2,8192]{1,0:T(2,128)(2,1)S(1)}, bf16[2,8192]{1,0:T(2,128)(2,1)S(1)}, u32[]{:S(2)}, u32[]{:S(2)}) collective-permute-start(bf16[2,8192]{1,0:T(2,128)(2,1)S(1)} %get-tuple-element.42), channel_id=1, source_target_pairs={{0,12},{2,14},{4,8},{6,10},{8,4},{10,6},{12,0},{14,2},{1,13},{3,15... | collective-permute-start | bytes 98312 | tf_op jit(solution)/shard_map/ppermute | solution.py:286
  41.8 5.1 %collective-permute-start.10 = (bf16[2,8192]{1,0:T(2,128)(2,1)S(1)}, bf16[2,8192]{1,0:T(2,128)(2,1)S(1)}, u32[]{:S(2)}, u32[]{:S(2)}) collective-permute-start(bf16[2,8192]{1,0:T(2,128)(2,1)S(1)} %get-tuple-element.43), channel_id=1, source_target_pairs={{0,8},{2,10},{4,12},{6,14},{8,0},{10,2},{12,4},{14,6},{1,9},{3,11}... | collective-permute-start | bytes 98312 | tf_op jit(solution)/shard_map/ppermute | solution.py:286
  42.5 4.4 %collective-permute-start.11 = (bf16[2,8192]{1,0:T(2,128)(2,1)S(1)}, bf16[2,8192]{1,0:T(2,128)(2,1)S(1)}, u32[]{:S(2)}, u32[]{:S(2)}) collective-permute-start(bf16[2,8192]{1,0:T(2,128)(2,1)S(1)} %get-tuple-element.44), channel_id=1, source_target_pairs={{0,4},{2,6},{4,0},{6,2},{8,12},{10,14},{12,8},{14,10},{1,5},{3,7},... | collective-permute-start | bytes 98312 | tf_op jit(solution)/shard_map/ppermute | solution.py:286
